TPU v7x, 512 devices: a whole 4x8x8 slice. The times are simulated.
512 devices in a mesh: blk: 128 (over z, y, core), rep: 4 (over x).
Axes of the slice: x: 4, y: 8, z: 8, core: 2. Of those that a mesh axis runs over, the one named last changes fastest.
Arguments:
- features: bfloat16 [262144, 128], P(('blk', 'rep')), may hold values from -6 to 6
- send_rows: int32 [65536, 8], P(('blk', 'rep')), may hold values from 0 to 511, as said below
- send_counts: int32 [65536], P(('blk', 'rep')), may hold values from 0 to 8, as said below
- tile_values: bfloat16 [2048, 4, 128, 128], P(('blk', 'rep')), may hold values from 0 to 1
- tile_rows: int32 [2048, 4], P(('blk', 'rep')), may hold values from 0 to 15
- tile_cols: int32 [2048, 4], P(('blk', 'rep')), may hold values from 0 to 3
- tile_counts: int32 [2048], P(('blk', 'rep')), may hold values from 2 to 4, as said below
- degree_scale: float32 [262144], P(('blk', 'rep')), may hold values from 0.1 to 0.5
- weight: bfloat16 [128, 256], replicated, may hold values from -0.5 to 0.5
- bias: float32 [256], replicated, may hold values from -3 to 3
- out_grad: bfloat16 [262144, 256], P(('blk', 'rep')), may hold values from -6 to 6
Outputs:
- hidden: bfloat16 [262144, 256], P(('blk', 'rep'))
- grad_features: bfloat16 [262144, 128], P(('blk', 'rep'))
- grad_weight: float32 [128, 256], replicated
- grad_bias: float32 [256], replicated
Inputs may be any that keep to these rules, and one draw needn't show every extreme that they name: `send_counts`: within each rep index, the counts of one sender over its owners sum to 512, as do the counts one owner receives; some counts equal 8 and some are 0. `send_rows`: entries of slots below the count are distinct local rows and cover every row of the device once; the other entries are 0. `tile_counts`: only the first count tiles of an entry are live; some entries are full.
All inputs are finite; a program needn't handle non-finite values.
Results may differ from a plain program's by a relative error of at most 0.008.
Values may be sent and summed in bfloat16 or wider, within the bound.
No kernel may reach another device: no remote copies, remote signals or barrier semaphores. Data moves between devices by JAX's collectives and lax.ppermute only.
A program may use at most 64 MiB of HBM per device.

v0:
```python
import jax
import jax.numpy as jnp
from jax import lax
from jax.sharding import PartitionSpec as P


def passed_along(value, axis, steps):
    count = lax.axis_size(axis)
    pairs = [(source, (source + steps) % count) for source in range(count)]
    return lax.ppermute(value, axis, pairs)


def select_table(index, count):
    return index[:, None] == jnp.arange(count, dtype=jnp.int32)[None, :]


def gather_terms(tiles, tile_rows, tile_cols, live, source, step, tile, row_tiles, width):
    col_tiles = source.shape[0] // tile
    picker = select_table(tile_cols[step], col_tiles).astype(jnp.bfloat16)
    operand = jnp.einsum(
        "is,sop->iop",
        picker,
        source.reshape(col_tiles, tile, width),
        preferred_element_type=jnp.float32,
    ).astype(jnp.bfloat16)
    prod = jnp.einsum("kab,kbf->kaf", tiles[step], operand, preferred_element_type=jnp.float32)
    prod = prod * live[step][:, None, None]
    placer = select_table(tile_rows[step], row_tiles).astype(jnp.float32)
    total = jnp.einsum(
        "kr,kaf->raf",
        placer,
        prod,
        precision=lax.Precision.HIGHEST,
        preferred_element_type=jnp.float32,
    )
    return total.reshape(row_tiles * tile, width)


def spread_terms(tiles, tile_rows, tile_cols, live, block, step, tile, col_tiles, width):
    row_tiles = block.shape[0] // tile
    picker = select_table(tile_rows[step], row_tiles).astype(jnp.bfloat16)
    operand = jnp.einsum(
        "kr,raf->kaf",
        picker,
        block.reshape(row_tiles, tile, width),
        preferred_element_type=jnp.float32,
    ).astype(jnp.bfloat16)
    prod = jnp.einsum("kab,kaf->kbf", tiles[step], operand, preferred_element_type=jnp.float32)
    prod = prod * live[step][:, None, None]
    placer = select_table(tile_cols[step], col_tiles).astype(jnp.float32)
    total = jnp.einsum(
        "mt,mxu->txu",
        placer,
        prod,
        precision=lax.Precision.HIGHEST,
        preferred_element_type=jnp.float32,
    )
    return total.reshape(col_tiles * tile, width)


def on_device(
    features,
    send_rows,
    send_counts,
    tile_values,
    tile_rows,
    tile_cols,
    tile_counts,
    degree_scale,
    weight,
    bias,
    out_grad,
):
    blocks = lax.axis_size("blk")
    quarters = lax.axis_size("rep")
    rows, width = features.shape
    slots = send_rows.shape[1]
    steps, most, tile = (tile_values.shape[0], tile_values.shape[1], tile_values.shape[2])
    row_tiles = quarters * rows // tile
    col_tiles = rows // tile
    slot = jnp.arange(slots, dtype=jnp.int32)
    valid_send = slot[None, :] < send_counts[:, None]
    outgoing = features[send_rows]
    incoming, arrived = (
        lax.all_to_all(outgoing, "blk", split_axis=0, concat_axis=0, tiled=True),
        lax.all_to_all(
            send_counts.reshape(blocks, 1), "blk", split_axis=0, concat_axis=0, tiled=True
        ),
    )
    arrived = arrived[:, 0]
    start = jnp.cumsum(arrived) - arrived
    place = jnp.where(
        slot[None, :] < arrived[:, None], start[:, None] + slot[None, :], rows
    ).astype(jnp.int32)
    owned = (
        jnp.zeros((rows + 1, width), jnp.bfloat16)
        .at[place.reshape(-1)]
        .set(incoming.reshape(-1, width))[:rows]
    )
    scale = degree_scale[:, None]
    scaled = (scale * owned.astype(jnp.float32)).astype(jnp.bfloat16)
    live = (jnp.arange(most, dtype=jnp.int32)[None, :] < tile_counts[:, None]).astype(jnp.float32)
    current = scaled
    partial_value = gather_terms(
        tile_values, tile_rows, tile_cols, live, current, 0, tile, row_tiles, width
    )
    for step in range(1, steps):
        current = passed_along(current, "blk", 1)
        partial_value = partial_value + gather_terms(
            tile_values, tile_rows, tile_cols, live, current, step, tile, row_tiles, width
        )
    summed = lax.psum_scatter(partial_value, "rep", scatter_dimension=0, tiled=True)
    agg = (scale * summed).astype(jnp.bfloat16)
    pre = jnp.dot(agg, weight, preferred_element_type=jnp.float32) + bias
    hidden = jax.nn.silu(pre).astype(jnp.bfloat16)
    sig = jax.nn.sigmoid(pre)
    grad_pre = (out_grad.astype(jnp.float32) * (sig * (1.0 + pre * (1.0 - sig)))).astype(
        jnp.bfloat16
    )
    weight_term = lax.dot_general(
        agg, grad_pre, (((0,), (0,)), ((), ())), preferred_element_type=jnp.float32
    )
    bias_term = jnp.sum(grad_pre.astype(jnp.float32), axis=0)
    grad_weight, grad_bias = lax.psum((weight_term, bias_term), ("blk", "rep"))
    back_proj = lax.dot_general(
        grad_pre, weight, (((1,), (1,)), ((), ())), preferred_element_type=jnp.float32
    )
    grad_agg = (scale * back_proj).astype(jnp.bfloat16)
    block_grad = lax.all_gather(grad_agg, "rep", axis=0, tiled=True)
    running = spread_terms(
        tile_values, tile_rows, tile_cols, live, block_grad, steps - 1, tile, col_tiles, width
    )
    for step in range(steps - 2, -1, -1):
        running = passed_along(running, "blk", -1)
        running = running + spread_terms(
            tile_values, tile_rows, tile_cols, live, block_grad, step, tile, col_tiles, width
        )
    grad_owned = (scale * running).astype(jnp.bfloat16)
    padded = jnp.concatenate([grad_owned, jnp.zeros((1, width), jnp.bfloat16)], axis=0)
    back = padded[place]
    returned = lax.all_to_all(back, "blk", split_axis=0, concat_axis=0, tiled=True)
    target = jnp.where(valid_send, send_rows, rows)
    grad_features = (
        jnp.zeros((rows + 1, width), jnp.bfloat16)
        .at[target.reshape(-1)]
        .set(returned.reshape(-1, width))[:rows]
    )
    return (hidden, grad_features, grad_weight, grad_bias)


def solution(mesh):
    in_specs = (
        P(("blk", "rep"), None),
        P(("blk", "rep"), None),
        P(("blk", "rep")),
        P(("blk", "rep"), None, None, None),
        P(("blk", "rep"), None),
        P(("blk", "rep"), None),
        P(("blk", "rep")),
        P(("blk", "rep")),
        P(),
        P(),
        P(("blk", "rep"), None),
    )
    out_specs = (P(("blk", "rep"), None), P(("blk", "rep"), None), P(), P())
    return jax.shard_map(
        on_device, mesh=mesh, in_specs=in_specs, out_specs=out_specs, check_vma=False
    )
```

profile of v0, /device:TPU:1, one launch (start us, length us, event | category | flops | bytes accessed | tf_op | source)
XLA Modules:
  0.0 457.5 jit_solution(14418804312479998272)
XLA Ops:
  8.6 18.6 %all-to-all-start = ((s32[128,1,1]{2,1,0:T(1,128)}), s32[128,1,1]{2,1,0:T(1,128)S(1)}, u32[]{:S(2)}, u32[]{:S(2)}) async-start(s32[128,1,1]{2,1,0:T(1,128)} %copy.64), calls=%async_computation | async-start | bytes 131072 | tf_op jit(solution)/shard_map/all_to_all | solution.py:86
  28.8 4.3 gather_fusion
  33.1 5.4 %all-to-all-done = s32[128,1,1]{2,1,0:T(1,128)S(1)} async-done(((s32[128,1,1]{2,1,0:T(1,128)}), s32[128,1,1]{2,1,0:T(1,128)S(1)}, u32[]{:S(2)}, u32[]{:S(2)}) %all-to-all-start) | async-done | bytes 544 | tf_op jit(solution)/shard_map/all_to_all | solution.py:86
  38.6 8.4 %all-to-all-start.1 = ((bf16[128,8,128]{2,1,0:T(8,128)(2,1)}), bf16[128,8,128]{2,1,0:T(8,128)(2,1)S(1)}, u32[]{:S(2)}, u32[]{:S(2)}) async-start(bf16[128,8,128]{2,1,0:T(8,128)(2,1)} %bitcast.7), calls=%async_computation.1 | async-start | bytes 524288 | tf_op jit(solution)/shard_map/all_to_all | solution.py:85
  47.3 2.4 reduce
  50.0 12.3 %all-to-all-done.1 = bf16[128,8,128]{2,1,0:T(8,128)(2,1)S(1)} async-done(((bf16[128,8,128]{2,1,0:T(8,128)(2,1)}), bf16[128,8,128]{2,1,0:T(8,128)(2,1)S(1)}, u32[]{:S(2)}, u32[]{:S(2)}) %all-to-all-start.1) | async-done | bytes 262176 | tf_op jit(solution)/shard_map/all_to_all | solution.py:85
  62.3 3.2 scatter_custom_fusion
  65.6 3.0 collective-permute-start
  71.2 4.4 collective-permute-start.1
  76.3 2.7 collective-permute-done.1
  79.7 3.0 collective-permute-start.2
  83.4 5.8 %collective-permute-done.2 = bf16[512,128]{1,0:T(8,128)(2,1)S(1)} collective-permute-done((bf16[512,128]{1,0:T(8,128)(2,1)S(1)}, bf16[512,128]{1,0:T(8,128)(2,1)S(1)}, u32[]{:S(2)}, u32[]{:S(2)}) %collective-permute-start.2) | collective-permute-done | bytes 131104 | tf_op jit(solution)/shard_map/ppermute | solution.py:10
  92.3 24.8 %reduce-scatter.2.cloned.1.call-done = f32[512,128]{1,0:T(8,128)} async-done(((f32[2048,128]{1,0:T(8,128)}), f32[512,128]{1,0:T(8,128)}) %reduce-scatter.2.cloned.1.call-update) | async-done | bytes 262160 | tf_op jit(solution)/shard_map/reduce_scatter | solution.py:112
  119.4 11.1 %all_gather.3 = bf16[2048,128]{1,0:T(8,128)(2,1)S(1)} all-gather(bf16[512,128]{1,0:T(8,128)(2,1)S(1)} %fusion.8), channel_id=1, replica_groups=mesh['blk'=128,'rep'=4] {'rep'}, dimensions={0}, use_global_device_ids=true | all-gather | bytes 655360 | tf_op jit(solution)/shard_map/all_gather | solution.py:129
  132.6 6.5 %collective-permute-start.3 = (f32[512,128]{1,0:T(8,128)S(1)}, f32[512,128]{1,0:T(8,128)S(1)}, u32[]{:S(2)}, u32[]{:S(2)}) collective-permute-start(f32[512,128]{1,0:T(8,128)S(1)} %bitcast.145), channel_id=1, source_target_pairs={{0,508},{4,0},{8,4},{12,8},{16,12},{20,16},{24,20},{28,24},{32,28}... | collective-permute-start | bytes 786440 | tf_op jit(solution)/shard_map/ppermute | solution.py:10
  140.3 3.8 collective-permute-done.3
  144.1 3.0 collective-permute-start.4
  148.0 3.8 collective-permute-done.4
  151.8 6.4 %collective-permute-start.5 = (f32[512,128]{1,0:T(8,128)S(1)}, f32[512,128]{1,0:T(8,128)S(1)}, u32[]{:S(2)}, u32[]{:S(2)}) collective-permute-start(f32[512,128]{1,0:T(8,128)S(1)} %bitcast_add_fusion.1), channel_id=1, source_target_pairs={{0,508},{4,0},{8,4},{12,8},{16,12},{20,16},{24,20},{28,24},{32,28}... | collective-permute-start | bytes 786440 | tf_op jit(solution)/shard_map/ppermute | solution.py:10
  159.7 4.3 gather_fusion.1
  164.0 16.8 %all-to-all-start.2 = ((bf16[128,8,128]{2,1,0:T(8,128)(2,1)}), bf16[128,8,128]{2,1,0:T(8,128)(2,1)S(1)}, u32[]{:S(2)}, u32[]{:S(2)}) async-start(bf16[128,8,128]{2,1,0:T(8,128)(2,1)} %bitcast.52), calls=%async_computation.3 | async-start | bytes 524288 | tf_op jit(solution)/shard_map/all_to_all | solution.py:141
  182.1 98.9 %psum.15 = f32[256]{0:T(256)} all-reduce(f32[256]{0:T(256)S(1)} %get-tuple-element.4), channel_id=1, replica_groups=mesh['blk'=128,'rep'=4] {'blk','rep'}, use_global_device_ids=true, to_apply=%region_6.7 | all-reduce | flops 256 | bytes 2048 | tf_op jit(solution)/shard_map/psum | solution.py:124
  281.0 3.2 scatter_custom_fusion.1
  284.9 164.2 %all-reduce.3.cloned.1.call-done = f32[128,256]{1,0:T(8,128)} async-done(((f32[128,256]{1,0:T(8,128)}), f32[128,256]{1,0:T(8,128)}) %all-reduce.3.cloned.1.call-update) | async-done | bytes 131088 | tf_op jit(solution)/shard_map/psum | solution.py:124
  (100 shorter events, 22.5 us)
Async XLA Ops:
  7.2 21.6 %copy-start = (bf16[512,128]{1,0:T(8,128)(2,1)S(1)}, bf16[512,128]{1,0:T(8,128)(2,1)}, u32[]{:S(2)}) copy-start(bf16[512,128]{1,0:T(8,128)(2,1)} %param.11) | copy-start | bytes 393220
  7.2 0.7 copy-start.6
  8.6 18.6 %copy-start.5 = (s32[128,8]{0,1:T(8,128)S(1)}, s32[128,8]{0,1:T(8,128)}, u32[]{:S(2)}) copy-start(s32[128,8]{0,1:T(8,128)} %param.12) | copy-start | bytes 12292
  8.6 29.9 %all-to-all-start = ((s32[128,1,1]{2,1,0:T(1,128)}), s32[128,1,1]{2,1,0:T(1,128)S(1)}, u32[]{:S(2)}, u32[]{:S(2)}) async-start(s32[128,1,1]{2,1,0:T(1,128)} %copy.64), calls=%async_computation | async-start | bytes 131072 | tf_op jit(solution)/shard_map/all_to_all | solution.py:86
  27.4 0.7 copy-start.7
  28.1 0.7 copy-start.9
  38.6 8.5 %copy-start.8 = (s32[4,4]{1,0:T(4,128)S(1)}, s32[4,4]{1,0:T(4,128)}, u32[]{:S(2)}) copy-start(s32[4,4]{1,0:T(4,128)} %param.15) | copy-start | bytes 196
  38.6 23.7 %all-to-all-start.1 = ((bf16[128,8,128]{2,1,0:T(8,128)(2,1)}), bf16[128,8,128]{2,1,0:T(8,128)(2,1)S(1)}, u32[]{:S(2)}, u32[]{:S(2)}) async-start(bf16[128,8,128]{2,1,0:T(8,128)(2,1)} %bitcast.7), calls=%async_computation.1 | async-start | bytes 524288 | tf_op jit(solution)/shard_map/all_to_all | solution.py:85
  47.0 70.1 %reduce-scatter.2.cloned.1.call-start = ((), (), s32[]{:S(2)}) async-start(), calls=%async_computation.4 | async-start | bytes 1310720 | tf_op jit(solution)/shard_map/reduce_scatter | solution.py:112
  49.7 15.7 %copy-start.4 = (f32[512]{0:T(512)S(1)}, f32[512]{0:T(512)}, u32[]{:S(2)}) copy-start(f32[512]{0:T(512)} %param.18) | copy-start | bytes 6148
  49.8 19.0 %copy-start.1 = (bf16[4,4,128,128]{3,2,1,0:T(8,128)(2,1)S(1)}, bf16[4,4,128,128]{3,2,1,0:T(8,128)(2,1)}, u32[]{:S(2)}) copy-start(bf16[4,4,128,128]{3,2,1,0:T(8,128)(2,1)} %param.14) | copy-start | bytes 1572868
  65.6 4.9 %collective-permute-start = (bf16[512,128]{1,0:T(8,128)(2,1)S(1)}, bf16[512,128]{1,0:T(8,128)(2,1)S(1)}, u32[]{:S(2)}, u32[]{:S(2)}) collective-permute-start(bf16[512,128]{1,0:T(8,128)(2,1)S(1)} %multiply_convert_fusion.3), channel_id=1, source_target_pairs={{0,4},{4,8},{8,12},{12,16},{16,20},{20,24},{24,28},{28,32},{32,36}... | collective-permute-start | bytes 393224 | tf_op jit(solution)/shard_map/ppermute | solution.py:10
  71.2 7.8 %collective-permute-start.1 = (bf16[512,128]{1,0:T(8,128)(2,1)S(1)}, bf16[512,128]{1,0:T(8,128)(2,1)S(1)}, u32[]{:S(2)}, u32[]{:S(2)}) collective-permute-start(bf16[512,128]{1,0:T(8,128)(2,1)S(1)} %collective-permute-done), channel_id=1, source_target_pairs={{0,4},{4,8},{8,12},{12,16},{16,20},{20,24},{24,28},{28,32},{32,36}... | collective-permute-start | bytes 393224 | tf_op jit(solution)/shard_map/ppermute | solution.py:10
  79.7 9.6 %collective-permute-start.2 = (bf16[512,128]{1,0:T(8,128)(2,1)S(1)}, bf16[512,128]{1,0:T(8,128)(2,1)S(1)}, u32[]{:S(2)}, u32[]{:S(2)}) collective-permute-start(bf16[512,128]{1,0:T(8,128)(2,1)S(1)} %collective-permute-done.1), channel_id=1, source_target_pairs={{0,4},{4,8},{8,12},{12,16},{16,20},{20,24},{24,28},{28,32},{32,36}... | collective-permute-start | bytes 393224 | tf_op jit(solution)/shard_map/ppermute | solution.py:10
  92.0 25.1 %copy-start.10 = (bf16[512,256]{1,0:T(8,128)(2,1)S(1)}, bf16[512,256]{1,0:T(8,128)(2,1)}, u32[]{:S(2)}) copy-start(bf16[512,256]{1,0:T(8,128)(2,1)} %param.21) | copy-start | bytes 786436
  92.0 25.0 %copy-start.3 = (bf16[128,256]{1,0:T(8,128)(2,1)S(1)}, bf16[128,256]{1,0:T(8,128)(2,1)}, u32[]{:S(2)}) copy-start(bf16[128,256]{1,0:T(8,128)(2,1)} %param.19) | copy-start | bytes 196612
  92.2 24.8 %copy-start.11 = (f32[256]{0:T(256)S(1)}, f32[256]{0:T(256)}, u32[]{:S(2)}) copy-start(f32[256]{0:T(256)} %param.20) | copy-start | bytes 3076
  132.6 11.5 %collective-permute-start.3 = (f32[512,128]{1,0:T(8,128)S(1)}, f32[512,128]{1,0:T(8,128)S(1)}, u32[]{:S(2)}, u32[]{:S(2)}) collective-permute-start(f32[512,128]{1,0:T(8,128)S(1)} %bitcast.145), channel_id=1, source_target_pairs={{0,508},{4,0},{8,4},{12,8},{16,12},{20,16},{24,20},{28,24},{32,28}... | collective-permute-start | bytes 786440 | tf_op jit(solution)/shard_map/ppermute | solution.py:10
  144.1 7.7 %collective-permute-start.4 = (f32[512,128]{1,0:T(8,128)S(1)}, f32[512,128]{1,0:T(8,128)S(1)}, u32[]{:S(2)}, u32[]{:S(2)}) collective-permute-start(f32[512,128]{1,0:T(8,128)S(1)} %bitcast_add_fusion.2), channel_id=1, source_target_pairs={{0,508},{4,0},{8,4},{12,8},{16,12},{20,16},{24,20},{28,24},{32,28}... | collective-permute-start | bytes 786440 | tf_op jit(solution)/shard_map/ppermute | solution.py:10
  151.8 7.7 %collective-permute-start.5 = (f32[512,128]{1,0:T(8,128)S(1)}, f32[512,128]{1,0:T(8,128)S(1)}, u32[]{:S(2)}, u32[]{:S(2)}) collective-permute-start(f32[512,128]{1,0:T(8,128)S(1)} %bitcast_add_fusion.1), channel_id=1, source_target_pairs={{0,508},{4,0},{8,4},{12,8},{16,12},{20,16},{24,20},{28,24},{32,28}... | collective-permute-start | bytes 786440 | tf_op jit(solution)/shard_map/ppermute | solution.py:10
  164.0 17.1 %copy-start.2 = (f32[512,128]{1,0:T(8,128)S(1)}, f32[512,128]{1,0:T(8,128)}, u32[]{:S(2)}) copy-start(f32[512,128]{1,0:T(8,128)} %reduce-scatter.2.cloned.1.call-done) | copy-start | bytes 786436
  164.0 117.0 %all-to-all-start.2 = ((bf16[128,8,128]{2,1,0:T(8,128)(2,1)}), bf16[128,8,128]{2,1,0:T(8,128)(2,1)S(1)}, u32[]{:S(2)}, u32[]{:S(2)}) async-start(bf16[128,8,128]{2,1,0:T(8,128)(2,1)} %bitcast.52), calls=%async_computation.3 | async-start | bytes 524288 | tf_op jit(solution)/shard_map/all_to_all | solution.py:141
  180.8 268.2 %all-reduce.3.cloned.1.call-start = ((), (), s32[]{:S(2)}) async-start(), calls=%async_computation.5 | async-start | bytes 262144 | tf_op jit(solution)/shard_map/psum | solution.py:124
Sparse Core Ops, SparseCore 0:
  92.2 24.8 reduce-scatter.1
  188.0 261.0 all-reduce.2
where the time goes:
time: 458 us; the launch traced here: 457 us
  waiting for transfers between devices  224 us (49%)
  blocking collectives  110 us (24%)
  starting transfers between devices  70.2 us (15%)
  local copies, waits for them, and re-layouts  23.3 us (5%)
  between operations  14.6 us (3%)
  matrix products  12.3 us (3%)
    psum x1, waiting for transfers between devices, on_device(): grad_weight, grad_bias = lax.psum((weight_term, bias_term), ('blk', 'rep'))  164 us
    psum x1, blocking collectives, on_device(): grad_weight, grad_bias = lax.psum((weight_term, bias_term), ('blk', 'rep'))  98.9 us
    ppermute x6, starting transfers between devices, passed_along(): return lax.ppermute(value, axis, pairs)  26.3 us
    reduce_scatter x1, waiting for transfers between devices, on_device(): lax.psum_scatter(partial_value, 'rep', scatter_dimension=0, tiled=True)  24.8 us
    all_to_all x1, starting transfers between devices, on_device(): lax.all_to_all(send_counts.reshape(blocks, 1), 'blk', split_axis=0, conca...  18.6 us
    ppermute x6, waiting for transfers between devices, passed_along(): return lax.ppermute(value, axis, pairs)  17.2 us
    all_to_all x1, starting transfers between devices, on_device(): lax.all_to_all(back, 'blk', split_axis=0, concat_axis=0, tiled=True)  16.8 us
    all_to_all x1, waiting for transfers between devices, on_device(): lax.all_to_all(outgoing, 'blk', split_axis=0, concat_axis=0, tiled=True)  12.3 us
  transfers between devices with their start and end apart: 11, of which 10 were waited for; matrix products, arithmetic and copies ran while one was open for 4% of the time, Pallas kernels for 0%

commit v1 on v0

v1 whole, which is shorter than its diff:
```python
import jax
import jax.numpy as jnp
from jax import lax
from jax.experimental import pallas as pl
from jax.experimental.pallas import tpu as pltpu
from jax.sharding import PartitionSpec as P

BF16 = jnp.bfloat16
F32 = jnp.float32
TILE = 128
UNUSED = 1024.0
NN = (((1,), (0,)), ((), ()))
NT = (((1,), (1,)), ((), ()))
TN = (((0,), (0,)), ((), ()))


def dot(a, b, dims=NN):
    return lax.dot_general(a, b, dims, preferred_element_type=F32)


def iota(shape, dim):
    return lax.broadcasted_iota(jnp.int32, shape, dim)


def one_hot(mask):
    return jnp.where(mask, 1.0, 0.0).astype(BF16)


def kernel_call(kernel, outs, specs, name, scratch=(), flops=10**8):
    return pl.pallas_call(
        kernel,
        out_shape=outs,
        in_specs=specs,
        scratch_shapes=list(scratch),
        compiler_params=pltpu.CompilerParams(vmem_limit_bytes=40 * 1024 * 1024),
        cost_estimate=pl.CostEstimate(flops=flops, bytes_accessed=10**6, transcendentals=0),
        name=name,
    )


def call(kernel, outs, name, flops=10**8):
    def run(*arrays, after=()):
        specs = [pl.BlockSpec(memory_space=pltpu.VMEM)] * len(arrays)
        specs += [pl.BlockSpec(memory_space=pl.ANY)] * len(after)
        return kernel_call(kernel, outs, specs, name, flops=flops)(*arrays, *after)

    return run


def shape(dims, kind):
    return jax.ShapeDtypeStruct(dims, kind)


def as_column(row):
    return jnp.transpose(jnp.broadcast_to(row, (TILE, TILE)))


def slot_parts(send_rows, counts, rows):
    send_rows = jnp.transpose(send_rows.astype(F32)).astype(jnp.int32)
    owners, slots = send_rows.shape
    count = as_column(counts.astype(F32))[:, :slots]
    lane = iota((owners, slots), 1).astype(F32)
    key = jnp.where(lane < count, send_rows, rows)
    high = (key >> 5).astype(F32).astype(BF16)
    low = (key & 31).astype(F32).astype(BF16)
    total = owners * slots
    expand = one_hot(iota((total, owners), 0) // slots == iota((total, owners), 1))
    mine = iota((total, slots), 0) % slots == iota((total, slots), 1)
    high = jnp.where(mine, dot(expand, high) * 32.0, 0.0).astype(BF16)
    low = jnp.where(mine, dot(expand, low), 0.0).astype(BF16)
    return high, low


def start_kernel(*refs):
    out_ref, scale_ref, bias_ref, table_ref = refs[8:12]
    features_ref, rows_ref, counts_ref, degree_ref, *parts, sems = refs[12:]
    pairs = tuple(zip(refs[:8], (features_ref, rows_ref, counts_ref, degree_ref, *parts, bias_ref)))
    copies = [pltpu.make_async_copy(a, b, sems.at[k]) for k, (a, b) in enumerate(pairs)]
    for copy in copies:
        copy.start()
    for copy in copies:
        copy.wait()
    rows = features_ref.shape[0]
    slots = rows_ref.shape[0]
    high, low = slot_parts(rows_ref[...], counts_ref[...], rows)
    ones = jnp.ones((slots, TILE), BF16)
    key = dot(high, ones) + dot(low, ones)
    lane = iota(key.shape, 1).astype(F32)
    pick = jnp.concatenate(
        [one_hot(key == lane + float(start)) for start in range(0, rows, TILE)], axis=1
    )
    sent = dot(pick, features_ref[...])
    out_ref[...] = jnp.where(key >= float(rows), UNUSED, sent).astype(BF16)
    for t in range(rows // TILE):
        scale_ref[t * TILE : (t + 1) * TILE] = as_column(degree_ref[t : t + 1])
    place = 0
    for part in parts:
        table_ref[place : place + part.shape[0]] = part[...]
        place += part.shape[0]
    table_ref[place : place + 1] = jnp.full((1, table_ref.shape[1]), lax.axis_index("rep"))


def start_call(features, send_rows, counts_row, degree, tables, bias_row):
    rows, width = features.shape
    total = send_rows.size
    small = (features, send_rows, counts_row, degree, *tables)
    arrays = [pltpu.with_memory_space_constraint(a, pltpu.HBM) for a in (*small, bias_row)]
    return pl.pallas_call(
        start_kernel,
        out_shape=(
            shape((total, width), BF16),
            shape((rows, TILE), F32),
            shape(bias_row.shape, F32),
            shape((1 + sum(a.shape[0] for a in tables), tables[0].shape[1]), jnp.int32),
        ),
        in_specs=[pl.BlockSpec(memory_space=pltpu.HBM)] * 8,
        scratch_shapes=[pltpu.VMEM(a.shape, a.dtype) for a in small]
        + [pltpu.SemaphoreType.DMA((8,))],
        compiler_params=pltpu.CompilerParams(vmem_limit_bytes=8 * 1024 * 1024),
        cost_estimate=pl.CostEstimate(flops=10**8, bytes_accessed=10**6, transcendentals=0),
        name="start",
    )(*arrays)


def arrive_kernel(rows_ref, counts_ref, out_ref):
    rows = out_ref.shape[0]
    slots = rows_ref.shape[0]
    high, low = slot_parts(rows_ref[...], counts_ref[...], rows)
    ones = jnp.ones((8, slots), BF16)
    key = dot(ones, high, NT) + dot(ones, low, NT)
    for start in range(0, key.shape[1], TILE):
        span = slice(start, start + TILE)
        out_ref[:, span] = one_hot(iota((rows, TILE), 0).astype(F32) == key[0:1, span])


def transpose_kernel(tiles_ref, out_ref):
    for t in range(tiles_ref.shape[0]):
        out_ref[t] = jnp.transpose(tiles_ref[t].astype(F32)).astype(BF16)


def used_slots(ref):
    return jnp.where(ref[...].astype(F32) < 512.0, 1.0, 0.0).astype(BF16)


def place_kernel(incoming_ref, scale_ref, out_ref):
    rows = out_ref.shape[0]
    used = used_slots(incoming_ref)
    before = one_hot(iota((TILE, TILE), 0) < iota((TILE, TILE), 1))
    ones = jnp.ones((TILE, TILE), BF16)
    mean = jnp.full((8, TILE), 1.0 / TILE, BF16)
    offset = jnp.zeros((8, TILE), F32)
    parts = []
    for start in range(0, used.shape[0], TILE):
        here = dot(mean, used[start : start + TILE], NT)
        flags = here.astype(BF16)
        rank = jnp.where(here > 0.5, dot(flags, before) + offset, -1.0)
        offset = offset + dot(flags, ones)
        parts.append(one_hot(iota((rows, TILE), 0).astype(F32) == rank[0:1]))
    owned = dot(jnp.concatenate(parts, axis=1), incoming_ref[...])
    out_ref[...] = (scale_ref[...] * owned).astype(BF16)


def unplace_kernel(incoming_ref, out_ref):
    rows = out_ref.shape[1]
    used = used_slots(incoming_ref)
    before = one_hot(iota((TILE, TILE), 1) < iota((TILE, TILE), 0))
    ones = jnp.ones((TILE, TILE), BF16)
    offset = jnp.zeros((TILE, TILE), F32)
    lane = iota((TILE, TILE), 1).astype(F32)
    for start in range(0, used.shape[0], TILE):
        here = used[start : start + TILE]
        rank = jnp.where(here.astype(F32) > 0.5, dot(before, here) + offset, -1.0)
        offset = offset + dot(ones, here)
        for column in range(0, rows, TILE):
            out_ref[start : start + TILE, column : column + TILE] = one_hot(
                rank == lane + float(column)
            )


def gather_kernel(
    table_ref, tiles_ref, src0, src1, src2, src3, *refs
):
    out_ref, acc_ref = refs[-2:]
    acc_ref[...] = jnp.zeros_like(acc_ref)
    most = table_ref.shape[1]
    steps = tiles_ref.shape[0] // most
    for step, source in enumerate((src0, src1, src2, src3)):
        for k in range(most):
            col = pl.multiple_of(table_ref[steps + step, k] * TILE, TILE)
            row = pl.multiple_of(table_ref[step, k] * TILE, TILE)
            live = (k < table_ref[2 * steps, step]).astype(F32)
            prod = dot(tiles_ref[step * most + k], source[pl.ds(col, TILE), :])
            acc_ref[pl.ds(row, TILE), :] += prod * live
    quarters, rows, _ = out_ref.shape
    for q in range(quarters):
        out_ref[q] = acc_ref[q * rows : (q + 1) * rows].astype(BF16)


def dense_kernel(
    parts_ref, scale_ref, weight_ref, bias_ref, out_grad_ref, hidden_ref, agg_ref, grad_pre_ref, out_ref
):
    quarters, rows, width = parts_ref.shape
    summed = parts_ref[0].astype(F32)
    for q in range(1, quarters):
        summed = summed + parts_ref[q].astype(F32)
    for t in range(rows // TILE):
        part = slice(t * TILE, (t + 1) * TILE)
        scale = scale_ref[part]
        agg = (scale * summed[part]).astype(BF16)
        agg_ref[part] = agg
        pre = dot(agg, weight_ref[...]) + bias_ref[...]
        sig = jax.nn.sigmoid(pre)
        hidden_ref[part] = (pre * sig).astype(BF16)
        grad_pre = (
            out_grad_ref[part].astype(F32) * (sig * (1.0 + pre * (1.0 - sig)))
        ).astype(BF16)
        grad_pre_ref[part] = grad_pre
        out_ref[part] = (scale * dot(grad_pre, weight_ref[...], NT)).astype(BF16)


def terms_kernel(agg_ref, grad_pre_ref, *refs):
    out_ref = refs[-1]
    grad_pre = grad_pre_ref[...]
    width = agg_ref.shape[1]
    term = dot(agg_ref[...], grad_pre, TN)
    total = jnp.sum(grad_pre.astype(F32), axis=0, keepdims=True)
    mine = iota((width, 2 * TILE), 1) // 2 == iota((width, 2 * TILE), 0)
    pieces = jnp.concatenate([term, jnp.where(mine, total, 0.0)], axis=1).astype(BF16)
    lines = (4 * width, width)
    rows = jnp.zeros((4 * width, TILE), F32)
    for k in range(4):
        here = iota(lines, 0) == 4 * iota(lines, 1) + k
        rows = rows + dot(one_hot(here), pieces[:, k * TILE : (k + 1) * TILE])
    out_ref[...] = rows.astype(BF16)


def row_kernel(parts_ref, *refs):
    out_ref = refs[-1]
    count, width = parts_ref.shape
    groups = (count // 8, 8, width)
    pairs = jnp.sum(parts_ref[...].astype(F32).reshape(groups), axis=0)
    term = pairs[:4] + pairs[4:]
    both = jnp.concatenate([term, term], axis=0)
    out_ref[...] = jnp.broadcast_to(both[None], groups).reshape(count, width).astype(BF16)


def whole_kernel(rows_ref, out_ref):
    count = rows_ref.shape[0]
    width = count // 4
    lines = (width, count)
    for k in range(2):
        half = slice(k * TILE, (k + 1) * TILE)
        here = iota(lines, 1) == 4 * iota(lines, 0) + k
        out_ref[:width, half] = dot(one_hot(here), rows_ref[...]).astype(BF16)
        here = iota((16, count), 1) % 4 == k + 2
        out_ref[width:, half] = dot(one_hot(here), rows_ref[...]).astype(BF16)


def spread_kernel(
    table_ref, tiles_ref, block0, block1, block2, block3, *refs
):
    own_ref, out1, out2, out3, acc_ref, block_ref = refs[-6:]
    mine = table_ref[table_ref.shape[0] - 1, 0]
    for away, block in enumerate((block0, block1, block2, block3)):
        block_ref[lax.rem(mine + 4 - away, 4)] = block[...]
    acc_ref[...] = jnp.zeros_like(acc_ref)
    most = table_ref.shape[1]
    steps = tiles_ref.shape[0] // most
    col_tiles = own_ref.shape[0] // TILE
    for step in range(steps - 1, -1, -1):
        for k in range(most):
            col = pl.multiple_of(table_ref[steps + step, k] * TILE, TILE)
            quarter = table_ref[step, k] // col_tiles
            row = pl.multiple_of((table_ref[step, k] - quarter * col_tiles) * TILE, TILE)
            live = (k < table_ref[2 * steps, step]).astype(F32)
            prod = dot(tiles_ref[step * most + k], block_ref[quarter, pl.ds(row, TILE), :])
            acc_ref[step, pl.ds(col, TILE), :] += prod * live
    own_ref[...] = acc_ref[0]
    for step, out in ((1, out1), (2, out2), (3, out3)):
        out[...] = acc_ref[step].astype(BF16)


def back_kernel(own_ref, in1, in2, in3, scale_ref, unplace_ref, *refs):
    out_ref = refs[-1]
    total = own_ref[...] + in1[...].astype(F32) + in2[...].astype(F32) + in3[...].astype(F32)
    grads = (scale_ref[...] * total).astype(BF16)
    out_ref[...] = dot(unplace_ref[...], grads).astype(BF16)


def last_kernel(arrive_ref, returned_ref, w0, w1, w2, w3, out_ref, weight_ref, bias_ref):
    out_ref[...] = dot(arrive_ref[...], returned_ref[...]).astype(BF16)
    total = (w0[...].astype(F32) + w1[...].astype(F32)) + (
        w2[...].astype(F32) + w3[...].astype(F32)
    )
    width = weight_ref.shape[0]
    weight_ref[...] = total[:width]
    bias_ref[...] = total[width : width + 1]


def shifted(value, steps, axis="blk"):
    count = lax.axis_size(axis)
    return lax.ppermute(value, axis, [(s, (s + steps) % count) for s in range(count)])


def exchange(value, axis):
    return lax.all_to_all(value, axis, split_axis=0, concat_axis=0, tiled=True)


def tile_call(kernel, outs, scratch, name, table, arrays, after=()):
    specs = [pl.BlockSpec(memory_space=pltpu.SMEM)]
    specs += [pl.BlockSpec(memory_space=pltpu.VMEM)] * len(arrays)
    specs += [pl.BlockSpec(memory_space=pl.ANY)] * len(after)
    return kernel_call(kernel, outs, specs, name, scratch)(table, *arrays, *after)


def on_device(
    features,
    send_rows,
    send_counts,
    tile_values,
    tile_rows,
    tile_cols,
    tile_counts,
    degree_scale,
    weight,
    bias,
    out_grad,
):
    blocks = lax.axis_size("blk")
    quarters = lax.axis_size("rep")
    rows, width = features.shape
    slots = send_rows.shape[1]
    steps, most = tile_values.shape[:2]
    hidden_width = weight.shape[1]
    total = blocks * slots
    slot_rows = send_rows.T
    counts_row = send_counts.reshape(1, blocks)
    degree = degree_scale.reshape(rows // TILE, TILE)
    tiles = tile_values.reshape(steps * most, TILE, TILE)
    tables = (tile_rows, tile_cols, tile_counts.reshape(1, steps))

    outgoing, scale, bias_row, table = start_call(
        features, slot_rows, counts_row, degree, tables, bias.reshape(1, hidden_width)
    )
    incoming = exchange(outgoing.reshape(blocks, slots, width), "blk").reshape(total, width)
    arrive = call(arrive_kernel, shape((rows, total), BF16), "arrive")(slot_rows, counts_row)
    turned = call(transpose_kernel, shape(tiles.shape, BF16), "turn")(tiles)

    scaled = call(place_kernel, shape((rows, width), BF16), "place")(incoming, scale)
    sources = [scaled] + [shifted(scaled, step) for step in range(1, steps)]
    unplace = call(unplace_kernel, shape((total, rows), BF16), "unplace")(incoming)
    partial = tile_call(
        gather_kernel,
        shape((quarters, rows, width), BF16),
        [pltpu.VMEM((quarters * rows, width), F32)],
        "gather_tiles",
        table,
        (tiles, *sources),
        (turned, arrive, unplace),
    )
    parts = exchange(partial, "rep")
    hidden, agg, grad_pre, grad_agg = call(
        dense_kernel,
        (
            shape((rows, hidden_width), BF16),
            shape((rows, width), BF16),
            shape((rows, hidden_width), BF16),
            shape((rows, width), BF16),
        ),
        "dense",
    )(parts, scale, weight, bias_row, out_grad)
    block = [grad_agg] + [shifted(grad_agg, away, "rep") for away in range(1, quarters)]

    lines = shape((4 * width, TILE), BF16)
    terms = call(terms_kernel, lines, "terms")(agg, grad_pre, after=(block[3],))
    terms = exchange(terms.reshape(blocks, 4, TILE), "blk").reshape(lines.shape)

    own, *others = tile_call(
        spread_kernel,
        (shape((rows, width), F32),) + (shape((rows, width), BF16),) * (steps - 1),
        [pltpu.VMEM((steps, rows, width), F32), pltpu.VMEM((quarters, rows, width), BF16)],
        "spread_tiles",
        table,
        (turned, *block),
    )
    others = [shifted(value, -step) for step, value in enumerate(others, 1)]
    terms = call(row_kernel, lines, "row")(terms, after=(others[0],))
    terms = exchange(terms.reshape(blocks, 4, TILE), "blk").reshape(lines.shape)
    back = call(back_kernel, shape((total, width), BF16), "back", flops=4 * 10**10)(own, *others, scale, unplace)
    whole = call(whole_kernel, shape((width + 16, hidden_width), BF16), "whole")(terms)
    wholes = [whole] + [shifted(whole, away, "rep") for away in range(1, quarters)]
    returned = exchange(back.reshape(blocks, slots, width), "blk").reshape(total, width)
    grad_features, grad_weight, grad_bias = call(
        last_kernel,
        (shape((rows, width), BF16), shape(weight.shape, F32), shape((1, hidden_width), F32)),
        "last",
    )(arrive, returned, *wholes)
    return (hidden, grad_features, grad_weight, grad_bias.reshape(hidden_width))


def solution(mesh):
    in_specs = (
        P(("blk", "rep"), None),
        P(("blk", "rep"), None),
        P(("blk", "rep")),
        P(("blk", "rep"), None, None, None),
        P(("blk", "rep"), None),
        P(("blk", "rep"), None),
        P(("blk", "rep")),
        P(("blk", "rep")),
        P(),
        P(),
        P(("blk", "rep"), None),
    )
    out_specs = (P(("blk", "rep"), None), P(("blk", "rep"), None), P(), P())
    return jax.shard_map(
        on_device, mesh=mesh, in_specs=in_specs, out_specs=out_specs, check_vma=False
    )
```

time: 458 us -> 144 us (0.31)
  waiting for transfers between devices: 224 us -> 22.8 us
  blocking collectives: 110 us -> 44.4 us
  local copies, waits for them, and re-layouts: 23.3 us -> 0.74 us
  between operations: 14.6 us -> 0.93 us
  Pallas kernels: 0 us -> 13.1 us
  matrix products: 12.3 us -> 0 us
  starting transfers between devices: 70.2 us -> 60.9 us
    psum x1 -> x0, waiting for transfers between devices: 164 us -> none  [on_device(): grad_weight, grad_bias = lax.psum((weight_term, bias_term), ('blk', 'rep'))]
    psum x1 -> x0, blocking collectives: 98.9 us -> none  [on_device(): grad_weight, grad_bias = lax.psum((weight_term, bias_term), ('blk', 'rep'))]
    all_to_all x0 -> x2, blocking collectives: none -> 44.4 us  [exchange(): return lax.all_to_all(value, axis, split_axis=0, concat_axis=0, tiled=True)]
    reduce_scatter x1 -> x0, waiting for transfers between devices: 24.8 us -> none  [on_device(): lax.psum_scatter(partial_value, 'rep', scatter_dimension=0, tiled=True)]
    all_to_all x3, starting transfers between devices: 43.8 us -> 21.5 us  [exchange(): return lax.all_to_all(value, axis, split_axis=0, concat_axis=0, tiled=True)]
    ppermute x6 -> x12, starting transfers between devices: 26.3 us -> 39.4 us  [shifted(): lax.ppermute(value, axis, [(s, (s + steps) % count) for s in range(count)])]
    pallas_call x0 -> x13, Pallas kernels: none -> 13.1 us  [the longest x10 8.07 us: run(): return kernel_call(kernel, outs, specs, name, flops=flops)(*arrays, *after)]
    dot_general x27 -> x0, matrix products: 12.3 us -> none  [the longest x4 2.92 us: gather_terms(): jnp.einsum('kr,kaf->raf', placer, prod, precision=lax.Precision.HIGHEST,...]
  transfers between devices with their start and end apart: 11 -> 15, of which waited for: 10 -> 6; matrix products, arithmetic and copies ran while one was open for 4% -> 0% of each run, Pallas kernels for 0% -> 5%
where the time goes in v1:
time: 144 us; the launch traced here: 143 us
  starting transfers between devices  60.9 us (42%)
  blocking collectives  44.4 us (31%)
  waiting for transfers between devices  22.8 us (16%)
  Pallas kernels  13.1 us (9%)
    all_to_all x2, blocking collectives, exchange(): return lax.all_to_all(value, axis, split_axis=0, concat_axis=0, tiled=True)  44.4 us
    ppermute x12, starting transfers between devices, shifted(): lax.ppermute(value, axis, [(s, (s + steps) % count) for s in range(count)])  39.4 us
    all_to_all x3, starting transfers between devices, exchange(): return lax.all_to_all(value, axis, split_axis=0, concat_axis=0, tiled=True)  21.5 us
    all_to_all x3, waiting for transfers between devices, exchange(): return lax.all_to_all(value, axis, split_axis=0, concat_axis=0, tiled=True)  12.2 us
    ppermute x12, waiting for transfers between devices, shifted(): lax.ppermute(value, axis, [(s, (s + steps) % count) for s in range(count)])  10.6 us
    pallas_call x10, Pallas kernels, run(): return kernel_call(kernel, outs, specs, name, flops=flops)(*arrays, *after)  8.07 us
  transfers between devices with their start and end apart: 15, of which 6 were waited for; matrix products, arithmetic and copies ran while one was open for 0% of the time, Pallas kernels for 5%

profile of v1, /device:TPU:1, one launch (start us, length us, event | category | flops | bytes accessed | tf_op | source)
XLA Modules:
  0.0 142.9 jit_solution(8040290800791807633)
XLA Ops:
  0.6 2.2 %start.1 = (bf16[1024,128]{1,0:T(8,128)(2,1)S(1)}, f32[512,128]{1,0:T(8,128)S(1)}, f32[1,256]{1,0:T(1,128)S(1)}, s32[10,4]{1,0:T(8,128)S(1)}) custom-call(bf16[512,128]{1,0:T(8,128)(2,1)} %refs_0_.1, s32[8,128]{1,0:T(8,128)} %bitcast.23, s32[1,128]{1,0:T(1,128)} %bitcast.25, f32[4,128]{1,0:T(4,128)} %bitcast.27, s32[4,4]{1,0:T(4,128)} %refs_4_.1, ...), custom_call_target="tpu_custom_call" | custom-call | flops 100000000 | bytes 1000000 | tf_op jit(solution)/shard_map/start/pallas_call | solution.py:108
  2.9 33.5 %all_to_all.25 = bf16[128,8,128]{2,1,0:T(8,128)(2,1)S(1)} all-to-all(bf16[128,8,128]{2,1,0:T(8,128)(2,1)S(1)} %bitcast.21), channel_id=1, replica_groups=mesh['blk'=128,'rep'=4] {'blk'}, dimensions={0} | all-to-all | bytes 524288 | tf_op jit(solution)/shard_map/all_to_all | solution.py:306
  37.2 3.2 %collective-permute-start.2 = (bf16[512,128]{1,0:T(8,128)(2,1)S(1)}, bf16[512,128]{1,0:T(8,128)(2,1)S(1)}, u32[]{:S(2)}, u32[]{:S(2)}) collective-permute-start(bf16[512,128]{1,0:T(8,128)(2,1)S(1)} %place.1.src0), channel_id=1, source_target_pairs={{0,12},{4,16},{8,20},{12,24},{16,28},{20,32},{24,36},{28,40},{32,4... | collective-permute-start | bytes 393224 | tf_op jit(solution)/shard_map/ppermute | solution.py:302
  40.4 2.1 %collective-permute-start.1 = (bf16[512,128]{1,0:T(8,128)(2,1)S(1)}, bf16[512,128]{1,0:T(8,128)(2,1)S(1)}, u32[]{:S(2)}, u32[]{:S(2)}) collective-permute-start(bf16[512,128]{1,0:T(8,128)(2,1)S(1)} %place.1.src0), channel_id=1, source_target_pairs={{0,8},{4,12},{8,16},{12,20},{16,24},{20,28},{24,32},{28,36},{32,40... | collective-permute-start | bytes 393224 | tf_op jit(solution)/shard_map/ppermute | solution.py:302
  42.5 2.3 %collective-permute-start = (bf16[512,128]{1,0:T(8,128)(2,1)S(1)}, bf16[512,128]{1,0:T(8,128)(2,1)S(1)}, u32[]{:S(2)}, u32[]{:S(2)}) collective-permute-start(bf16[512,128]{1,0:T(8,128)(2,1)S(1)} %place.1.src0), channel_id=1, source_target_pairs={{0,4},{4,8},{8,12},{12,16},{16,20},{20,24},{24,28},{28,32},{32,36}... | collective-permute-start | bytes 393224 | tf_op jit(solution)/shard_map/ppermute | solution.py:302
  46.6 2.9 %collective-permute-done.2.src3 = bf16[512,128]{1,0:T(8,128)(2,1)S(1)} collective-permute-done((bf16[512,128]{1,0:T(8,128)(2,1)S(1)}, bf16[512,128]{1,0:T(8,128)(2,1)S(1)}, u32[]{:S(2)}, u32[]{:S(2)}) %collective-permute-start.2) | collective-permute-done | bytes 131104 | tf_op jit(solution)/shard_map/ppermute | solution.py:302
  49.5 3.1 %collective-permute-done.1.src2 = bf16[512,128]{1,0:T(8,128)(2,1)S(1)} collective-permute-done((bf16[512,128]{1,0:T(8,128)(2,1)S(1)}, bf16[512,128]{1,0:T(8,128)(2,1)S(1)}, u32[]{:S(2)}, u32[]{:S(2)}) %collective-permute-start.1) | collective-permute-done | bytes 131104 | tf_op jit(solution)/shard_map/ppermute | solution.py:302
  53.7 10.9 %all_to_all.26.parts_ref = bf16[4,512,128]{2,1,0:T(8,128)(2,1)S(1)} all-to-all(bf16[4,512,128]{2,1,0:T(8,128)(2,1)S(1)} %gather_tiles.1), channel_id=1, replica_groups=mesh['blk'=128,'rep'=4] {'rep'}, dimensions={0} | all-to-all | bytes 1048576 | tf_op jit(solution)/shard_map/all_to_all | solution.py:306
  65.7 2.8 %collective-permute-start.5 = (bf16[512,128]{1,0:T(8,128)(2,1)S(1)}, bf16[512,128]{1,0:T(8,128)(2,1)S(1)}, u32[]{:S(2)}, u32[]{:S(2)}) collective-permute-start(bf16[512,128]{1,0:T(8,128)(2,1)S(1)} %get-tuple-element.24.block0), channel_id=1, source_target_pairs={{0,3},{1,0},{2,1},{3,2},{4,7},{5,4},{6,5},{7,6},{8,11},{9,8},{10,9... | collective-permute-start | bytes 393224 | tf_op jit(solution)/shard_map/ppermute | solution.py:302
  68.5 3.1 %collective-permute-start.4 = (bf16[512,128]{1,0:T(8,128)(2,1)S(1)}, bf16[512,128]{1,0:T(8,128)(2,1)S(1)}, u32[]{:S(2)}, u32[]{:S(2)}) collective-permute-start(bf16[512,128]{1,0:T(8,128)(2,1)S(1)} %get-tuple-element.24.block0), channel_id=1, source_target_pairs={{0,2},{1,3},{2,0},{3,1},{4,6},{5,7},{6,4},{7,5},{8,10},{9,11},{10,... | collective-permute-start | bytes 393224 | tf_op jit(solution)/shard_map/ppermute | solution.py:302
  71.6 1.9 %collective-permute-start.3 = (bf16[512,128]{1,0:T(8,128)(2,1)S(1)}, bf16[512,128]{1,0:T(8,128)(2,1)S(1)}, u32[]{:S(2)}, u32[]{:S(2)}) collective-permute-start(bf16[512,128]{1,0:T(8,128)(2,1)S(1)} %get-tuple-element.24.block0), channel_id=1, source_target_pairs={{0,1},{1,2},{2,3},{3,0},{4,5},{5,6},{6,7},{7,4},{8,9},{9,10},{10,1... | collective-permute-start | bytes 393224 | tf_op jit(solution)/shard_map/ppermute | solution.py:302
  74.7 9.2 %all-to-all-start.3 = ((bf16[128,4,128]{2,1,0:T(4,128)(2,1)}), bf16[128,4,128]{2,1,0:T(4,128)(2,1)S(1)}, u32[]{:S(2)}, u32[]{:S(2)}) async-start(bf16[128,4,128]{2,1,0:T(4,128)(2,1)} %bitcast.10), calls=%async_computation.3 | async-start | bytes 262144 | tf_op jit(solution)/shard_map/all_to_all | solution.py:306
  83.9 1.8 %spread_tiles.1 = (f32[512,128]{1,0:T(8,128)S(1)}, bf16[512,128]{1,0:T(8,128)(2,1)S(1)}, bf16[512,128]{1,0:T(8,128)(2,1)}, bf16[512,128]{1,0:T(8,128)(2,1)}) custom-call(s32[10,4]{1,0:T(8,128)S(1)} %get-tuple-element.19.table_ref, bf16[16,128,128]{2,1,0:T(8,128)(2,1)S(1)} %turn.1.refs_0_.tiles_ref, bf16[512,128]{1,0:T(8,128)(2,1)S(1)} %get-tuple-element.24.block0, ...), custom_call_target="tpu_custom_call" | custom-call | flops 100000000 | bytes 1000000 | tf_op jit(solution)/shard_map/spread_tiles/pallas_call | solution.py:313
  86.4 2.9 %collective-permute-start.6 = (bf16[512,128]{1,0:T(8,128)(2,1)S(1)}, bf16[512,128]{1,0:T(8,128)(2,1)S(1)}, u32[]{:S(2)}, u32[]{:S(2)}) collective-permute-start(bf16[512,128]{1,0:T(8,128)(2,1)S(1)} %get-tuple-element.26), channel_id=1, source_target_pairs={{0,508},{4,0},{8,4},{12,8},{16,12},{20,16},{24,20},{28,24},{32,28}... | collective-permute-start | bytes 393224 | tf_op jit(solution)/shard_map/ppermute | solution.py:302
  89.3 6.8 %collective-permute-start.7 = (bf16[512,128]{1,0:T(8,128)(2,1)}, bf16[512,128]{1,0:T(8,128)(2,1)S(1)}, u32[]{:S(2)}, u32[]{:S(2)}) collective-permute-start(bf16[512,128]{1,0:T(8,128)(2,1)} %get-tuple-element.27), channel_id=1, source_target_pairs={{0,504},{4,508},{8,0},{12,4},{16,8},{20,12},{24,16},{28,20},{32,24... | collective-permute-start | bytes 393224 | tf_op jit(solution)/shard_map/ppermute | solution.py:302
  96.1 4.5 %collective-permute-start.8 = (bf16[512,128]{1,0:T(8,128)(2,1)}, bf16[512,128]{1,0:T(8,128)(2,1)S(1)}, u32[]{:S(2)}, u32[]{:S(2)}) collective-permute-start(bf16[512,128]{1,0:T(8,128)(2,1)} %get-tuple-element.28), channel_id=1, source_target_pairs={{0,500},{4,504},{8,508},{12,0},{16,4},{20,8},{24,12},{28,16},{32,2... | collective-permute-start | bytes 393224 | tf_op jit(solution)/shard_map/ppermute | solution.py:302
  101.3 6.5 %all-to-all-start.4 = ((bf16[128,4,128]{2,1,0:T(4,128)(2,1)}), bf16[128,4,128]{2,1,0:T(4,128)(2,1)S(1)}, u32[]{:S(2)}, u32[]{:S(2)}) async-start(bf16[128,4,128]{2,1,0:T(4,128)(2,1)} %bitcast.12), calls=%async_computation.4 | async-start | bytes 262144 | tf_op jit(solution)/shard_map/all_to_all | solution.py:306
  109.1 11.5 %all-to-all-done.4 = bf16[128,4,128]{2,1,0:T(4,128)(2,1)S(1)} async-done(((bf16[128,4,128]{2,1,0:T(4,128)(2,1)}), bf16[128,4,128]{2,1,0:T(4,128)(2,1)S(1)}, u32[]{:S(2)}, u32[]{:S(2)}) %all-to-all-start.4) | async-done | bytes 131104 | tf_op jit(solution)/shard_map/all_to_all | solution.py:306
  120.6 5.7 %all-to-all-start.2 = ((bf16[128,8,128]{2,1,0:T(8,128)(2,1)}), bf16[128,8,128]{2,1,0:T(8,128)(2,1)S(1)}, u32[]{:S(2)}, u32[]{:S(2)}) async-start(bf16[128,8,128]{2,1,0:T(8,128)(2,1)} %bitcast.8), calls=%async_computation.2 | async-start | bytes 524288 | tf_op jit(solution)/shard_map/all_to_all | solution.py:306
  126.7 4.9 %collective-permute-start.11 = (bf16[144,256]{1,0:T(8,128)(2,1)S(1)}, bf16[144,256]{1,0:T(8,128)(2,1)S(1)}, u32[]{:S(2)}, u32[]{:S(2)}) collective-permute-start(bf16[144,256]{1,0:T(8,128)(2,1)S(1)} %whole.1.w0), channel_id=1, source_target_pairs={{0,3},{1,0},{2,1},{3,2},{4,7},{5,4},{6,5},{7,6},{8,11},{9,8},{10,9... | collective-permute-start | bytes 221192 | tf_op jit(solution)/shard_map/ppermute | solution.py:302
  131.5 2.5 %collective-permute-start.10 = (bf16[144,256]{1,0:T(8,128)(2,1)S(1)}, bf16[144,256]{1,0:T(8,128)(2,1)S(1)}, u32[]{:S(2)}, u32[]{:S(2)}) collective-permute-start(bf16[144,256]{1,0:T(8,128)(2,1)S(1)} %whole.1.w0), channel_id=1, source_target_pairs={{0,2},{1,3},{2,0},{3,1},{4,6},{5,7},{6,4},{7,5},{8,10},{9,11},{10,... | collective-permute-start | bytes 221192 | tf_op jit(solution)/shard_map/ppermute | solution.py:302
  134.0 2.5 %collective-permute-start.9 = (bf16[144,256]{1,0:T(8,128)(2,1)S(1)}, bf16[144,256]{1,0:T(8,128)(2,1)S(1)}, u32[]{:S(2)}, u32[]{:S(2)}) collective-permute-start(bf16[144,256]{1,0:T(8,128)(2,1)S(1)} %whole.1.w0), channel_id=1, source_target_pairs={{0,1},{1,2},{2,3},{3,0},{4,5},{5,6},{6,7},{7,4},{8,9},{9,10},{10,1... | collective-permute-start | bytes 221192 | tf_op jit(solution)/shard_map/ppermute | solution.py:302
  136.5 1.9 %collective-permute-done.10.w2 = bf16[144,256]{1,0:T(8,128)(2,1)S(1)} collective-permute-done((bf16[144,256]{1,0:T(8,128)(2,1)S(1)}, bf16[144,256]{1,0:T(8,128)(2,1)S(1)}, u32[]{:S(2)}, u32[]{:S(2)}) %collective-permute-start.10) | collective-permute-done | bytes 73760 | tf_op jit(solution)/shard_map/ppermute | solution.py:302
  138.4 2.7 %collective-permute-done.9.w1 = bf16[144,256]{1,0:T(8,128)(2,1)S(1)} collective-permute-done((bf16[144,256]{1,0:T(8,128)(2,1)S(1)}, bf16[144,256]{1,0:T(8,128)(2,1)S(1)}, u32[]{:S(2)}, u32[]{:S(2)}) %collective-permute-start.9) | collective-permute-done | bytes 73760 | tf_op jit(solution)/shard_map/ppermute | solution.py:302
  (35 shorter events, 10.5 us)
Async XLA Ops:
  36.3 8.5 %copy-start.3 = (s32[128,8]{0,1:T(8,128)S(1)}, s32[128,8]{0,1:T(8,128)}, u32[]{:S(2)}) copy-start(s32[128,8]{0,1:T(8,128)} %param.12) | copy-start | bytes 12292
  36.3 8.5 %copy-start.4 = (s32[128]{0:T(128)S(1)}, s32[128]{0:T(128)}, u32[]{:S(2)}) copy-start(s32[128]{0:T(128)} %param.13) | copy-start | bytes 1540
  37.2 8.7 %copy-start = (bf16[4,4,128,128]{3,2,1,0:T(8,128)(2,1)S(1)}, bf16[4,4,128,128]{3,2,1,0:T(8,128)(2,1)}, u32[]{:S(2)}) copy-start(bf16[4,4,128,128]{3,2,1,0:T(8,128)(2,1)} %param.14) | copy-start | bytes 1572868
  37.2 12.3 %collective-permute-start.2 = (bf16[512,128]{1,0:T(8,128)(2,1)S(1)}, bf16[512,128]{1,0:T(8,128)(2,1)S(1)}, u32[]{:S(2)}, u32[]{:S(2)}) collective-permute-start(bf16[512,128]{1,0:T(8,128)(2,1)S(1)} %place.1.src0), channel_id=1, source_target_pairs={{0,12},{4,16},{8,20},{12,24},{16,28},{20,32},{24,36},{28,40},{32,4... | collective-permute-start | bytes 393224 | tf_op jit(solution)/shard_map/ppermute | solution.py:302
  40.4 12.2 %collective-permute-start.1 = (bf16[512,128]{1,0:T(8,128)(2,1)S(1)}, bf16[512,128]{1,0:T(8,128)(2,1)S(1)}, u32[]{:S(2)}, u32[]{:S(2)}) collective-permute-start(bf16[512,128]{1,0:T(8,128)(2,1)S(1)} %place.1.src0), channel_id=1, source_target_pairs={{0,8},{4,12},{8,16},{12,20},{16,24},{20,28},{24,32},{28,36},{32,40... | collective-permute-start | bytes 393224 | tf_op jit(solution)/shard_map/ppermute | solution.py:302
  42.5 10.1 %collective-permute-start = (bf16[512,128]{1,0:T(8,128)(2,1)S(1)}, bf16[512,128]{1,0:T(8,128)(2,1)S(1)}, u32[]{:S(2)}, u32[]{:S(2)}) collective-permute-start(bf16[512,128]{1,0:T(8,128)(2,1)S(1)} %place.1.src0), channel_id=1, source_target_pairs={{0,4},{4,8},{8,12},{12,16},{16,20},{20,24},{24,28},{28,32},{32,36}... | collective-permute-start | bytes 393224 | tf_op jit(solution)/shard_map/ppermute | solution.py:302
  53.7 10.9 %copy-start.1 = (bf16[512,256]{1,0:T(8,128)(2,1)S(1)}, bf16[512,256]{1,0:T(8,128)(2,1)}, u32[]{:S(2)}) copy-start(bf16[512,256]{1,0:T(8,128)(2,1)} %out_grad_ref.1) | copy-start | bytes 786436
  53.7 10.9 %copy-start.2 = (bf16[128,256]{1,0:T(8,128)(2,1)S(1)}, bf16[128,256]{1,0:T(8,128)(2,1)}, u32[]{:S(2)}) copy-start(bf16[128,256]{1,0:T(8,128)(2,1)} %weight_ref.1) | copy-start | bytes 196612
  65.7 7.8 %collective-permute-start.5 = (bf16[512,128]{1,0:T(8,128)(2,1)S(1)}, bf16[512,128]{1,0:T(8,128)(2,1)S(1)}, u32[]{:S(2)}, u32[]{:S(2)}) collective-permute-start(bf16[512,128]{1,0:T(8,128)(2,1)S(1)} %get-tuple-element.24.block0), channel_id=1, source_target_pairs={{0,3},{1,0},{2,1},{3,2},{4,7},{5,4},{6,5},{7,6},{8,11},{9,8},{10,9... | collective-permute-start | bytes 393224 | tf_op jit(solution)/shard_map/ppermute | solution.py:302
  68.5 15.4 %collective-permute-start.4 = (bf16[512,128]{1,0:T(8,128)(2,1)S(1)}, bf16[512,128]{1,0:T(8,128)(2,1)S(1)}, u32[]{:S(2)}, u32[]{:S(2)}) collective-permute-start(bf16[512,128]{1,0:T(8,128)(2,1)S(1)} %get-tuple-element.24.block0), channel_id=1, source_target_pairs={{0,2},{1,3},{2,0},{3,1},{4,6},{5,7},{6,4},{7,5},{8,10},{9,11},{10,... | collective-permute-start | bytes 393224 | tf_op jit(solution)/shard_map/ppermute | solution.py:302
  71.6 12.3 %collective-permute-start.3 = (bf16[512,128]{1,0:T(8,128)(2,1)S(1)}, bf16[512,128]{1,0:T(8,128)(2,1)S(1)}, u32[]{:S(2)}, u32[]{:S(2)}) collective-permute-start(bf16[512,128]{1,0:T(8,128)(2,1)S(1)} %get-tuple-element.24.block0), channel_id=1, source_target_pairs={{0,1},{1,2},{2,3},{3,0},{4,5},{5,6},{6,7},{7,4},{8,9},{9,10},{10,1... | collective-permute-start | bytes 393224 | tf_op jit(solution)/shard_map/ppermute | solution.py:302
  74.7 25.9 %all-to-all-start.3 = ((bf16[128,4,128]{2,1,0:T(4,128)(2,1)}), bf16[128,4,128]{2,1,0:T(4,128)(2,1)S(1)}, u32[]{:S(2)}, u32[]{:S(2)}) async-start(bf16[128,4,128]{2,1,0:T(4,128)(2,1)} %bitcast.10), calls=%async_computation.3 | async-start | bytes 262144 | tf_op jit(solution)/shard_map/all_to_all | solution.py:306
  85.7 0.7 copy-start.5
  86.4 14.2 %collective-permute-start.6 = (bf16[512,128]{1,0:T(8,128)(2,1)S(1)}, bf16[512,128]{1,0:T(8,128)(2,1)S(1)}, u32[]{:S(2)}, u32[]{:S(2)}) collective-permute-start(bf16[512,128]{1,0:T(8,128)(2,1)S(1)} %get-tuple-element.26), channel_id=1, source_target_pairs={{0,508},{4,0},{8,4},{12,8},{16,12},{20,16},{24,20},{28,24},{32,28}... | collective-permute-start | bytes 393224 | tf_op jit(solution)/shard_map/ppermute | solution.py:302
  89.3 18.6 %collective-permute-start.7 = (bf16[512,128]{1,0:T(8,128)(2,1)}, bf16[512,128]{1,0:T(8,128)(2,1)S(1)}, u32[]{:S(2)}, u32[]{:S(2)}) collective-permute-start(bf16[512,128]{1,0:T(8,128)(2,1)} %get-tuple-element.27), channel_id=1, source_target_pairs={{0,504},{4,508},{8,0},{12,4},{16,8},{20,12},{24,16},{28,20},{32,24... | collective-permute-start | bytes 393224 | tf_op jit(solution)/shard_map/ppermute | solution.py:302
  96.1 11.8 %collective-permute-start.8 = (bf16[512,128]{1,0:T(8,128)(2,1)}, bf16[512,128]{1,0:T(8,128)(2,1)S(1)}, u32[]{:S(2)}, u32[]{:S(2)}) collective-permute-start(bf16[512,128]{1,0:T(8,128)(2,1)} %get-tuple-element.28), channel_id=1, source_target_pairs={{0,500},{4,504},{8,508},{12,0},{16,4},{20,8},{24,12},{28,16},{32,2... | collective-permute-start | bytes 393224 | tf_op jit(solution)/shard_map/ppermute | solution.py:302
  100.6 7.3 %copy-start.6 = (f32[512,128]{1,0:T(8,128)S(1)}, f32[512,128]{1,0:T(8,128)}, u32[]{:S(2)}) copy-start(f32[512,128]{1,0:T(8,128)} %copy-done.5) | copy-start | bytes 786436
  101.3 19.3 %all-to-all-start.4 = ((bf16[128,4,128]{2,1,0:T(4,128)(2,1)}), bf16[128,4,128]{2,1,0:T(4,128)(2,1)S(1)}, u32[]{:S(2)}, u32[]{:S(2)}) async-start(bf16[128,4,128]{2,1,0:T(4,128)(2,1)} %bitcast.12), calls=%async_computation.4 | async-start | bytes 262144 | tf_op jit(solution)/shard_map/all_to_all | solution.py:306
  120.6 21.1 %all-to-all-start.2 = ((bf16[128,8,128]{2,1,0:T(8,128)(2,1)}), bf16[128,8,128]{2,1,0:T(8,128)(2,1)S(1)}, u32[]{:S(2)}, u32[]{:S(2)}) async-start(bf16[128,8,128]{2,1,0:T(8,128)(2,1)} %bitcast.8), calls=%async_computation.2 | async-start | bytes 524288 | tf_op jit(solution)/shard_map/all_to_all | solution.py:306
  126.7 9.9 %collective-permute-start.11 = (bf16[144,256]{1,0:T(8,128)(2,1)S(1)}, bf16[144,256]{1,0:T(8,128)(2,1)S(1)}, u32[]{:S(2)}, u32[]{:S(2)}) collective-permute-start(bf16[144,256]{1,0:T(8,128)(2,1)S(1)} %whole.1.w0), channel_id=1, source_target_pairs={{0,3},{1,0},{2,1},{3,2},{4,7},{5,4},{6,5},{7,6},{8,11},{9,8},{10,9... | collective-permute-start | bytes 221192 | tf_op jit(solution)/shard_map/ppermute | solution.py:302
  131.5 6.9 %collective-permute-start.10 = (bf16[144,256]{1,0:T(8,128)(2,1)S(1)}, bf16[144,256]{1,0:T(8,128)(2,1)S(1)}, u32[]{:S(2)}, u32[]{:S(2)}) collective-permute-start(bf16[144,256]{1,0:T(8,128)(2,1)S(1)} %whole.1.w0), channel_id=1, source_target_pairs={{0,2},{1,3},{2,0},{3,1},{4,6},{5,7},{6,4},{7,5},{8,10},{9,11},{10,... | collective-permute-start | bytes 221192 | tf_op jit(solution)/shard_map/ppermute | solution.py:302
  134.0 7.1 %collective-permute-start.9 = (bf16[144,256]{1,0:T(8,128)(2,1)S(1)}, bf16[144,256]{1,0:T(8,128)(2,1)S(1)}, u32[]{:S(2)}, u32[]{:S(2)}) collective-permute-start(bf16[144,256]{1,0:T(8,128)(2,1)S(1)} %whole.1.w0), channel_id=1, source_target_pairs={{0,1},{1,2},{2,3},{3,0},{4,5},{5,6},{6,7},{7,4},{8,9},{9,10},{10,1... | collective-permute-start | bytes 221192 | tf_op jit(solution)/shard_map/ppermute | solution.py:302

commit v2 on v1

--- a/solution.py
+++ b/solution.py
@@ -8,6 +8,7 @@
 BF16 = jnp.bfloat16
 F32 = jnp.float32
 TILE = 128
+LONG = 10**11
 UNUSED = 1024.0
 NN = (((1,), (0,)), ((), ()))
 NT = (((1,), (1,)), ((), ()))
@@ -32,23 +33,27 @@
         out_shape=outs,
         in_specs=specs,
         scratch_shapes=list(scratch),
-        compiler_params=pltpu.CompilerParams(vmem_limit_bytes=40 * 1024 * 1024),
+        compiler_params=pltpu.CompilerParams(vmem_limit_bytes=16 * 1024 * 1024),
         cost_estimate=pl.CostEstimate(flops=flops, bytes_accessed=10**6, transcendentals=0),
         name=name,
     )
 
 
-def call(kernel, outs, name, flops=10**8):
+def call(kernel, outs, name, scratch=(), flops=10**8):
     def run(*arrays, after=()):
         specs = [pl.BlockSpec(memory_space=pltpu.VMEM)] * len(arrays)
         specs += [pl.BlockSpec(memory_space=pl.ANY)] * len(after)
-        return kernel_call(kernel, outs, specs, name, flops=flops)(*arrays, *after)
+        return kernel_call(kernel, outs, specs, name, scratch, flops)(*arrays, *after)
 
     return run
 
 
 def shape(dims, kind):
     return jax.ShapeDtypeStruct(dims, kind)
+
+
+def quotient(value, divisor):
+    return jnp.floor((value.astype(F32) + 0.5) * (1.0 / divisor)).astype(jnp.int32)
 
 
 def as_column(row):
@@ -64,16 +69,17 @@
     high = (key >> 5).astype(F32).astype(BF16)
     low = (key & 31).astype(F32).astype(BF16)
     total = owners * slots
-    expand = one_hot(iota((total, owners), 0) // slots == iota((total, owners), 1))
-    mine = iota((total, slots), 0) % slots == iota((total, slots), 1)
+    expand = one_hot(quotient(iota((total, owners), 0), slots) == iota((total, owners), 1))
+    row = iota((total, slots), 0)
+    mine = row - quotient(row, slots) * slots == iota((total, slots), 1)
     high = jnp.where(mine, dot(expand, high) * 32.0, 0.0).astype(BF16)
     low = jnp.where(mine, dot(expand, low), 0.0).astype(BF16)
     return high, low
 
 
 def start_kernel(*refs):
-    out_ref, scale_ref, bias_ref, table_ref = refs[8:12]
-    features_ref, rows_ref, counts_ref, degree_ref, *parts, sems = refs[12:]
+    out_ref, degree_ref, bias_ref, table_ref, key_ref = refs[8:13]
+    features_ref, rows_ref, counts_ref, *parts, sems = refs[13:]
     pairs = tuple(zip(refs[:8], (features_ref, rows_ref, counts_ref, degree_ref, *parts, bias_ref)))
     copies = [pltpu.make_async_copy(a, b, sems.at[k]) for k, (a, b) in enumerate(pairs)]
     for copy in copies:
@@ -91,13 +97,15 @@
     )
     sent = dot(pick, features_ref[...])
     out_ref[...] = jnp.where(key >= float(rows), UNUSED, sent).astype(BF16)
-    for t in range(rows // TILE):
-        scale_ref[t * TILE : (t + 1) * TILE] = as_column(degree_ref[t : t + 1])
+    ones = jnp.ones((8, slots), BF16)
+    key_ref[...] = dot(ones, high, NT) + dot(ones, low, NT)
     place = 0
     for part in parts:
         table_ref[place : place + part.shape[0]] = part[...]
         place += part.shape[0]
-    table_ref[place : place + 1] = jnp.full((1, table_ref.shape[1]), lax.axis_index("rep"))
+    odd = lax.rem(lax.axis_index("blk"), 2)
+    lane = iota((1, table_ref.shape[1]), 1)
+    table_ref[place : place + 1] = jnp.where(lane == 0, odd, lax.axis_index("rep"))
 
 
 def start_call(features, send_rows, counts_row, degree, tables, bias_row):
@@ -109,12 +117,13 @@
         start_kernel,
         out_shape=(
             shape((total, width), BF16),
-            shape((rows, TILE), F32),
+            shape(degree.shape, F32),
             shape(bias_row.shape, F32),
             shape((1 + sum(a.shape[0] for a in tables), tables[0].shape[1]), jnp.int32),
+            shape((8, total), F32),
         ),
         in_specs=[pl.BlockSpec(memory_space=pltpu.HBM)] * 8,
-        scratch_shapes=[pltpu.VMEM(a.shape, a.dtype) for a in small]
+        scratch_shapes=[pltpu.VMEM(a.shape, a.dtype) for a in (features, send_rows, counts_row, *tables)]
         + [pltpu.SemaphoreType.DMA((8,))],
         compiler_params=pltpu.CompilerParams(vmem_limit_bytes=8 * 1024 * 1024),
         cost_estimate=pl.CostEstimate(flops=10**8, bytes_accessed=10**6, transcendentals=0),
@@ -122,18 +131,8 @@
     )(*arrays)
 
 
-def arrive_kernel(rows_ref, counts_ref, out_ref):
-    rows = out_ref.shape[0]
-    slots = rows_ref.shape[0]
-    high, low = slot_parts(rows_ref[...], counts_ref[...], rows)
-    ones = jnp.ones((8, slots), BF16)
-    key = dot(ones, high, NT) + dot(ones, low, NT)
-    for start in range(0, key.shape[1], TILE):
-        span = slice(start, start + TILE)
-        out_ref[:, span] = one_hot(iota((rows, TILE), 0).astype(F32) == key[0:1, span])
-
-
-def transpose_kernel(tiles_ref, out_ref):
+def transpose_kernel(tiles_ref, *refs):
+    out_ref = refs[-1]
     for t in range(tiles_ref.shape[0]):
         out_ref[t] = jnp.transpose(tiles_ref[t].astype(F32)).astype(BF16)
 
@@ -142,7 +141,15 @@
     return jnp.where(ref[...].astype(F32) < 512.0, 1.0, 0.0).astype(BF16)
 
 
-def place_kernel(incoming_ref, scale_ref, out_ref):
+def scaled_rows(degree_ref, values):
+    count = values.shape[0] // TILE
+    parts = [
+        as_column(degree_ref[t : t + 1]) * values[t * TILE : (t + 1) * TILE] for t in range(count)
+    ]
+    return jnp.concatenate(parts, axis=0)
+
+
+def place_kernel(incoming_ref, degree_ref, out_ref):
     rows = out_ref.shape[0]
     used = used_slots(incoming_ref)
     before = one_hot(iota((TILE, TILE), 0) < iota((TILE, TILE), 1))
@@ -157,7 +164,7 @@
         offset = offset + dot(flags, ones)
         parts.append(one_hot(iota((rows, TILE), 0).astype(F32) == rank[0:1]))
     owned = dot(jnp.concatenate(parts, axis=1), incoming_ref[...])
-    out_ref[...] = (scale_ref[...] * owned).astype(BF16)
+    out_ref[...] = scaled_rows(degree_ref, owned).astype(BF16)
 
 
 def unplace_kernel(incoming_ref, out_ref):
@@ -177,14 +184,13 @@
             )
 
 
-def gather_kernel(
-    table_ref, tiles_ref, src0, src1, src2, src3, *refs
-):
+def gather_kernel(table_ref, tiles_ref, src0, two, apart, near, *refs):
     out_ref, acc_ref = refs[-2:]
     acc_ref[...] = jnp.zeros_like(acc_ref)
     most = table_ref.shape[1]
     steps = tiles_ref.shape[0] // most
-    for step, source in enumerate((src0, src1, src2, src3)):
+    odd = table_ref[2 * steps + 1, 0]
+    for step, source in ((0, src0), (2, two), (3 - 2 * odd, apart), (1 + 2 * odd, near)):
         for k in range(most):
             col = pl.multiple_of(table_ref[steps + step, k] * TILE, TILE)
             row = pl.multiple_of(table_ref[step, k] * TILE, TILE)
@@ -197,7 +203,7 @@
 
 
 def dense_kernel(
-    parts_ref, scale_ref, weight_ref, bias_ref, out_grad_ref, hidden_ref, agg_ref, grad_pre_ref, out_ref
+    parts_ref, degree_ref, weight_ref, bias_ref, out_grad_ref, hidden_ref, agg_ref, grad_pre_ref, out_ref
 ):
     quarters, rows, width = parts_ref.shape
     summed = parts_ref[0].astype(F32)
@@ -205,7 +211,7 @@
         summed = summed + parts_ref[q].astype(F32)
     for t in range(rows // TILE):
         part = slice(t * TILE, (t + 1) * TILE)
-        scale = scale_ref[part]
+        scale = as_column(degree_ref[t : t + 1])
         agg = (scale * summed[part]).astype(BF16)
         agg_ref[part] = agg
         pre = dot(agg, weight_ref[...]) + bias_ref[...]
@@ -237,35 +243,22 @@
 def row_kernel(parts_ref, *refs):
     out_ref = refs[-1]
     count, width = parts_ref.shape
-    groups = (count // 8, 8, width)
-    pairs = jnp.sum(parts_ref[...].astype(F32).reshape(groups), axis=0)
-    term = pairs[:4] + pairs[4:]
-    both = jnp.concatenate([term, term], axis=0)
-    out_ref[...] = jnp.broadcast_to(both[None], groups).reshape(count, width).astype(BF16)
-
-
-def whole_kernel(rows_ref, out_ref):
-    count = rows_ref.shape[0]
-    width = count // 4
-    lines = (width, count)
-    for k in range(2):
-        half = slice(k * TILE, (k + 1) * TILE)
-        here = iota(lines, 1) == 4 * iota(lines, 0) + k
-        out_ref[:width, half] = dot(one_hot(here), rows_ref[...]).astype(BF16)
-        here = iota((16, count), 1) % 4 == k + 2
-        out_ref[width:, half] = dot(one_hot(here), rows_ref[...]).astype(BF16)
+    pairs = jnp.sum(parts_ref[...].astype(F32).reshape(count // 8, 8, width), axis=0)
+    term = jnp.concatenate([pairs[:4] + pairs[4:], jnp.zeros((4, width), F32)], axis=0)
+    for copy in range(out_ref.shape[0]):
+        out_ref[copy] = term
 
 
 def spread_kernel(
     table_ref, tiles_ref, block0, block1, block2, block3, *refs
 ):
-    own_ref, out1, out2, out3, acc_ref, block_ref = refs[-6:]
-    mine = table_ref[table_ref.shape[0] - 1, 0]
-    for away, block in enumerate((block0, block1, block2, block3)):
-        block_ref[lax.rem(mine + 4 - away, 4)] = block[...]
+    own_ref, two_ref, near_ref, apart_ref, done_ref, acc_ref, block_ref = refs[-7:]
     acc_ref[...] = jnp.zeros_like(acc_ref)
     most = table_ref.shape[1]
     steps = tiles_ref.shape[0] // most
+    mine = table_ref[2 * steps + 1, 1]
+    for away, block in enumerate((block0, block1, block2, block3)):
+        block_ref[lax.rem(mine + 4 - away, 4)] = block[...]
     col_tiles = own_ref.shape[0] // TILE
     for step in range(steps - 1, -1, -1):
         for k in range(most):
@@ -275,31 +268,94 @@
             live = (k < table_ref[2 * steps, step]).astype(F32)
             prod = dot(tiles_ref[step * most + k], block_ref[quarter, pl.ds(row, TILE), :])
             acc_ref[step, pl.ds(col, TILE), :] += prod * live
+    odd = table_ref[2 * steps + 1, 0]
     own_ref[...] = acc_ref[0]
-    for step, out in ((1, out1), (2, out2), (3, out3)):
-        out[...] = acc_ref[step].astype(BF16)
-
-
-def back_kernel(own_ref, in1, in2, in3, scale_ref, unplace_ref, *refs):
-    out_ref = refs[-1]
-    total = own_ref[...] + in1[...].astype(F32) + in2[...].astype(F32) + in3[...].astype(F32)
-    grads = (scale_ref[...] * total).astype(BF16)
-    out_ref[...] = dot(unplace_ref[...], grads).astype(BF16)
-
-
-def last_kernel(arrive_ref, returned_ref, w0, w1, w2, w3, out_ref, weight_ref, bias_ref):
-    out_ref[...] = dot(arrive_ref[...], returned_ref[...]).astype(BF16)
-    total = (w0[...].astype(F32) + w1[...].astype(F32)) + (
-        w2[...].astype(F32) + w3[...].astype(F32)
-    )
-    width = weight_ref.shape[0]
-    weight_ref[...] = total[:width]
-    bias_ref[...] = total[width : width + 1]
-
-
-def shifted(value, steps, axis="blk"):
-    count = lax.axis_size(axis)
-    return lax.ppermute(value, axis, [(s, (s + steps) % count) for s in range(count)])
+    two_ref[...] = acc_ref[2]
+    near_ref[...] = acc_ref[1 + 2 * odd].astype(BF16)
+    apart_ref[...] = acc_ref[3 - 2 * odd].astype(BF16)
+    done_ref[...] = jnp.zeros_like(done_ref)
+
+
+def add_kernel(a_ref, b_ref, out_ref):
+    out_ref[...] = (a_ref[...] + b_ref[...].astype(F32)).astype(BF16)
+
+
+def slot_of(lines, dim):
+    index = iota(lines, dim)
+    owner = quotient(index, 12)
+    return owner, index - 12 * owner
+
+
+def back_kernel(own_ref, in1, in2, degree_ref, unplace_ref, terms_ref, out_ref):
+    total = own_ref[...] + in1[...].astype(F32) + in2[...].astype(F32)
+    grads = scaled_rows(degree_ref, total).astype(BF16)
+    slots = dot(unplace_ref[...], grads).astype(BF16)
+    term = (terms_ref[0] + terms_ref[1]) + (terms_ref[2] + terms_ref[3])
+    term = jnp.concatenate([term, jnp.zeros((TILE - 8, term.shape[1]), F32)], axis=0).astype(BF16)
+    lines = (TILE // 8 * 12, TILE)
+    owner, slot = slot_of(lines, 0)
+    widen = one_hot((slot < 8) & (owner * 8 + slot == iota(lines, 1)))
+    ends = dot(one_hot(slot == 8 + iota(lines, 1)), term)
+    for t in range(slots.shape[0] // TILE):
+        group = dot(widen, slots[t * TILE : (t + 1) * TILE]) + ends
+        out_ref[t * lines[0] : (t + 1) * lines[0]] = group.astype(BF16)
+
+
+def last_kernel(key_ref, returned_ref, out_ref, weight_ref, bias_ref):
+    rows = out_ref.shape[0]
+    owners = TILE // 8
+    lines = (TILE + 3 * owners, 12 * owners)
+    owner, slot = slot_of(lines, 1)
+    row = iota(lines, 0)
+    wanted = (slot < 8) & (owner * 8 + slot == row)
+    wanted |= (slot == 8) & (owner + TILE == row)
+    wanted |= (slot == 9) & (owner + TILE + owners == row)
+    wanted |= ((slot == 10) & (row == TILE + 2 * owners)) | ((slot == 11) & (row == TILE + 2 * owners + 1))
+    pick = one_hot(wanted)
+    total = jnp.zeros((rows, TILE), F32)
+    bias = jnp.zeros((owners, TILE), F32)
+    for t in range(returned_ref.shape[0] // lines[1]):
+        found = dot(pick, returned_ref[t * lines[1] : (t + 1) * lines[1]])
+        span = slice(t * TILE, (t + 1) * TILE)
+        here = one_hot(iota((rows, TILE), 0).astype(F32) == key_ref[0:1, span])
+        total = total + dot(here, found[:TILE].astype(BF16))
+        for k in range(2):
+            part = found[TILE + k * owners : TILE + (k + 1) * owners]
+            weight_ref[t * owners : (t + 1) * owners, k * TILE : (k + 1) * TILE] = part
+        bias = bias + found[TILE + 2 * owners :]
+    out_ref[...] = total.astype(BF16)
+    bias_ref[:, :TILE] = bias[0:1]
+    bias_ref[:, TILE:] = bias[1:2]
+
+
+def moved(value, target):
+    count = lax.axis_size("blk")
+    return lax.ppermute(value, "blk", [(s, target(s) % count) for s in range(count)])
+
+
+def around(value, steps):
+    count = lax.axis_size("rep")
+    return lax.ppermute(value, "rep", [(s, (s + steps) % count) for s in range(count)])
+
+
+def two_on(blk):
+    return blk + 2
+
+
+def two_back(blk):
+    return blk - 2
+
+
+def apart_on(blk):
+    return blk + 1 + 2 * (blk % 2)
+
+
+def apart_back(blk):
+    return blk - 3 + 2 * (blk % 2)
+
+
+def other_core(blk):
+    return blk + 1 - 2 * (blk % 2)
 
 
 def exchange(value, axis):
@@ -339,16 +395,17 @@
     tiles = tile_values.reshape(steps * most, TILE, TILE)
     tables = (tile_rows, tile_cols, tile_counts.reshape(1, steps))
 
-    outgoing, scale, bias_row, table = start_call(
+    outgoing, scale, bias_row, table, key = start_call(
         features, slot_rows, counts_row, degree, tables, bias.reshape(1, hidden_width)
     )
     incoming = exchange(outgoing.reshape(blocks, slots, width), "blk").reshape(total, width)
-    arrive = call(arrive_kernel, shape((rows, total), BF16), "arrive")(slot_rows, counts_row)
-    turned = call(transpose_kernel, shape(tiles.shape, BF16), "turn")(tiles)
-
     scaled = call(place_kernel, shape((rows, width), BF16), "place")(incoming, scale)
-    sources = [scaled] + [shifted(scaled, step) for step in range(1, steps)]
-    unplace = call(unplace_kernel, shape((total, rows), BF16), "unplace")(incoming)
+    two = moved(scaled, two_on)
+    sources = (scaled, two, moved(scaled, apart_on), moved(two, other_core))
+    unplace = call(unplace_kernel, shape((total, rows), BF16), "unplace", flops=10**8)(incoming)
+    turned = call(transpose_kernel, shape(tiles.shape, BF16), "turn", flops=LONG)(
+        tiles, after=(scaled,)
+    )
     partial = tile_call(
         gather_kernel,
         shape((quarters, rows, width), BF16),
@@ -356,7 +413,7 @@
         "gather_tiles",
         table,
         (tiles, *sources),
-        (turned, arrive, unplace),
+        (turned, unplace),
     )
     parts = exchange(partial, "rep")
     hidden, agg, grad_pre, grad_agg = call(
@@ -369,32 +426,36 @@
         ),
         "dense",
     )(parts, scale, weight, bias_row, out_grad)
-    block = [grad_agg] + [shifted(grad_agg, away, "rep") for away in range(1, quarters)]
-
-    lines = shape((4 * width, TILE), BF16)
-    terms = call(terms_kernel, lines, "terms")(agg, grad_pre, after=(block[3],))
-    terms = exchange(terms.reshape(blocks, 4, TILE), "blk").reshape(lines.shape)
-
-    own, *others = tile_call(
+    block = [grad_agg] + [around(grad_agg, away) for away in range(1, quarters)]
+    terms = call(terms_kernel, shape((4 * width, TILE), BF16), "terms")(
+        agg, grad_pre, after=(block[3],)
+    )
+    terms = exchange(terms.reshape(blocks, 4, TILE), "blk").reshape(4 * width, TILE)
+
+    own, two, near, apart, spread = tile_call(
         spread_kernel,
-        (shape((rows, width), F32),) + (shape((rows, width), BF16),) * (steps - 1),
+        (shape((rows, width), F32),) * 2
+        + (shape((rows, width), BF16),) * 2
+        + (shape((8, TILE), F32),),
         [pltpu.VMEM((steps, rows, width), F32), pltpu.VMEM((quarters, rows, width), BF16)],
         "spread_tiles",
         table,
         (turned, *block),
     )
-    others = [shifted(value, -step) for step, value in enumerate(others, 1)]
-    terms = call(row_kernel, lines, "row")(terms, after=(others[0],))
-    terms = exchange(terms.reshape(blocks, 4, TILE), "blk").reshape(lines.shape)
-    back = call(back_kernel, shape((total, width), BF16), "back", flops=4 * 10**10)(own, *others, scale, unplace)
-    whole = call(whole_kernel, shape((width + 16, hidden_width), BF16), "whole")(terms)
-    wholes = [whole] + [shifted(whole, away, "rep") for away in range(1, quarters)]
-    returned = exchange(back.reshape(blocks, slots, width), "blk").reshape(total, width)
+    near = moved(near, other_core)
+    apart = moved(apart, apart_back)
+    two = moved(call(add_kernel, shape((rows, width), BF16), "add")(two, near), two_back)
+    terms = call(row_kernel, shape((quarters, 8, TILE), F32), "row")(terms, after=(spread,))
+    terms = exchange(terms, "rep")
+    back = call(back_kernel, shape((blocks * (slots + 4), width), BF16), "back", flops=4 * 10**10)(
+        own, apart, two, scale, unplace, terms
+    )
+    returned = exchange(back.reshape(blocks, 3, 4, width), "blk").reshape(back.shape)
     grad_features, grad_weight, grad_bias = call(
         last_kernel,
         (shape((rows, width), BF16), shape(weight.shape, F32), shape((1, hidden_width), F32)),
         "last",
-    )(arrive, returned, *wholes)
+    )(key, returned)
     return (hidden, grad_features, grad_weight, grad_bias.reshape(hidden_width))
 
 

time: 144 us -> 137 us (0.951)
  blocking collectives: 44.4 us -> 73.6 us
  starting transfers between devices: 60.9 us -> 40.9 us
  waiting for transfers between devices: 22.8 us -> 8.9 us
    all_to_all x2 -> x3, blocking collectives: 44.4 us -> 73.6 us  [exchange(): return lax.all_to_all(value, axis, split_axis=0, concat_axis=0, tiled=True)]
    ppermute x12 -> x9, starting transfers between devices: 39.4 us -> 28.1 us  [the longest x6 20.3 us: moved(): lax.ppermute(value, 'blk', [(s, target(s) % count) for s in range(count)])]
    all_to_all x3 -> x2, starting transfers between devices: 21.5 us -> 12.7 us  [exchange(): return lax.all_to_all(value, axis, split_axis=0, concat_axis=0, tiled=True)]
    all_to_all x3 -> x2, waiting for transfers between devices: 12.2 us -> 4.21 us  [exchange(): return lax.all_to_all(value, axis, split_axis=0, concat_axis=0, tiled=True)]
    ppermute x12 -> x9, waiting for transfers between devices: 10.6 us -> 4.69 us  [the longest x6 4.69 us: moved(): lax.ppermute(value, 'blk', [(s, target(s) % count) for s in range(count)])]
    pallas_call x10 -> x9, Pallas kernels: 8.07 us -> 7.07 us  [run(): kernel_call(kernel, outs, specs, name, scratch, flops)(*arrays, *after)]
  transfers between devices with their start and end apart: 15 -> 11, of which waited for: 6 -> 3; matrix products, arithmetic and copies ran while one was open for 0% -> 0% of each run, Pallas kernels for 5% -> 3%
where the time goes in v2:
time: 137 us; the launch traced here: 136 us
  blocking collectives  73.6 us (54%)
  starting transfers between devices  40.9 us (30%)
  Pallas kernels  11.7 us (9%)
  waiting for transfers between devices  8.9 us (6%)
    all_to_all x3, blocking collectives, exchange(): return lax.all_to_all(value, axis, split_axis=0, concat_axis=0, tiled=True)  73.6 us
    ppermute x6, starting transfers between devices, moved(): lax.ppermute(value, 'blk', [(s, target(s) % count) for s in range(count)])  20.3 us
    all_to_all x2, starting transfers between devices, exchange(): return lax.all_to_all(value, axis, split_axis=0, concat_axis=0, tiled=True)  12.7 us
    ppermute x3, starting transfers between devices, around(): lax.ppermute(value, 'rep', [(s, (s + steps) % count) for s in range(count)])  7.8 us
    pallas_call x9, Pallas kernels, run(): kernel_call(kernel, outs, specs, name, scratch, flops)(*arrays, *after)  7.07 us
    ppermute x6, waiting for transfers between devices, moved(): lax.ppermute(value, 'blk', [(s, target(s) % count) for s in range(count)])  4.69 us
    all_to_all x2, waiting for transfers between devices, exchange(): return lax.all_to_all(value, axis, split_axis=0, concat_axis=0, tiled=True)  4.21 us
  transfers between devices with their start and end apart: 11, of which 3 were waited for; matrix products, arithmetic and copies ran while one was open for 0% of the time, Pallas kernels for 3%

profile of v2, /device:TPU:1, one launch (start us, length us, event | category | flops | bytes accessed | tf_op | source)
XLA Modules:
  0.0 135.9 jit_solution(3225444280875027706)
XLA Ops:
  0.6 2.4 %start.1 = (bf16[1024,128]{1,0:T(8,128)(2,1)S(1)}, f32[4,128]{1,0:T(4,128)S(1)}, f32[1,256]{1,0:T(1,128)S(1)}, s32[10,4]{1,0:T(8,128)S(1)}, f32[8,1024]{1,0:T(8,128)S(1)}) custom-call(bf16[512,128]{1,0:T(8,128)(2,1)} %refs_0_.1, s32[8,128]{1,0:T(8,128)} %bitcast.21, s32[1,128]{1,0:T(1,128)} %bitcast.25, f32[4,128]{1,0:T(4,128)} %bitcast.22, s32[4,4]{1,0:T(4,128)} %refs_4_.1, ...), custom_call_target="tpu_custom_call" | custom-call | flops 100000000 | bytes 1000000 | tf_op jit(solution)/shard_map/start/pallas_call | solution.py:116
  3.1 33.6 %all_to_all.25 = bf16[128,8,128]{2,1,0:T(8,128)(2,1)S(1)} all-to-all(bf16[128,8,128]{2,1,0:T(8,128)(2,1)S(1)} %bitcast.19), channel_id=1, replica_groups=mesh['blk'=128,'rep'=4] {'blk'}, dimensions={0} | all-to-all | bytes 524288 | tf_op jit(solution)/shard_map/all_to_all | solution.py:362
  36.7 0.8 place.1.refs_0_.src0
  37.5 2.5 %collective-permute-start = (bf16[512,128]{1,0:T(8,128)(2,1)S(1)}, bf16[512,128]{1,0:T(8,128)(2,1)S(1)}, u32[]{:S(2)}, u32[]{:S(2)}) collective-permute-start(bf16[512,128]{1,0:T(8,128)(2,1)S(1)} %place.1.refs_0_.src0), channel_id=1, source_target_pairs={{0,8},{4,12},{8,16},{12,20},{16,24},{20,28},{24,32},{28,36},{32,40... | collective-permute-start | bytes 393224 | tf_op jit(solution)/shard_map/ppermute | solution.py:333
  40.0 3.0 %collective-permute-start.1 = (bf16[512,128]{1,0:T(8,128)(2,1)S(1)}, bf16[512,128]{1,0:T(8,128)(2,1)S(1)}, u32[]{:S(2)}, u32[]{:S(2)}) collective-permute-start(bf16[512,128]{1,0:T(8,128)(2,1)S(1)} %place.1.refs_0_.src0), channel_id=1, source_target_pairs={{0,4},{4,16},{8,12},{12,24},{16,20},{20,32},{24,28},{28,40},{32,36... | collective-permute-start | bytes 393224 | tf_op jit(solution)/shard_map/ppermute | solution.py:333
  43.0 4.5 %collective-permute-done.two = bf16[512,128]{1,0:T(8,128)(2,1)S(1)} collective-permute-done((bf16[512,128]{1,0:T(8,128)(2,1)S(1)}, bf16[512,128]{1,0:T(8,128)(2,1)S(1)}, u32[]{:S(2)}, u32[]{:S(2)}) %collective-permute-start) | collective-permute-done | bytes 131104 | tf_op jit(solution)/shard_map/ppermute | solution.py:333
  47.4 3.1 %collective-permute-start.2 = (bf16[512,128]{1,0:T(8,128)(2,1)S(1)}, bf16[512,128]{1,0:T(8,128)(2,1)S(1)}, u32[]{:S(2)}, u32[]{:S(2)}) collective-permute-start(bf16[512,128]{1,0:T(8,128)(2,1)S(1)} %collective-permute-done.two), channel_id=1, source_target_pairs={{0,4},{4,0},{8,12},{12,8},{16,20},{20,16},{24,28},{28,24},{32,36},... | collective-permute-start | bytes 393224 | tf_op jit(solution)/shard_map/ppermute | solution.py:333
  51.5 1.0 gather_tiles.1
  52.6 11.9 %all_to_all.26.parts_ref = bf16[4,512,128]{2,1,0:T(8,128)(2,1)S(1)} all-to-all(bf16[4,512,128]{2,1,0:T(8,128)(2,1)S(1)} %gather_tiles.1), channel_id=1, replica_groups=mesh['blk'=128,'rep'=4] {'rep'}, dimensions={0} | all-to-all | bytes 1048576 | tf_op jit(solution)/shard_map/all_to_all | solution.py:362
  64.4 1.1 dense.1
  65.6 2.8 %collective-permute-start.5 = (bf16[512,128]{1,0:T(8,128)(2,1)S(1)}, bf16[512,128]{1,0:T(8,128)(2,1)S(1)}, u32[]{:S(2)}, u32[]{:S(2)}) collective-permute-start(bf16[512,128]{1,0:T(8,128)(2,1)S(1)} %get-tuple-element.27.block0), channel_id=1, source_target_pairs={{0,3},{1,0},{2,1},{3,2},{4,7},{5,4},{6,5},{7,6},{8,11},{9,8},{10,9... | collective-permute-start | bytes 393224 | tf_op jit(solution)/shard_map/ppermute | solution.py:338
  68.3 3.1 %collective-permute-start.4 = (bf16[512,128]{1,0:T(8,128)(2,1)S(1)}, bf16[512,128]{1,0:T(8,128)(2,1)S(1)}, u32[]{:S(2)}, u32[]{:S(2)}) collective-permute-start(bf16[512,128]{1,0:T(8,128)(2,1)S(1)} %get-tuple-element.27.block0), channel_id=1, source_target_pairs={{0,2},{1,3},{2,0},{3,1},{4,6},{5,7},{6,4},{7,5},{8,10},{9,11},{10,... | collective-permute-start | bytes 393224 | tf_op jit(solution)/shard_map/ppermute | solution.py:338
  71.4 1.9 %collective-permute-start.3 = (bf16[512,128]{1,0:T(8,128)(2,1)S(1)}, bf16[512,128]{1,0:T(8,128)(2,1)S(1)}, u32[]{:S(2)}, u32[]{:S(2)}) collective-permute-start(bf16[512,128]{1,0:T(8,128)(2,1)S(1)} %get-tuple-element.27.block0), channel_id=1, source_target_pairs={{0,1},{1,2},{2,3},{3,0},{4,5},{5,6},{6,7},{7,4},{8,9},{9,10},{10,1... | collective-permute-start | bytes 393224 | tf_op jit(solution)/shard_map/ppermute | solution.py:338
  73.4 1.2 terms.1
  74.6 8.2 %all-to-all-start.2 = ((bf16[128,4,128]{2,1,0:T(4,128)(2,1)}), bf16[128,4,128]{2,1,0:T(4,128)(2,1)S(1)}, u32[]{:S(2)}, u32[]{:S(2)}) async-start(bf16[128,4,128]{2,1,0:T(4,128)(2,1)} %bitcast.8), calls=%async_computation.2 | async-start | bytes 262144 | tf_op jit(solution)/shard_map/all_to_all | solution.py:362
  82.9 1.1 spread_tiles.1
  84.0 2.9 %collective-permute-start.7 = (bf16[512,128]{1,0:T(8,128)(2,1)S(1)}, bf16[512,128]{1,0:T(8,128)(2,1)S(1)}, u32[]{:S(2)}, u32[]{:S(2)}) collective-permute-start(bf16[512,128]{1,0:T(8,128)(2,1)S(1)} %get-tuple-element.31), channel_id=1, source_target_pairs={{0,4},{4,0},{8,12},{12,8},{16,20},{20,16},{24,28},{28,24},{32,36},... | collective-permute-start | bytes 393224 | tf_op jit(solution)/shard_map/ppermute | solution.py:333
  86.9 1.9 %collective-permute-start.6 = (bf16[512,128]{1,0:T(8,128)(2,1)S(1)}, bf16[512,128]{1,0:T(8,128)(2,1)S(1)}, u32[]{:S(2)}, u32[]{:S(2)}) collective-permute-start(bf16[512,128]{1,0:T(8,128)(2,1)S(1)} %get-tuple-element.29), channel_id=1, source_target_pairs={{0,500},{4,0},{8,508},{12,8},{16,4},{20,16},{24,12},{28,24},{32,20... | collective-permute-start | bytes 393224 | tf_op jit(solution)/shard_map/ppermute | solution.py:333
  88.9 7.0 %collective-permute-start.8 = (bf16[512,128]{1,0:T(8,128)(2,1)S(1)}, bf16[512,128]{1,0:T(8,128)(2,1)S(1)}, u32[]{:S(2)}, u32[]{:S(2)}) collective-permute-start(bf16[512,128]{1,0:T(8,128)(2,1)S(1)} %add.1), channel_id=1, source_target_pairs={{0,504},{4,508},{8,0},{12,4},{16,8},{20,12},{24,16},{28,20},{32,24... | collective-permute-start | bytes 393224 | tf_op jit(solution)/shard_map/ppermute | solution.py:333
  96.5 4.5 %all-to-all-start.3 = ((f32[4,8,128]{2,1,0:T(8,128)}), f32[4,8,128]{2,1,0:T(8,128)S(1)}, u32[]{:S(2)}, u32[]{:S(2)}) async-start(f32[4,8,128]{2,1,0:T(8,128)} %row.1), calls=%async_computation.3 | async-start | bytes 32768 | tf_op jit(solution)/shard_map/all_to_all | solution.py:362
  101.1 4.2 %all-to-all-done.3.terms_ref = f32[4,8,128]{2,1,0:T(8,128)S(1)} async-done(((f32[4,8,128]{2,1,0:T(8,128)}), f32[4,8,128]{2,1,0:T(8,128)S(1)}, u32[]{:S(2)}, u32[]{:S(2)}) %all-to-all-start.3) | async-done | bytes 16416 | tf_op jit(solution)/shard_map/all_to_all | solution.py:362
  105.3 0.8 back.1
  106.1 28.1 %all_to_all.27 = bf16[128,3,4,128]{3,2,1,0:T(4,128)(2,1)S(1)} all-to-all(bf16[128,3,4,128]{3,2,1,0:T(4,128)(2,1)S(1)} %bitcast.18), channel_id=1, replica_groups=mesh['blk'=128,'rep'=4] {'blk'}, dimensions={0} | all-to-all | bytes 786432 | tf_op jit(solution)/shard_map/all_to_all | solution.py:362
  134.2 1.7 %last.1 = (bf16[512,128]{1,0:T(8,128)(2,1)}, f32[128,256]{1,0:T(8,128)}, f32[1,256]{1,0:T(1,128)}) custom-call(f32[8,1024]{1,0:T(8,128)S(1)} %get-tuple-element.26.key_ref, bf16[1536,128]{1,0:T(8,128)(2,1)S(1)} %bitcast.15), custom_call_target="tpu_custom_call" | custom-call | flops 100000000 | bytes 1000000 | tf_op jit(solution)/shard_map/last/pallas_call | solution.py:46
  (19 shorter events, 1.7 us)
Async XLA Ops:
  3.1 47.5 %copy-start = (bf16[4,4,128,128]{3,2,1,0:T(8,128)(2,1)S(1)}, bf16[4,4,128,128]{3,2,1,0:T(8,128)(2,1)}, u32[]{:S(2)}) copy-start(bf16[4,4,128,128]{3,2,1,0:T(8,128)(2,1)} %param.14) | copy-start | bytes 1572868
  37.5 9.9 %collective-permute-start = (bf16[512,128]{1,0:T(8,128)(2,1)S(1)}, bf16[512,128]{1,0:T(8,128)(2,1)S(1)}, u32[]{:S(2)}, u32[]{:S(2)}) collective-permute-start(bf16[512,128]{1,0:T(8,128)(2,1)S(1)} %place.1.refs_0_.src0), channel_id=1, source_target_pairs={{0,8},{4,12},{8,16},{12,20},{16,24},{20,28},{24,32},{28,36},{32,40... | collective-permute-start | bytes 393224 | tf_op jit(solution)/shard_map/ppermute | solution.py:333
  40.0 11.3 %collective-permute-start.1 = (bf16[512,128]{1,0:T(8,128)(2,1)S(1)}, bf16[512,128]{1,0:T(8,128)(2,1)S(1)}, u32[]{:S(2)}, u32[]{:S(2)}) collective-permute-start(bf16[512,128]{1,0:T(8,128)(2,1)S(1)} %place.1.refs_0_.src0), channel_id=1, source_target_pairs={{0,4},{4,16},{8,12},{12,24},{16,20},{20,32},{24,28},{28,40},{32,36... | collective-permute-start | bytes 393224 | tf_op jit(solution)/shard_map/ppermute | solution.py:333
  47.4 4.1 %collective-permute-start.2 = (bf16[512,128]{1,0:T(8,128)(2,1)S(1)}, bf16[512,128]{1,0:T(8,128)(2,1)S(1)}, u32[]{:S(2)}, u32[]{:S(2)}) collective-permute-start(bf16[512,128]{1,0:T(8,128)(2,1)S(1)} %collective-permute-done.two), channel_id=1, source_target_pairs={{0,4},{4,0},{8,12},{12,8},{16,20},{20,16},{24,28},{28,24},{32,36},... | collective-permute-start | bytes 393224 | tf_op jit(solution)/shard_map/ppermute | solution.py:333
  52.6 11.9 %copy-start.1 = (bf16[512,256]{1,0:T(8,128)(2,1)S(1)}, bf16[512,256]{1,0:T(8,128)(2,1)}, u32[]{:S(2)}) copy-start(bf16[512,256]{1,0:T(8,128)(2,1)} %out_grad_ref.1) | copy-start | bytes 786436
  52.6 11.9 %copy-start.2 = (bf16[128,256]{1,0:T(8,128)(2,1)S(1)}, bf16[128,256]{1,0:T(8,128)(2,1)}, u32[]{:S(2)}) copy-start(bf16[128,256]{1,0:T(8,128)(2,1)} %weight_ref.1) | copy-start | bytes 196612
  65.6 7.8 %collective-permute-start.5 = (bf16[512,128]{1,0:T(8,128)(2,1)S(1)}, bf16[512,128]{1,0:T(8,128)(2,1)S(1)}, u32[]{:S(2)}, u32[]{:S(2)}) collective-permute-start(bf16[512,128]{1,0:T(8,128)(2,1)S(1)} %get-tuple-element.27.block0), channel_id=1, source_target_pairs={{0,3},{1,0},{2,1},{3,2},{4,7},{5,4},{6,5},{7,6},{8,11},{9,8},{10,9... | collective-permute-start | bytes 393224 | tf_op jit(solution)/shard_map/ppermute | solution.py:338
  68.3 14.5 %collective-permute-start.4 = (bf16[512,128]{1,0:T(8,128)(2,1)S(1)}, bf16[512,128]{1,0:T(8,128)(2,1)S(1)}, u32[]{:S(2)}, u32[]{:S(2)}) collective-permute-start(bf16[512,128]{1,0:T(8,128)(2,1)S(1)} %get-tuple-element.27.block0), channel_id=1, source_target_pairs={{0,2},{1,3},{2,0},{3,1},{4,6},{5,7},{6,4},{7,5},{8,10},{9,11},{10,... | collective-permute-start | bytes 393224 | tf_op jit(solution)/shard_map/ppermute | solution.py:338
  71.4 11.4 %collective-permute-start.3 = (bf16[512,128]{1,0:T(8,128)(2,1)S(1)}, bf16[512,128]{1,0:T(8,128)(2,1)S(1)}, u32[]{:S(2)}, u32[]{:S(2)}) collective-permute-start(bf16[512,128]{1,0:T(8,128)(2,1)S(1)} %get-tuple-element.27.block0), channel_id=1, source_target_pairs={{0,1},{1,2},{2,3},{3,0},{4,5},{5,6},{6,7},{7,4},{8,9},{9,10},{10,1... | collective-permute-start | bytes 393224 | tf_op jit(solution)/shard_map/ppermute | solution.py:338
  74.6 21.3 %all-to-all-start.2 = ((bf16[128,4,128]{2,1,0:T(4,128)(2,1)}), bf16[128,4,128]{2,1,0:T(4,128)(2,1)S(1)}, u32[]{:S(2)}, u32[]{:S(2)}) async-start(bf16[128,4,128]{2,1,0:T(4,128)(2,1)} %bitcast.8), calls=%async_computation.2 | async-start | bytes 262144 | tf_op jit(solution)/shard_map/all_to_all | solution.py:362
  84.0 4.9 %collective-permute-start.7 = (bf16[512,128]{1,0:T(8,128)(2,1)S(1)}, bf16[512,128]{1,0:T(8,128)(2,1)S(1)}, u32[]{:S(2)}, u32[]{:S(2)}) collective-permute-start(bf16[512,128]{1,0:T(8,128)(2,1)S(1)} %get-tuple-element.31), channel_id=1, source_target_pairs={{0,4},{4,0},{8,12},{12,8},{16,20},{20,16},{24,28},{28,24},{32,36},... | collective-permute-start | bytes 393224 | tf_op jit(solution)/shard_map/ppermute | solution.py:333
  86.9 14.2 %collective-permute-start.6 = (bf16[512,128]{1,0:T(8,128)(2,1)S(1)}, bf16[512,128]{1,0:T(8,128)(2,1)S(1)}, u32[]{:S(2)}, u32[]{:S(2)}) collective-permute-start(bf16[512,128]{1,0:T(8,128)(2,1)S(1)} %get-tuple-element.29), channel_id=1, source_target_pairs={{0,500},{4,0},{8,508},{12,8},{16,4},{20,16},{24,12},{28,24},{32,20... | collective-permute-start | bytes 393224 | tf_op jit(solution)/shard_map/ppermute | solution.py:333
  88.9 12.2 %collective-permute-start.8 = (bf16[512,128]{1,0:T(8,128)(2,1)S(1)}, bf16[512,128]{1,0:T(8,128)(2,1)S(1)}, u32[]{:S(2)}, u32[]{:S(2)}) collective-permute-start(bf16[512,128]{1,0:T(8,128)(2,1)S(1)} %add.1), channel_id=1, source_target_pairs={{0,504},{4,508},{8,0},{12,4},{16,8},{20,12},{24,16},{28,20},{32,24... | collective-permute-start | bytes 393224 | tf_op jit(solution)/shard_map/ppermute | solution.py:333
  96.5 8.7 %all-to-all-start.3 = ((f32[4,8,128]{2,1,0:T(8,128)}), f32[4,8,128]{2,1,0:T(8,128)S(1)}, u32[]{:S(2)}, u32[]{:S(2)}) async-start(f32[4,8,128]{2,1,0:T(8,128)} %row.1), calls=%async_computation.3 | async-start | bytes 32768 | tf_op jit(solution)/shard_map/all_to_all | solution.py:362

commit v3 on v2

--- a/solution.py
+++ b/solution.py
@@ -104,8 +104,7 @@
         table_ref[place : place + part.shape[0]] = part[...]
         place += part.shape[0]
     odd = lax.rem(lax.axis_index("blk"), 2)
-    lane = iota((1, table_ref.shape[1]), 1)
-    table_ref[place : place + 1] = jnp.where(lane == 0, odd, lax.axis_index("rep"))
+    table_ref[place : place + 1] = jnp.full((1, table_ref.shape[1]), odd, jnp.int32)
 
 
 def start_call(features, send_rows, counts_row, degree, tables, bias_row):
@@ -203,7 +202,7 @@
 
 
 def dense_kernel(
-    parts_ref, degree_ref, weight_ref, bias_ref, out_grad_ref, hidden_ref, agg_ref, grad_pre_ref, out_ref
+    parts_ref, degree_ref, weight_ref, bias_ref, out_grad_ref, hidden_ref, out_ref, agg_ref, grad_pre_ref
 ):
     quarters, rows, width = parts_ref.shape
     summed = parts_ref[0].astype(F32)
@@ -221,50 +220,57 @@
             out_grad_ref[part].astype(F32) * (sig * (1.0 + pre * (1.0 - sig)))
         ).astype(BF16)
         grad_pre_ref[part] = grad_pre
-        out_ref[part] = (scale * dot(grad_pre, weight_ref[...], NT)).astype(BF16)
-
-
-def terms_kernel(agg_ref, grad_pre_ref, *refs):
+        grad_agg = (scale * dot(grad_pre, weight_ref[...], NT)).astype(BF16)
+        for q in range(quarters):
+            out_ref[q, part] = grad_agg
+    grad_pre = grad_pre_ref[...]
+    term = dot(agg_ref[...], grad_pre, TN).astype(BF16)
+    total = jnp.sum(grad_pre.astype(F32), axis=0, keepdims=True)
+    high = total.astype(BF16).astype(F32)
+    pieces = (high[:, :TILE], high[:, TILE:], (total - high)[:, :TILE], (total - high)[:, TILE:])
+    row = iota((16, TILE), 0)
+    ends = jnp.zeros((16, TILE), F32)
+    for k, piece in enumerate(pieces):
+        ends = jnp.where(row == k, piece, ends)
+    for q in range(quarters):
+        out_ref[q, rows : rows + width] = term[:, :TILE]
+        out_ref[q, rows + width : rows + 2 * width] = term[:, TILE:]
+        out_ref[q, rows + 2 * width :] = ends.astype(BF16)
+
+
+def terms_kernel(block_ref, *refs):
     out_ref = refs[-1]
-    grad_pre = grad_pre_ref[...]
-    width = agg_ref.shape[1]
-    term = dot(agg_ref[...], grad_pre, TN)
-    total = jnp.sum(grad_pre.astype(F32), axis=0, keepdims=True)
-    mine = iota((width, 2 * TILE), 1) // 2 == iota((width, 2 * TILE), 0)
-    pieces = jnp.concatenate([term, jnp.where(mine, total, 0.0)], axis=1).astype(BF16)
+    quarters, all_rows, width = block_ref.shape
+    rows = all_rows - 2 * width - 16
+    total = block_ref[0, rows:].astype(F32)
+    for q in range(1, quarters):
+        total = total + block_ref[q, rows:].astype(F32)
+    ends = total[2 * width :]
     lines = (4 * width, width)
-    rows = jnp.zeros((4 * width, TILE), F32)
+    out = jnp.zeros((4 * width, TILE), F32)
     for k in range(4):
+        if k < 2:
+            piece = total[k * width : (k + 1) * width]
+        else:
+            bias = ends[k - 2 : k - 1] + ends[k : k + 1]
+            mine = (iota((width, TILE), 1) + (k - 2) * TILE) // 2 == iota((width, TILE), 0)
+            piece = jnp.where(mine, bias, 0.0)
         here = iota(lines, 0) == 4 * iota(lines, 1) + k
-        rows = rows + dot(one_hot(here), pieces[:, k * TILE : (k + 1) * TILE])
-    out_ref[...] = rows.astype(BF16)
-
-
-def row_kernel(parts_ref, *refs):
-    out_ref = refs[-1]
-    count, width = parts_ref.shape
-    pairs = jnp.sum(parts_ref[...].astype(F32).reshape(count // 8, 8, width), axis=0)
-    term = jnp.concatenate([pairs[:4] + pairs[4:], jnp.zeros((4, width), F32)], axis=0)
-    for copy in range(out_ref.shape[0]):
-        out_ref[copy] = term
-
-
-def spread_kernel(
-    table_ref, tiles_ref, block0, block1, block2, block3, *refs
-):
-    own_ref, two_ref, near_ref, apart_ref, done_ref, acc_ref, block_ref = refs[-7:]
+        out = out + dot(one_hot(here), piece.astype(BF16))
+    out_ref[...] = out.astype(BF16)
+
+
+def spread_kernel(table_ref, tiles_ref, block_ref, *refs):
+    own_ref, two_ref, near_ref, apart_ref, acc_ref = refs[-5:]
     acc_ref[...] = jnp.zeros_like(acc_ref)
     most = table_ref.shape[1]
     steps = tiles_ref.shape[0] // most
-    mine = table_ref[2 * steps + 1, 1]
-    for away, block in enumerate((block0, block1, block2, block3)):
-        block_ref[lax.rem(mine + 4 - away, 4)] = block[...]
     col_tiles = own_ref.shape[0] // TILE
     for step in range(steps - 1, -1, -1):
         for k in range(most):
             col = pl.multiple_of(table_ref[steps + step, k] * TILE, TILE)
             quarter = table_ref[step, k] // col_tiles
-            row = pl.multiple_of((table_ref[step, k] - quarter * col_tiles) * TILE, TILE)
+            row = pl.multiple_of(table_ref[step, k] % col_tiles * TILE, TILE)
             live = (k < table_ref[2 * steps, step]).astype(F32)
             prod = dot(tiles_ref[step * most + k], block_ref[quarter, pl.ds(row, TILE), :])
             acc_ref[step, pl.ds(col, TILE), :] += prod * live
@@ -273,7 +279,6 @@
     two_ref[...] = acc_ref[2]
     near_ref[...] = acc_ref[1 + 2 * odd].astype(BF16)
     apart_ref[...] = acc_ref[3 - 2 * odd].astype(BF16)
-    done_ref[...] = jnp.zeros_like(done_ref)
 
 
 def add_kernel(a_ref, b_ref, out_ref):
@@ -290,8 +295,10 @@
     total = own_ref[...] + in1[...].astype(F32) + in2[...].astype(F32)
     grads = scaled_rows(degree_ref, total).astype(BF16)
     slots = dot(unplace_ref[...], grads).astype(BF16)
-    term = (terms_ref[0] + terms_ref[1]) + (terms_ref[2] + terms_ref[3])
-    term = jnp.concatenate([term, jnp.zeros((TILE - 8, term.shape[1]), F32)], axis=0).astype(BF16)
+    count, width = terms_ref.shape
+    pairs = jnp.sum(terms_ref[...].astype(F32).reshape(count // 8, 8, width), axis=0)
+    term = jnp.concatenate([pairs[:4] + pairs[4:], jnp.zeros((TILE - 4, width), F32)], axis=0)
+    term = term.astype(BF16)
     lines = (TILE // 8 * 12, TILE)
     owner, slot = slot_of(lines, 0)
     widen = one_hot((slot < 8) & (owner * 8 + slot == iota(lines, 1)))
@@ -333,11 +340,6 @@
     return lax.ppermute(value, "blk", [(s, target(s) % count) for s in range(count)])
 
 
-def around(value, steps):
-    count = lax.axis_size("rep")
-    return lax.ppermute(value, "rep", [(s, (s + steps) % count) for s in range(count)])
-
-
 def two_on(blk):
     return blk + 2
 
@@ -416,38 +418,33 @@
         (turned, unplace),
     )
     parts = exchange(partial, "rep")
-    hidden, agg, grad_pre, grad_agg = call(
+    hidden, sent = call(
         dense_kernel,
         (
             shape((rows, hidden_width), BF16),
-            shape((rows, width), BF16),
-            shape((rows, hidden_width), BF16),
-            shape((rows, width), BF16),
+            shape((quarters, rows + 2 * width + 16, width), BF16),
         ),
         "dense",
+        (pltpu.VMEM((rows, width), BF16), pltpu.VMEM((rows, hidden_width), BF16)),
     )(parts, scale, weight, bias_row, out_grad)
-    block = [grad_agg] + [around(grad_agg, away) for away in range(1, quarters)]
-    terms = call(terms_kernel, shape((4 * width, TILE), BF16), "terms")(
-        agg, grad_pre, after=(block[3],)
-    )
+    block = exchange(sent, "rep")
+    terms = call(terms_kernel, shape((4 * width, TILE), BF16), "terms")(block)
+    lines = terms
     terms = exchange(terms.reshape(blocks, 4, TILE), "blk").reshape(4 * width, TILE)
 
-    own, two, near, apart, spread = tile_call(
+    own, two, near, apart = tile_call(
         spread_kernel,
-        (shape((rows, width), F32),) * 2
-        + (shape((rows, width), BF16),) * 2
-        + (shape((8, TILE), F32),),
-        [pltpu.VMEM((steps, rows, width), F32), pltpu.VMEM((quarters, rows, width), BF16)],
+        (shape((rows, width), F32),) * 2 + (shape((rows, width), BF16),) * 2,
+        [pltpu.VMEM((steps, rows, width), F32)],
         "spread_tiles",
         table,
-        (turned, *block),
+        (turned, block),
+        (lines,),
     )
     near = moved(near, other_core)
     apart = moved(apart, apart_back)
     two = moved(call(add_kernel, shape((rows, width), BF16), "add")(two, near), two_back)
-    terms = call(row_kernel, shape((quarters, 8, TILE), F32), "row")(terms, after=(spread,))
-    terms = exchange(terms, "rep")
-    back = call(back_kernel, shape((blocks * (slots + 4), width), BF16), "back", flops=4 * 10**10)(
+    back = call(back_kernel, shape((blocks * (slots + 4), width), BF16), "back")(
         own, apart, two, scale, unplace, terms
     )
     returned = exchange(back.reshape(blocks, 3, 4, width), "blk").reshape(back.shape)

time: 137 us -> 136 us (level)
  blocking collectives: 73.6 us -> 86.8 us
  starting transfers between devices: 40.9 us -> 28.8 us
    all_to_all x3 -> x4, blocking collectives: 73.6 us -> 86.8 us  [exchange(): return lax.all_to_all(value, axis, split_axis=0, concat_axis=0, tiled=True)]
    ppermute x3 -> x0, starting transfers between devices: 7.8 us -> none  [around(): lax.ppermute(value, 'rep', [(s, (s + steps) % count) for s in range(count)])]
    all_to_all x2 -> x1, starting transfers between devices: 12.7 us -> 5.31 us  [exchange(): return lax.all_to_all(value, axis, split_axis=0, concat_axis=0, tiled=True)]
    ppermute x6, starting transfers between devices: 20.3 us -> 23.5 us  [moved(): lax.ppermute(value, 'blk', [(s, target(s) % count) for s in range(count)])]
    all_to_all x2 -> x1, waiting for transfers between devices: 4.21 us -> 3.01 us  [exchange(): return lax.all_to_all(value, axis, split_axis=0, concat_axis=0, tiled=True)]
    pallas_call x9 -> x8, Pallas kernels: 7.07 us -> 6.21 us  [run(): kernel_call(kernel, outs, specs, name, scratch, flops)(*arrays, *after)]
  transfers between devices with their start and end apart: 11 -> 7, of which waited for: 3 -> 4; matrix products, arithmetic and copies ran while one was open for 0% -> 0% of each run, Pallas kernels for 3% -> 1%
where the time goes in v3:
time: 136 us
  blocking collectives  86.8 us (64%)
  starting transfers between devices  28.8 us (21%)
  Pallas kernels  10.7 us (8%)
  waiting for transfers between devices  8.63 us (6%)
    all_to_all x4, blocking collectives, exchange(): return lax.all_to_all(value, axis, split_axis=0, concat_axis=0, tiled=True)  86.8 us
    ppermute x6, starting transfers between devices, moved(): lax.ppermute(value, 'blk', [(s, target(s) % count) for s in range(count)])  23.5 us
    pallas_call x8, Pallas kernels, run(): kernel_call(kernel, outs, specs, name, scratch, flops)(*arrays, *after)  6.21 us
    ppermute x6, waiting for transfers between devices, moved(): lax.ppermute(value, 'blk', [(s, target(s) % count) for s in range(count)])  5.62 us
    all_to_all x1, starting transfers between devices, exchange(): return lax.all_to_all(value, axis, split_axis=0, concat_axis=0, tiled=True)  5.31 us
    all_to_all x1, waiting for transfers between devices, exchange(): return lax.all_to_all(value, axis, split_axis=0, concat_axis=0, tiled=True)  3.01 us
  transfers between devices with their start and end apart: 7, of which 4 were waited for; matrix products, arithmetic and copies ran while one was open for 0% of the time, Pallas kernels for 1%

profile of v3, /device:TPU:1, one launch (start us, length us, event | category | flops | bytes accessed | tf_op | source)
XLA Modules:
  0.0 135.8 jit_solution(7030635601462512441)
XLA Ops:
  0.6 2.4 %start.1 = (bf16[1024,128]{1,0:T(8,128)(2,1)S(1)}, f32[4,128]{1,0:T(4,128)S(1)}, f32[1,256]{1,0:T(1,128)S(1)}, s32[10,4]{1,0:T(8,128)S(1)}, f32[8,1024]{1,0:T(8,128)S(1)}) custom-call(bf16[512,128]{1,0:T(8,128)(2,1)} %refs_0_.1, s32[8,128]{1,0:T(8,128)} %bitcast.21, s32[1,128]{1,0:T(1,128)} %bitcast.25, f32[4,128]{1,0:T(4,128)} %bitcast.22, s32[4,4]{1,0:T(4,128)} %refs_4_.1, ...), custom_call_target="tpu_custom_call" | custom-call | flops 100000000 | bytes 1000000 | tf_op jit(solution)/shard_map/start/pallas_call | solution.py:115
  3.1 33.6 %all_to_all.25 = bf16[128,8,128]{2,1,0:T(8,128)(2,1)S(1)} all-to-all(bf16[128,8,128]{2,1,0:T(8,128)(2,1)S(1)} %bitcast.20), channel_id=1, replica_groups=mesh['blk'=128,'rep'=4] {'blk'}, dimensions={0} | all-to-all | bytes 524288 | tf_op jit(solution)/shard_map/all_to_all | solution.py:364
  36.7 0.8 place.1.refs_0_.src0
  37.5 2.5 %collective-permute-start = (bf16[512,128]{1,0:T(8,128)(2,1)S(1)}, bf16[512,128]{1,0:T(8,128)(2,1)S(1)}, u32[]{:S(2)}, u32[]{:S(2)}) collective-permute-start(bf16[512,128]{1,0:T(8,128)(2,1)S(1)} %place.1.refs_0_.src0), channel_id=1, source_target_pairs={{0,8},{4,12},{8,16},{12,20},{16,24},{20,28},{24,32},{28,36},{32,40... | collective-permute-start | bytes 393224 | tf_op jit(solution)/shard_map/ppermute | solution.py:340
  40.0 3.0 %collective-permute-start.1 = (bf16[512,128]{1,0:T(8,128)(2,1)S(1)}, bf16[512,128]{1,0:T(8,128)(2,1)S(1)}, u32[]{:S(2)}, u32[]{:S(2)}) collective-permute-start(bf16[512,128]{1,0:T(8,128)(2,1)S(1)} %place.1.refs_0_.src0), channel_id=1, source_target_pairs={{0,4},{4,16},{8,12},{12,24},{16,20},{20,32},{24,28},{28,40},{32,36... | collective-permute-start | bytes 393224 | tf_op jit(solution)/shard_map/ppermute | solution.py:340
  43.0 4.5 %collective-permute-done.two = bf16[512,128]{1,0:T(8,128)(2,1)S(1)} collective-permute-done((bf16[512,128]{1,0:T(8,128)(2,1)S(1)}, bf16[512,128]{1,0:T(8,128)(2,1)S(1)}, u32[]{:S(2)}, u32[]{:S(2)}) %collective-permute-start) | collective-permute-done | bytes 131104 | tf_op jit(solution)/shard_map/ppermute | solution.py:340
  47.4 3.1 %collective-permute-start.2 = (bf16[512,128]{1,0:T(8,128)(2,1)S(1)}, bf16[512,128]{1,0:T(8,128)(2,1)S(1)}, u32[]{:S(2)}, u32[]{:S(2)}) collective-permute-start(bf16[512,128]{1,0:T(8,128)(2,1)S(1)} %collective-permute-done.two), channel_id=1, source_target_pairs={{0,4},{4,0},{8,12},{12,8},{16,20},{20,16},{24,28},{28,24},{32,36},... | collective-permute-start | bytes 393224 | tf_op jit(solution)/shard_map/ppermute | solution.py:340
  50.8 0.5 unplace.1.refs_1_.unplace_ref
  51.3 0.2 collective-permute-done.2.near
  51.5 1.0 gather_tiles.1
  52.6 11.9 %all_to_all.26.parts_ref = bf16[4,512,128]{2,1,0:T(8,128)(2,1)S(1)} all-to-all(bf16[4,512,128]{2,1,0:T(8,128)(2,1)S(1)} %gather_tiles.1), channel_id=1, replica_groups=mesh['blk'=128,'rep'=4] {'rep'}, dimensions={0} | all-to-all | bytes 1048576 | tf_op jit(solution)/shard_map/all_to_all | solution.py:364
  64.4 1.2 dense.1
  65.6 12.4 %all_to_all.27.block_ref = bf16[4,784,128]{2,1,0:T(8,128)(2,1)S(1)} all-to-all(bf16[4,784,128]{2,1,0:T(8,128)(2,1)S(1)} %get-tuple-element.24), channel_id=1, replica_groups=mesh['blk'=128,'rep'=4] {'rep'}, dimensions={0} | all-to-all | bytes 1605632 | tf_op jit(solution)/shard_map/all_to_all | solution.py:364
  78.0 1.0 terms.1.refs_0_
  79.0 1.0 spread_tiles.1
  80.0 5.3 %collective-permute-start.4 = (bf16[512,128]{1,0:T(8,128)(2,1)S(1)}, bf16[512,128]{1,0:T(8,128)(2,1)S(1)}, u32[]{:S(2)}, u32[]{:S(2)}) collective-permute-start(bf16[512,128]{1,0:T(8,128)(2,1)S(1)} %get-tuple-element.28), channel_id=1, source_target_pairs={{0,4},{4,0},{8,12},{12,8},{16,20},{20,16},{24,28},{28,24},{32,36},... | collective-permute-start | bytes 393224 | tf_op jit(solution)/shard_map/ppermute | solution.py:340
  85.4 5.3 %all-to-all-start.3 = ((bf16[128,4,128]{2,1,0:T(4,128)(2,1)}), bf16[128,4,128]{2,1,0:T(4,128)(2,1)S(1)}, u32[]{:S(2)}, u32[]{:S(2)}) async-start(bf16[128,4,128]{2,1,0:T(4,128)(2,1)} %bitcast.8), calls=%async_computation.3 | async-start | bytes 262144 | tf_op jit(solution)/shard_map/all_to_all | solution.py:364
  90.7 2.8 %collective-permute-start.3 = (bf16[512,128]{1,0:T(8,128)(2,1)S(1)}, bf16[512,128]{1,0:T(8,128)(2,1)S(1)}, u32[]{:S(2)}, u32[]{:S(2)}) collective-permute-start(bf16[512,128]{1,0:T(8,128)(2,1)S(1)} %get-tuple-element.26), channel_id=1, source_target_pairs={{0,500},{4,0},{8,508},{12,8},{16,4},{20,16},{24,12},{28,24},{32,20... | collective-permute-start | bytes 393224 | tf_op jit(solution)/shard_map/ppermute | solution.py:340
  93.5 6.8 %collective-permute-start.5 = (bf16[512,128]{1,0:T(8,128)(2,1)S(1)}, bf16[512,128]{1,0:T(8,128)(2,1)S(1)}, u32[]{:S(2)}, u32[]{:S(2)}) collective-permute-start(bf16[512,128]{1,0:T(8,128)(2,1)S(1)} %add.1), channel_id=1, source_target_pairs={{0,504},{4,508},{8,0},{12,4},{16,8},{20,12},{24,16},{28,20},{32,24... | collective-permute-start | bytes 393224 | tf_op jit(solution)/shard_map/ppermute | solution.py:340
  100.4 3.0 %all-to-all-done.3 = bf16[128,4,128]{2,1,0:T(4,128)(2,1)S(1)} async-done(((bf16[128,4,128]{2,1,0:T(4,128)(2,1)}), bf16[128,4,128]{2,1,0:T(4,128)(2,1)S(1)}, u32[]{:S(2)}, u32[]{:S(2)}) %all-to-all-start.3) | async-done | bytes 131104 | tf_op jit(solution)/shard_map/all_to_all | solution.py:364
  103.4 0.9 collective-permute-done.5.in2
  104.3 0.8 back.1
  105.1 29.0 %all_to_all.28 = bf16[128,3,4,128]{3,2,1,0:T(4,128)(2,1)S(1)} all-to-all(bf16[128,3,4,128]{3,2,1,0:T(4,128)(2,1)S(1)} %bitcast.15), channel_id=1, replica_groups=mesh['blk'=128,'rep'=4] {'blk'}, dimensions={0} | all-to-all | bytes 786432 | tf_op jit(solution)/shard_map/all_to_all | solution.py:364
  134.1 1.7 %last.1 = (bf16[512,128]{1,0:T(8,128)(2,1)}, f32[128,256]{1,0:T(8,128)}, f32[1,256]{1,0:T(1,128)}) custom-call(f32[8,1024]{1,0:T(8,128)S(1)} %get-tuple-element.23.key_ref, bf16[1536,128]{1,0:T(8,128)(2,1)S(1)} %bitcast.16), custom_call_target="tpu_custom_call" | custom-call | flops 100000000 | bytes 1000000 | tf_op jit(solution)/shard_map/last/pallas_call | solution.py:46
  (11 shorter events, 0.3 us)
Async XLA Ops:
  3.1 47.5 %copy-start = (bf16[4,4,128,128]{3,2,1,0:T(8,128)(2,1)S(1)}, bf16[4,4,128,128]{3,2,1,0:T(8,128)(2,1)}, u32[]{:S(2)}) copy-start(bf16[4,4,128,128]{3,2,1,0:T(8,128)(2,1)} %param.14) | copy-start | bytes 1572868
  37.5 9.9 %collective-permute-start = (bf16[512,128]{1,0:T(8,128)(2,1)S(1)}, bf16[512,128]{1,0:T(8,128)(2,1)S(1)}, u32[]{:S(2)}, u32[]{:S(2)}) collective-permute-start(bf16[512,128]{1,0:T(8,128)(2,1)S(1)} %place.1.refs_0_.src0), channel_id=1, source_target_pairs={{0,8},{4,12},{8,16},{12,20},{16,24},{20,28},{24,32},{28,36},{32,40... | collective-permute-start | bytes 393224 | tf_op jit(solution)/shard_map/ppermute | solution.py:340
  40.0 11.3 %collective-permute-start.1 = (bf16[512,128]{1,0:T(8,128)(2,1)S(1)}, bf16[512,128]{1,0:T(8,128)(2,1)S(1)}, u32[]{:S(2)}, u32[]{:S(2)}) collective-permute-start(bf16[512,128]{1,0:T(8,128)(2,1)S(1)} %place.1.refs_0_.src0), channel_id=1, source_target_pairs={{0,4},{4,16},{8,12},{12,24},{16,20},{20,32},{24,28},{28,40},{32,36... | collective-permute-start | bytes 393224 | tf_op jit(solution)/shard_map/ppermute | solution.py:340
  47.4 4.1 %collective-permute-start.2 = (bf16[512,128]{1,0:T(8,128)(2,1)S(1)}, bf16[512,128]{1,0:T(8,128)(2,1)S(1)}, u32[]{:S(2)}, u32[]{:S(2)}) collective-permute-start(bf16[512,128]{1,0:T(8,128)(2,1)S(1)} %collective-permute-done.two), channel_id=1, source_target_pairs={{0,4},{4,0},{8,12},{12,8},{16,20},{20,16},{24,28},{28,24},{32,36},... | collective-permute-start | bytes 393224 | tf_op jit(solution)/shard_map/ppermute | solution.py:340
  52.5 11.9 %copy-start.1 = (bf16[512,256]{1,0:T(8,128)(2,1)S(1)}, bf16[512,256]{1,0:T(8,128)(2,1)}, u32[]{:S(2)}) copy-start(bf16[512,256]{1,0:T(8,128)(2,1)} %out_grad_ref.1) | copy-start | bytes 786436
  52.6 11.9 %copy-start.2 = (bf16[128,256]{1,0:T(8,128)(2,1)S(1)}, bf16[128,256]{1,0:T(8,128)(2,1)}, u32[]{:S(2)}) copy-start(bf16[128,256]{1,0:T(8,128)(2,1)} %weight_ref.1) | copy-start | bytes 196612
  80.0 13.5 %collective-permute-start.4 = (bf16[512,128]{1,0:T(8,128)(2,1)S(1)}, bf16[512,128]{1,0:T(8,128)(2,1)S(1)}, u32[]{:S(2)}, u32[]{:S(2)}) collective-permute-start(bf16[512,128]{1,0:T(8,128)(2,1)S(1)} %get-tuple-element.28), channel_id=1, source_target_pairs={{0,4},{4,0},{8,12},{12,8},{16,20},{20,16},{24,28},{28,24},{32,36},... | collective-permute-start | bytes 393224 | tf_op jit(solution)/shard_map/ppermute | solution.py:340
  85.4 18.0 %all-to-all-start.3 = ((bf16[128,4,128]{2,1,0:T(4,128)(2,1)}), bf16[128,4,128]{2,1,0:T(4,128)(2,1)S(1)}, u32[]{:S(2)}, u32[]{:S(2)}) async-start(bf16[128,4,128]{2,1,0:T(4,128)(2,1)} %bitcast.8), calls=%async_computation.3 | async-start | bytes 262144 | tf_op jit(solution)/shard_map/all_to_all | solution.py:364
  90.7 9.7 %collective-permute-start.3 = (bf16[512,128]{1,0:T(8,128)(2,1)S(1)}, bf16[512,128]{1,0:T(8,128)(2,1)S(1)}, u32[]{:S(2)}, u32[]{:S(2)}) collective-permute-start(bf16[512,128]{1,0:T(8,128)(2,1)S(1)} %get-tuple-element.26), channel_id=1, source_target_pairs={{0,500},{4,0},{8,508},{12,8},{16,4},{20,16},{24,12},{28,24},{32,20... | collective-permute-start | bytes 393224 | tf_op jit(solution)/shard_map/ppermute | solution.py:340
  93.5 10.8 %collective-permute-start.5 = (bf16[512,128]{1,0:T(8,128)(2,1)S(1)}, bf16[512,128]{1,0:T(8,128)(2,1)S(1)}, u32[]{:S(2)}, u32[]{:S(2)}) collective-permute-start(bf16[512,128]{1,0:T(8,128)(2,1)S(1)} %add.1), channel_id=1, source_target_pairs={{0,504},{4,508},{8,0},{12,4},{16,8},{20,12},{24,16},{28,20},{32,24... | collective-permute-start | bytes 393224 | tf_op jit(solution)/shard_map/ppermute | solution.py:340

commit v4 on v3

--- a/solution.py
+++ b/solution.py
@@ -238,16 +238,16 @@
         out_ref[q, rows + 2 * width :] = ends.astype(BF16)
 
 
-def terms_kernel(block_ref, *refs):
-    out_ref = refs[-1]
+def terms_halves(block_ref):
     quarters, all_rows, width = block_ref.shape
     rows = all_rows - 2 * width - 16
     total = block_ref[0, rows:].astype(F32)
     for q in range(1, quarters):
         total = total + block_ref[q, rows:].astype(F32)
     ends = total[2 * width :]
-    lines = (4 * width, width)
-    out = jnp.zeros((4 * width, TILE), F32)
+    half = width // 2
+    lines = (4 * half, half)
+    out = [jnp.zeros((4 * half, TILE), F32) for _ in range(2)]
     for k in range(4):
         if k < 2:
             piece = total[k * width : (k + 1) * width]
@@ -255,13 +255,14 @@
             bias = ends[k - 2 : k - 1] + ends[k : k + 1]
             mine = (iota((width, TILE), 1) + (k - 2) * TILE) // 2 == iota((width, TILE), 0)
             piece = jnp.where(mine, bias, 0.0)
-        here = iota(lines, 0) == 4 * iota(lines, 1) + k
-        out = out + dot(one_hot(here), piece.astype(BF16))
-    out_ref[...] = out.astype(BF16)
+        here = one_hot(iota(lines, 0) == 4 * iota(lines, 1) + k)
+        piece = piece.astype(BF16)
+        out = [out[h] + dot(here, piece[h * half : (h + 1) * half]) for h in range(2)]
+    return out
 
 
 def spread_kernel(table_ref, tiles_ref, block_ref, *refs):
-    own_ref, two_ref, near_ref, apart_ref, acc_ref = refs[-5:]
+    own_ref, two_ref, near_ref, apart_ref, mine_ref, acc_ref = refs
     acc_ref[...] = jnp.zeros_like(acc_ref)
     most = table_ref.shape[1]
     steps = tiles_ref.shape[0] // most
@@ -277,12 +278,18 @@
     odd = table_ref[2 * steps + 1, 0]
     own_ref[...] = acc_ref[0]
     two_ref[...] = acc_ref[2]
-    near_ref[...] = acc_ref[1 + 2 * odd].astype(BF16)
+    rows = own_ref.shape[0]
+    near_ref[:rows] = acc_ref[1 + 2 * odd].astype(BF16)
+    first, second = terms_halves(block_ref)
+    mine_ref[...] = jnp.where(odd == 0, first, second)
+    near_ref[rows:] = jnp.where(odd == 0, second, first).astype(BF16)
     apart_ref[...] = acc_ref[3 - 2 * odd].astype(BF16)
 
 
-def add_kernel(a_ref, b_ref, out_ref):
-    out_ref[...] = (a_ref[...] + b_ref[...].astype(F32)).astype(BF16)
+def add_kernel(two_ref, mine_ref, near_ref, out_ref, terms_ref):
+    rows = out_ref.shape[0]
+    out_ref[...] = (two_ref[...] + near_ref[:rows].astype(F32)).astype(BF16)
+    terms_ref[...] = (mine_ref[...] + near_ref[rows:].astype(F32)).astype(BF16)
 
 
 def slot_of(lines, dim):
@@ -315,8 +322,8 @@
     owner, slot = slot_of(lines, 1)
     row = iota(lines, 0)
     wanted = (slot < 8) & (owner * 8 + slot == row)
-    wanted |= (slot == 8) & (owner + TILE == row)
-    wanted |= (slot == 9) & (owner + TILE + owners == row)
+    place = TILE + owner % 2 * (owners // 2) + owner // 2
+    wanted |= ((slot == 8) & (place == row)) | ((slot == 9) & (place + owners == row))
     wanted |= ((slot == 10) & (row == TILE + 2 * owners)) | ((slot == 11) & (row == TILE + 2 * owners + 1))
     pick = one_hot(wanted)
     total = jnp.zeros((rows, TILE), F32)
@@ -327,8 +334,11 @@
         here = one_hot(iota((rows, TILE), 0).astype(F32) == key_ref[0:1, span])
         total = total + dot(here, found[:TILE].astype(BF16))
         for k in range(2):
-            part = found[TILE + k * owners : TILE + (k + 1) * owners]
-            weight_ref[t * owners : (t + 1) * owners, k * TILE : (k + 1) * TILE] = part
+            for core in range(2):
+                start = TILE + (2 * k + core) * (owners // 2)
+                line = core * (weight_ref.shape[0] // 2) + t * (owners // 2)
+                part = found[start : start + owners // 2]
+                weight_ref[line : line + owners // 2, k * TILE : (k + 1) * TILE] = part
         bias = bias + found[TILE + 2 * owners :]
     out_ref[...] = total.astype(BF16)
     bias_ref[:, :TILE] = bias[0:1]
@@ -360,8 +370,10 @@
     return blk + 1 - 2 * (blk % 2)
 
 
-def exchange(value, axis):
-    return lax.all_to_all(value, axis, split_axis=0, concat_axis=0, tiled=True)
+def exchange(value, axis, groups=None):
+    return lax.all_to_all(
+        value, axis, split_axis=0, concat_axis=0, axis_index_groups=groups, tiled=True
+    )
 
 
 def tile_call(kernel, outs, scratch, name, table, arrays, after=()):
@@ -428,22 +440,28 @@
         (pltpu.VMEM((rows, width), BF16), pltpu.VMEM((rows, hidden_width), BF16)),
     )(parts, scale, weight, bias_row, out_grad)
     block = exchange(sent, "rep")
-    terms = call(terms_kernel, shape((4 * width, TILE), BF16), "terms")(block)
-    lines = terms
-    terms = exchange(terms.reshape(blocks, 4, TILE), "blk").reshape(4 * width, TILE)
-
-    own, two, near, apart = tile_call(
+    own, two, near, apart, mine = tile_call(
         spread_kernel,
-        (shape((rows, width), F32),) * 2 + (shape((rows, width), BF16),) * 2,
+        (
+            shape((rows, width), F32),
+            shape((rows, width), F32),
+            shape((rows + 2 * width, width), BF16),
+            shape((rows, width), BF16),
+            shape((2 * width, width), F32),
+        ),
         [pltpu.VMEM((steps, rows, width), F32)],
         "spread_tiles",
         table,
         (turned, block),
-        (lines,),
     )
     near = moved(near, other_core)
     apart = moved(apart, apart_back)
-    two = moved(call(add_kernel, shape((rows, width), BF16), "add")(two, near), two_back)
+    two, terms = call(
+        add_kernel, (shape((rows, width), BF16), shape((2 * width, width), BF16)), "add"
+    )(two, mine, near)
+    two = moved(two, two_back)
+    cores = [list(range(core, blocks, 2)) for core in range(2)]
+    terms = exchange(terms.reshape(blocks // 2, 4, width), "blk", cores).reshape(terms.shape)
     back = call(back_kernel, shape((blocks * (slots + 4), width), BF16), "back")(
         own, apart, two, scale, unplace, terms
     )

time: 136 us -> 134 us (0.985)
  waiting for transfers between devices: 8.63 us -> 15.8 us
  starting transfers between devices: 28.8 us -> 22.4 us
  blocking collectives: 86.8 us -> 84.5 us
    all_to_all x1, waiting for transfers between devices: 3.01 us -> 11.1 us  [exchange(): lax.all_to_all(value, axis, split_axis=0, concat_axis=0, axis_index_group...]
    ppermute x6, starting transfers between devices: 23.5 us -> 17.7 us  [moved(): lax.ppermute(value, 'blk', [(s, target(s) % count) for s in range(count)])]
    all_to_all x4, blocking collectives: 86.8 us -> 84.5 us  [exchange(): lax.all_to_all(value, axis, split_axis=0, concat_axis=0, axis_index_group...]
    pallas_call x8 -> x7, Pallas kernels: 6.21 us -> 5.87 us  [run(): kernel_call(kernel, outs, specs, name, scratch, flops)(*arrays, *after)]
  transfers between devices with their start and end apart: 7 -> 7, of which waited for: 4 -> 3; matrix products, arithmetic and copies ran while one was open for 0% -> 0% of each run, Pallas kernels for 1% -> 1%
where the time goes in v4:
time: 134 us
  blocking collectives  84.5 us (63%)
  starting transfers between devices  22.4 us (17%)
  waiting for transfers between devices  15.8 us (12%)
  Pallas kernels  10.5 us (8%)
    all_to_all x4, blocking collectives, exchange(): lax.all_to_all(value, axis, split_axis=0, concat_axis=0, axis_index_group...  84.5 us
    ppermute x6, starting transfers between devices, moved(): lax.ppermute(value, 'blk', [(s, target(s) % count) for s in range(count)])  17.7 us
    all_to_all x1, waiting for transfers between devices, exchange(): lax.all_to_all(value, axis, split_axis=0, concat_axis=0, axis_index_group...  11.1 us
    pallas_call x7, Pallas kernels, run(): kernel_call(kernel, outs, specs, name, scratch, flops)(*arrays, *after)  5.87 us
    all_to_all x1, starting transfers between devices, exchange(): lax.all_to_all(value, axis, split_axis=0, concat_axis=0, axis_index_group...  4.7 us
    ppermute x6, waiting for transfers between devices, moved(): lax.ppermute(value, 'blk', [(s, target(s) % count) for s in range(count)])  4.69 us
  transfers between devices with their start and end apart: 7, of which 3 were waited for; matrix products, arithmetic and copies ran while one was open for 0% of the time, Pallas kernels for 1%

profile of v4, /device:TPU:1, one launch (start us, length us, event | category | flops | bytes accessed | tf_op | source)
XLA Modules:
  0.0 134.0 jit_solution(2002458727411503195)
XLA Ops:
  0.6 2.4 %start.1 = (bf16[1024,128]{1,0:T(8,128)(2,1)S(1)}, f32[4,128]{1,0:T(4,128)S(1)}, f32[1,256]{1,0:T(1,128)S(1)}, s32[10,4]{1,0:T(8,128)S(1)}, f32[8,1024]{1,0:T(8,128)S(1)}) custom-call(bf16[512,128]{1,0:T(8,128)(2,1)} %refs_0_.1, s32[8,128]{1,0:T(8,128)} %bitcast.21, s32[1,128]{1,0:T(1,128)} %bitcast.25, f32[4,128]{1,0:T(4,128)} %bitcast.22, s32[4,4]{1,0:T(4,128)} %refs_4_.1, ...), custom_call_target="tpu_custom_call" | custom-call | flops 100000000 | bytes 1000000 | tf_op jit(solution)/shard_map/start/pallas_call | solution.py:115
  3.1 33.6 %all_to_all.25 = bf16[128,8,128]{2,1,0:T(8,128)(2,1)S(1)} all-to-all(bf16[128,8,128]{2,1,0:T(8,128)(2,1)S(1)} %bitcast.20), channel_id=1, replica_groups=mesh['blk'=128,'rep'=4] {'blk'}, dimensions={0} | all-to-all | bytes 524288 | tf_op jit(solution)/shard_map/all_to_all | solution.py:374
  36.7 0.8 place.1.refs_0_.src0
  37.5 2.5 %collective-permute-start = (bf16[512,128]{1,0:T(8,128)(2,1)S(1)}, bf16[512,128]{1,0:T(8,128)(2,1)S(1)}, u32[]{:S(2)}, u32[]{:S(2)}) collective-permute-start(bf16[512,128]{1,0:T(8,128)(2,1)S(1)} %place.1.refs_0_.src0), channel_id=1, source_target_pairs={{0,8},{4,12},{8,16},{12,20},{16,24},{20,28},{24,32},{28,36},{32,40... | collective-permute-start | bytes 393224 | tf_op jit(solution)/shard_map/ppermute | solution.py:350
  40.0 3.0 %collective-permute-start.1 = (bf16[512,128]{1,0:T(8,128)(2,1)S(1)}, bf16[512,128]{1,0:T(8,128)(2,1)S(1)}, u32[]{:S(2)}, u32[]{:S(2)}) collective-permute-start(bf16[512,128]{1,0:T(8,128)(2,1)S(1)} %place.1.refs_0_.src0), channel_id=1, source_target_pairs={{0,4},{4,16},{8,12},{12,24},{16,20},{20,32},{24,28},{28,40},{32,36... | collective-permute-start | bytes 393224 | tf_op jit(solution)/shard_map/ppermute | solution.py:350
  43.0 4.5 %collective-permute-done.two = bf16[512,128]{1,0:T(8,128)(2,1)S(1)} collective-permute-done((bf16[512,128]{1,0:T(8,128)(2,1)S(1)}, bf16[512,128]{1,0:T(8,128)(2,1)S(1)}, u32[]{:S(2)}, u32[]{:S(2)}) %collective-permute-start) | collective-permute-done | bytes 131104 | tf_op jit(solution)/shard_map/ppermute | solution.py:350
  47.4 3.1 %collective-permute-start.2 = (bf16[512,128]{1,0:T(8,128)(2,1)S(1)}, bf16[512,128]{1,0:T(8,128)(2,1)S(1)}, u32[]{:S(2)}, u32[]{:S(2)}) collective-permute-start(bf16[512,128]{1,0:T(8,128)(2,1)S(1)} %collective-permute-done.two), channel_id=1, source_target_pairs={{0,4},{4,0},{8,12},{12,8},{16,20},{20,16},{24,28},{28,24},{32,36},... | collective-permute-start | bytes 393224 | tf_op jit(solution)/shard_map/ppermute | solution.py:350
  50.6 0.2 turn.1.refs_0_.tiles_ref
  50.8 0.5 unplace.1.refs_1_.unplace_ref
  51.3 0.2 collective-permute-done.2.near
  51.5 1.0 gather_tiles.1
  52.6 11.9 %all_to_all.26.parts_ref = bf16[4,512,128]{2,1,0:T(8,128)(2,1)S(1)} all-to-all(bf16[4,512,128]{2,1,0:T(8,128)(2,1)S(1)} %gather_tiles.1), channel_id=1, replica_groups=mesh['blk'=128,'rep'=4] {'rep'}, dimensions={0} | all-to-all | bytes 1048576 | tf_op jit(solution)/shard_map/all_to_all | solution.py:374
  64.4 1.2 dense.1
  65.6 12.3 %all_to_all.27.block_ref = bf16[4,784,128]{2,1,0:T(8,128)(2,1)S(1)} all-to-all(bf16[4,784,128]{2,1,0:T(8,128)(2,1)S(1)} %get-tuple-element.27), channel_id=1, replica_groups=mesh['blk'=128,'rep'=4] {'rep'}, dimensions={0} | all-to-all | bytes 1605632 | tf_op jit(solution)/shard_map/all_to_all | solution.py:374
  77.9 1.2 spread_tiles.1
  79.1 5.4 %collective-permute-start.4 = (bf16[768,128]{1,0:T(8,128)(2,1)S(1)}, bf16[768,128]{1,0:T(8,128)(2,1)S(1)}, u32[]{:S(2)}, u32[]{:S(2)}) collective-permute-start(bf16[768,128]{1,0:T(8,128)(2,1)S(1)} %get-tuple-element.32), channel_id=1, source_target_pairs={{0,4},{4,0},{8,12},{12,8},{16,20},{20,16},{24,28},{28,24},{32,36},... | collective-permute-start | bytes 589832 | tf_op jit(solution)/shard_map/ppermute | solution.py:350
  84.5 1.9 %collective-permute-start.3 = (bf16[512,128]{1,0:T(8,128)(2,1)S(1)}, bf16[512,128]{1,0:T(8,128)(2,1)S(1)}, u32[]{:S(2)}, u32[]{:S(2)}) collective-permute-start(bf16[512,128]{1,0:T(8,128)(2,1)S(1)} %get-tuple-element.29), channel_id=1, source_target_pairs={{0,500},{4,0},{8,508},{12,8},{16,4},{20,16},{24,12},{28,24},{32,20... | collective-permute-start | bytes 393224 | tf_op jit(solution)/shard_map/ppermute | solution.py:350
  86.4 0.7 add.1
  87.1 1.9 %collective-permute-start.5 = (bf16[512,128]{1,0:T(8,128)(2,1)S(1)}, bf16[512,128]{1,0:T(8,128)(2,1)S(1)}, u32[]{:S(2)}, u32[]{:S(2)}) collective-permute-start(bf16[512,128]{1,0:T(8,128)(2,1)S(1)} %get-tuple-element.33), channel_id=1, source_target_pairs={{0,504},{4,508},{8,0},{12,4},{16,8},{20,12},{24,16},{28,20},{32,24... | collective-permute-start | bytes 393224 | tf_op jit(solution)/shard_map/ppermute | solution.py:350
  89.0 4.7 %all-to-all-start.3 = ((bf16[64,4,128]{2,1,0:T(4,128)(2,1)}), bf16[64,4,128]{2,1,0:T(4,128)(2,1)S(1)}, u32[]{:S(2)}, u32[]{:S(2)}) async-start(bf16[64,4,128]{2,1,0:T(4,128)(2,1)} %bitcast.8), calls=%async_computation.3 | async-start | bytes 131072 | tf_op jit(solution)/shard_map/all_to_all | solution.py:374
  93.7 11.1 %all-to-all-done.3 = bf16[64,4,128]{2,1,0:T(4,128)(2,1)S(1)} async-done(((bf16[64,4,128]{2,1,0:T(4,128)(2,1)}), bf16[64,4,128]{2,1,0:T(4,128)(2,1)S(1)}, u32[]{:S(2)}, u32[]{:S(2)}) %all-to-all-start.3) | async-done | bytes 65568 | tf_op jit(solution)/shard_map/all_to_all | solution.py:374
  104.8 0.8 back.1
  105.6 26.7 %all_to_all.28 = bf16[128,3,4,128]{3,2,1,0:T(4,128)(2,1)S(1)} all-to-all(bf16[128,3,4,128]{3,2,1,0:T(4,128)(2,1)S(1)} %bitcast.15), channel_id=1, replica_groups=mesh['blk'=128,'rep'=4] {'blk'}, dimensions={0} | all-to-all | bytes 786432 | tf_op jit(solution)/shard_map/all_to_all | solution.py:374
  132.3 1.7 %last.1 = (bf16[512,128]{1,0:T(8,128)(2,1)}, f32[128,256]{1,0:T(8,128)}, f32[1,256]{1,0:T(1,128)}) custom-call(f32[8,1024]{1,0:T(8,128)S(1)} %get-tuple-element.26.key_ref, bf16[1536,128]{1,0:T(8,128)(2,1)S(1)} %bitcast.16), custom_call_target="tpu_custom_call" | custom-call | flops 100000000 | bytes 1000000 | tf_op jit(solution)/shard_map/last/pallas_call | solution.py:46
  (10 shorter events, 0.0 us)
Async XLA Ops:
  3.1 47.5 %copy-start = (bf16[4,4,128,128]{3,2,1,0:T(8,128)(2,1)S(1)}, bf16[4,4,128,128]{3,2,1,0:T(8,128)(2,1)}, u32[]{:S(2)}) copy-start(bf16[4,4,128,128]{3,2,1,0:T(8,128)(2,1)} %param.14) | copy-start | bytes 1572868
  37.5 9.9 %collective-permute-start = (bf16[512,128]{1,0:T(8,128)(2,1)S(1)}, bf16[512,128]{1,0:T(8,128)(2,1)S(1)}, u32[]{:S(2)}, u32[]{:S(2)}) collective-permute-start(bf16[512,128]{1,0:T(8,128)(2,1)S(1)} %place.1.refs_0_.src0), channel_id=1, source_target_pairs={{0,8},{4,12},{8,16},{12,20},{16,24},{20,28},{24,32},{28,36},{32,40... | collective-permute-start | bytes 393224 | tf_op jit(solution)/shard_map/ppermute | solution.py:350
  40.0 11.3 %collective-permute-start.1 = (bf16[512,128]{1,0:T(8,128)(2,1)S(1)}, bf16[512,128]{1,0:T(8,128)(2,1)S(1)}, u32[]{:S(2)}, u32[]{:S(2)}) collective-permute-start(bf16[512,128]{1,0:T(8,128)(2,1)S(1)} %place.1.refs_0_.src0), channel_id=1, source_target_pairs={{0,4},{4,16},{8,12},{12,24},{16,20},{20,32},{24,28},{28,40},{32,36... | collective-permute-start | bytes 393224 | tf_op jit(solution)/shard_map/ppermute | solution.py:350
  47.4 4.1 %collective-permute-start.2 = (bf16[512,128]{1,0:T(8,128)(2,1)S(1)}, bf16[512,128]{1,0:T(8,128)(2,1)S(1)}, u32[]{:S(2)}, u32[]{:S(2)}) collective-permute-start(bf16[512,128]{1,0:T(8,128)(2,1)S(1)} %collective-permute-done.two), channel_id=1, source_target_pairs={{0,4},{4,0},{8,12},{12,8},{16,20},{20,16},{24,28},{28,24},{32,36},... | collective-permute-start | bytes 393224 | tf_op jit(solution)/shard_map/ppermute | solution.py:350
  52.5 11.9 %copy-start.1 = (bf16[512,256]{1,0:T(8,128)(2,1)S(1)}, bf16[512,256]{1,0:T(8,128)(2,1)}, u32[]{:S(2)}) copy-start(bf16[512,256]{1,0:T(8,128)(2,1)} %out_grad_ref.1) | copy-start | bytes 786436
  52.6 11.9 %copy-start.2 = (bf16[128,256]{1,0:T(8,128)(2,1)S(1)}, bf16[128,256]{1,0:T(8,128)(2,1)}, u32[]{:S(2)}) copy-start(bf16[128,256]{1,0:T(8,128)(2,1)} %weight_ref.1) | copy-start | bytes 196612
  79.1 7.3 %collective-permute-start.4 = (bf16[768,128]{1,0:T(8,128)(2,1)S(1)}, bf16[768,128]{1,0:T(8,128)(2,1)S(1)}, u32[]{:S(2)}, u32[]{:S(2)}) collective-permute-start(bf16[768,128]{1,0:T(8,128)(2,1)S(1)} %get-tuple-element.32), channel_id=1, source_target_pairs={{0,4},{4,0},{8,12},{12,8},{16,20},{20,16},{24,28},{28,24},{32,36},... | collective-permute-start | bytes 589832 | tf_op jit(solution)/shard_map/ppermute | solution.py:350
  84.5 9.2 %collective-permute-start.3 = (bf16[512,128]{1,0:T(8,128)(2,1)S(1)}, bf16[512,128]{1,0:T(8,128)(2,1)S(1)}, u32[]{:S(2)}, u32[]{:S(2)}) collective-permute-start(bf16[512,128]{1,0:T(8,128)(2,1)S(1)} %get-tuple-element.29), channel_id=1, source_target_pairs={{0,500},{4,0},{8,508},{12,8},{16,4},{20,16},{24,12},{28,24},{32,20... | collective-permute-start | bytes 393224 | tf_op jit(solution)/shard_map/ppermute | solution.py:350
  87.1 17.7 %collective-permute-start.5 = (bf16[512,128]{1,0:T(8,128)(2,1)S(1)}, bf16[512,128]{1,0:T(8,128)(2,1)S(1)}, u32[]{:S(2)}, u32[]{:S(2)}) collective-permute-start(bf16[512,128]{1,0:T(8,128)(2,1)S(1)} %get-tuple-element.33), channel_id=1, source_target_pairs={{0,504},{4,508},{8,0},{12,4},{16,8},{20,12},{24,16},{28,20},{32,24... | collective-permute-start | bytes 393224 | tf_op jit(solution)/shard_map/ppermute | solution.py:350
  89.0 15.8 %all-to-all-start.3 = ((bf16[64,4,128]{2,1,0:T(4,128)(2,1)}), bf16[64,4,128]{2,1,0:T(4,128)(2,1)S(1)}, u32[]{:S(2)}, u32[]{:S(2)}) async-start(bf16[64,4,128]{2,1,0:T(4,128)(2,1)} %bitcast.8), calls=%async_computation.3 | async-start | bytes 131072 | tf_op jit(solution)/shard_map/all_to_all | solution.py:374

commit v5 on v3

--- a/solution.py
+++ b/solution.py
@@ -281,6 +281,12 @@
     apart_ref[...] = acc_ref[3 - 2 * odd].astype(BF16)
 
 
+def row_kernel(parts_ref, out_ref):
+    count, width = parts_ref.shape
+    pairs = jnp.sum(parts_ref[...].astype(F32).reshape(count // 8, 8, width), axis=0)
+    out_ref[...] = jnp.concatenate([pairs[:4] + pairs[4:], jnp.zeros((4, width), F32)], axis=0)
+
+
 def add_kernel(a_ref, b_ref, out_ref):
     out_ref[...] = (a_ref[...] + b_ref[...].astype(F32)).astype(BF16)
 
@@ -295,10 +301,8 @@
     total = own_ref[...] + in1[...].astype(F32) + in2[...].astype(F32)
     grads = scaled_rows(degree_ref, total).astype(BF16)
     slots = dot(unplace_ref[...], grads).astype(BF16)
-    count, width = terms_ref.shape
-    pairs = jnp.sum(terms_ref[...].astype(F32).reshape(count // 8, 8, width), axis=0)
-    term = jnp.concatenate([pairs[:4] + pairs[4:], jnp.zeros((TILE - 4, width), F32)], axis=0)
-    term = term.astype(BF16)
+    empty = jnp.zeros((TILE - 8, terms_ref.shape[1]), F32)
+    term = jnp.concatenate([terms_ref[...], empty], axis=0).astype(BF16)
     lines = (TILE // 8 * 12, TILE)
     owner, slot = slot_of(lines, 0)
     widen = one_hot((slot < 8) & (owner * 8 + slot == iota(lines, 1)))
@@ -444,6 +448,7 @@
     near = moved(near, other_core)
     apart = moved(apart, apart_back)
     two = moved(call(add_kernel, shape((rows, width), BF16), "add")(two, near), two_back)
+    terms = call(row_kernel, shape((8, TILE), F32), "row", flops=LONG)(terms)
     back = call(back_kernel, shape((blocks * (slots + 4), width), BF16), "back")(
         own, apart, two, scale, unplace, terms
     )

time: 136 us -> 137 us (level)
    all_to_all x1, starting transfers between devices: 5.31 us -> 8.6 us  [exchange(): return lax.all_to_all(value, axis, split_axis=0, concat_axis=0, tiled=True)]
    ppermute x6, starting transfers between devices: 23.5 us -> 20.3 us  [moved(): lax.ppermute(value, 'blk', [(s, target(s) % count) for s in range(count)])]
    ppermute x6, waiting for transfers between devices: 5.62 us -> 8.76 us  [moved(): lax.ppermute(value, 'blk', [(s, target(s) % count) for s in range(count)])]
    all_to_all x1, waiting for transfers between devices: 3.01 us -> 0.01 us  [exchange(): return lax.all_to_all(value, axis, split_axis=0, concat_axis=0, tiled=True)]
    pallas_call x8 -> x9, Pallas kernels: 6.21 us -> 6.29 us  [run(): kernel_call(kernel, outs, specs, name, scratch, flops)(*arrays, *after)]
where the time goes in v5:
time: 137 us; the launch traced here: 136 us
  blocking collectives  86.8 us (63%)
  starting transfers between devices  28.9 us (21%)
  Pallas kernels  10.8 us (8%)
  waiting for transfers between devices  8.76 us (6%)
    all_to_all x4, blocking collectives, exchange(): return lax.all_to_all(value, axis, split_axis=0, concat_axis=0, tiled=True)  86.8 us
    ppermute x6, starting transfers between devices, moved(): lax.ppermute(value, 'blk', [(s, target(s) % count) for s in range(count)])  20.3 us
    ppermute x6, waiting for transfers between devices, moved(): lax.ppermute(value, 'blk', [(s, target(s) % count) for s in range(count)])  8.76 us
    all_to_all x1, starting transfers between devices, exchange(): return lax.all_to_all(value, axis, split_axis=0, concat_axis=0, tiled=True)  8.6 us
    pallas_call x9, Pallas kernels, run(): kernel_call(kernel, outs, specs, name, scratch, flops)(*arrays, *after)  6.29 us
  transfers between devices with their start and end apart: 7, of which 4 were waited for; matrix products, arithmetic and copies ran while one was open for 0% of the time, Pallas kernels for 1%

profile of v5, /device:TPU:1, one launch (start us, length us, event | category | flops | bytes accessed | tf_op | source)
XLA Modules:
  0.0 136.1 jit_solution(11994453733316163471)
XLA Ops:
  0.6 2.4 %start.1 = (bf16[1024,128]{1,0:T(8,128)(2,1)S(1)}, f32[4,128]{1,0:T(4,128)S(1)}, f32[1,256]{1,0:T(1,128)S(1)}, s32[10,4]{1,0:T(8,128)S(1)}, f32[8,1024]{1,0:T(8,128)S(1)}) custom-call(bf16[512,128]{1,0:T(8,128)(2,1)} %refs_0_.1, s32[8,128]{1,0:T(8,128)} %bitcast.21, s32[1,128]{1,0:T(1,128)} %bitcast.25, f32[4,128]{1,0:T(4,128)} %bitcast.22, s32[4,4]{1,0:T(4,128)} %refs_4_.1, ...), custom_call_target="tpu_custom_call" | custom-call | flops 100000000 | bytes 1000000 | tf_op jit(solution)/shard_map/start/pallas_call | solution.py:115
  3.1 33.6 %all_to_all.25 = bf16[128,8,128]{2,1,0:T(8,128)(2,1)S(1)} all-to-all(bf16[128,8,128]{2,1,0:T(8,128)(2,1)S(1)} %bitcast.19), channel_id=1, replica_groups=mesh['blk'=128,'rep'=4] {'blk'}, dimensions={0} | all-to-all | bytes 524288 | tf_op jit(solution)/shard_map/all_to_all | solution.py:368
  36.7 0.8 place.1.refs_0_.src0
  37.5 2.5 %collective-permute-start = (bf16[512,128]{1,0:T(8,128)(2,1)S(1)}, bf16[512,128]{1,0:T(8,128)(2,1)S(1)}, u32[]{:S(2)}, u32[]{:S(2)}) collective-permute-start(bf16[512,128]{1,0:T(8,128)(2,1)S(1)} %place.1.refs_0_.src0), channel_id=1, source_target_pairs={{0,8},{4,12},{8,16},{12,20},{16,24},{20,28},{24,32},{28,36},{32,40... | collective-permute-start | bytes 393224 | tf_op jit(solution)/shard_map/ppermute | solution.py:344
  40.0 3.0 %collective-permute-start.1 = (bf16[512,128]{1,0:T(8,128)(2,1)S(1)}, bf16[512,128]{1,0:T(8,128)(2,1)S(1)}, u32[]{:S(2)}, u32[]{:S(2)}) collective-permute-start(bf16[512,128]{1,0:T(8,128)(2,1)S(1)} %place.1.refs_0_.src0), channel_id=1, source_target_pairs={{0,4},{4,16},{8,12},{12,24},{16,20},{20,32},{24,28},{28,40},{32,36... | collective-permute-start | bytes 393224 | tf_op jit(solution)/shard_map/ppermute | solution.py:344
  43.0 4.5 %collective-permute-done.two = bf16[512,128]{1,0:T(8,128)(2,1)S(1)} collective-permute-done((bf16[512,128]{1,0:T(8,128)(2,1)S(1)}, bf16[512,128]{1,0:T(8,128)(2,1)S(1)}, u32[]{:S(2)}, u32[]{:S(2)}) %collective-permute-start) | collective-permute-done | bytes 131104 | tf_op jit(solution)/shard_map/ppermute | solution.py:344
  47.4 3.1 %collective-permute-start.2 = (bf16[512,128]{1,0:T(8,128)(2,1)S(1)}, bf16[512,128]{1,0:T(8,128)(2,1)S(1)}, u32[]{:S(2)}, u32[]{:S(2)}) collective-permute-start(bf16[512,128]{1,0:T(8,128)(2,1)S(1)} %collective-permute-done.two), channel_id=1, source_target_pairs={{0,4},{4,0},{8,12},{12,8},{16,20},{20,16},{24,28},{28,24},{32,36},... | collective-permute-start | bytes 393224 | tf_op jit(solution)/shard_map/ppermute | solution.py:344
  50.8 0.5 unplace.1.refs_1_.unplace_ref
  51.3 0.2 collective-permute-done.2.near
  51.5 1.0 gather_tiles.1
  52.6 11.9 %all_to_all.26.parts_ref = bf16[4,512,128]{2,1,0:T(8,128)(2,1)S(1)} all-to-all(bf16[4,512,128]{2,1,0:T(8,128)(2,1)S(1)} %gather_tiles.1), channel_id=1, replica_groups=mesh['blk'=128,'rep'=4] {'rep'}, dimensions={0} | all-to-all | bytes 1048576 | tf_op jit(solution)/shard_map/all_to_all | solution.py:368
  64.4 1.2 dense.1
  65.6 12.3 %all_to_all.27.block_ref = bf16[4,784,128]{2,1,0:T(8,128)(2,1)S(1)} all-to-all(bf16[4,784,128]{2,1,0:T(8,128)(2,1)S(1)} %get-tuple-element.24), channel_id=1, replica_groups=mesh['blk'=128,'rep'=4] {'rep'}, dimensions={0} | all-to-all | bytes 1605632 | tf_op jit(solution)/shard_map/all_to_all | solution.py:368
  77.9 1.0 terms.1.refs_0_
  78.9 8.6 %all-to-all-start.3 = ((bf16[128,4,128]{2,1,0:T(4,128)(2,1)}), bf16[128,4,128]{2,1,0:T(4,128)(2,1)S(1)}, u32[]{:S(2)}, u32[]{:S(2)}) async-start(bf16[128,4,128]{2,1,0:T(4,128)(2,1)} %bitcast.8), calls=%async_computation.3 | async-start | bytes 262144 | tf_op jit(solution)/shard_map/all_to_all | solution.py:368
  87.6 1.1 spread_tiles.1
  88.6 2.9 %collective-permute-start.4 = (bf16[512,128]{1,0:T(8,128)(2,1)S(1)}, bf16[512,128]{1,0:T(8,128)(2,1)S(1)}, u32[]{:S(2)}, u32[]{:S(2)}) collective-permute-start(bf16[512,128]{1,0:T(8,128)(2,1)S(1)} %get-tuple-element.28), channel_id=1, source_target_pairs={{0,4},{4,0},{8,12},{12,8},{16,20},{20,16},{24,28},{28,24},{32,36},... | collective-permute-start | bytes 393224 | tf_op jit(solution)/shard_map/ppermute | solution.py:344
  91.5 1.9 %collective-permute-start.3 = (bf16[512,128]{1,0:T(8,128)(2,1)S(1)}, bf16[512,128]{1,0:T(8,128)(2,1)S(1)}, u32[]{:S(2)}, u32[]{:S(2)}) collective-permute-start(bf16[512,128]{1,0:T(8,128)(2,1)S(1)} %get-tuple-element.26), channel_id=1, source_target_pairs={{0,500},{4,0},{8,508},{12,8},{16,4},{20,16},{24,12},{28,24},{32,20... | collective-permute-start | bytes 393224 | tf_op jit(solution)/shard_map/ppermute | solution.py:344
  93.5 7.0 %collective-permute-start.5 = (bf16[512,128]{1,0:T(8,128)(2,1)S(1)}, bf16[512,128]{1,0:T(8,128)(2,1)S(1)}, u32[]{:S(2)}, u32[]{:S(2)}) collective-permute-start(bf16[512,128]{1,0:T(8,128)(2,1)S(1)} %add.1), channel_id=1, source_target_pairs={{0,504},{4,508},{8,0},{12,4},{16,8},{20,12},{24,16},{28,20},{32,24... | collective-permute-start | bytes 393224 | tf_op jit(solution)/shard_map/ppermute | solution.py:344
  100.6 0.4 collective-permute-done.3.in1
  101.0 3.7 %collective-permute-done.5.in2 = bf16[512,128]{1,0:T(8,128)(2,1)S(1)} collective-permute-done((bf16[512,128]{1,0:T(8,128)(2,1)S(1)}, bf16[512,128]{1,0:T(8,128)(2,1)S(1)}, u32[]{:S(2)}, u32[]{:S(2)}) %collective-permute-start.5) | collective-permute-done | bytes 131104 | tf_op jit(solution)/shard_map/ppermute | solution.py:344
  104.6 0.8 back.1
  105.4 29.0 %all_to_all.28 = bf16[128,3,4,128]{3,2,1,0:T(4,128)(2,1)S(1)} all-to-all(bf16[128,3,4,128]{3,2,1,0:T(4,128)(2,1)S(1)} %bitcast.16), channel_id=1, replica_groups=mesh['blk'=128,'rep'=4] {'blk'}, dimensions={0} | all-to-all | bytes 786432 | tf_op jit(solution)/shard_map/all_to_all | solution.py:368
  134.4 1.7 %last.1 = (bf16[512,128]{1,0:T(8,128)(2,1)}, f32[128,256]{1,0:T(8,128)}, f32[1,256]{1,0:T(1,128)}) custom-call(f32[8,1024]{1,0:T(8,128)S(1)} %get-tuple-element.23.key_ref, bf16[1536,128]{1,0:T(8,128)(2,1)S(1)} %bitcast.15), custom_call_target="tpu_custom_call" | custom-call | flops 100000000 | bytes 1000000 | tf_op jit(solution)/shard_map/last/pallas_call | solution.py:46
  (12 shorter events, 0.3 us)
Async XLA Ops:
  3.1 47.5 %copy-start = (bf16[4,4,128,128]{3,2,1,0:T(8,128)(2,1)S(1)}, bf16[4,4,128,128]{3,2,1,0:T(8,128)(2,1)}, u32[]{:S(2)}) copy-start(bf16[4,4,128,128]{3,2,1,0:T(8,128)(2,1)} %param.14) | copy-start | bytes 1572868
  37.5 9.9 %collective-permute-start = (bf16[512,128]{1,0:T(8,128)(2,1)S(1)}, bf16[512,128]{1,0:T(8,128)(2,1)S(1)}, u32[]{:S(2)}, u32[]{:S(2)}) collective-permute-start(bf16[512,128]{1,0:T(8,128)(2,1)S(1)} %place.1.refs_0_.src0), channel_id=1, source_target_pairs={{0,8},{4,12},{8,16},{12,20},{16,24},{20,28},{24,32},{28,36},{32,40... | collective-permute-start | bytes 393224 | tf_op jit(solution)/shard_map/ppermute | solution.py:344
  40.0 11.3 %collective-permute-start.1 = (bf16[512,128]{1,0:T(8,128)(2,1)S(1)}, bf16[512,128]{1,0:T(8,128)(2,1)S(1)}, u32[]{:S(2)}, u32[]{:S(2)}) collective-permute-start(bf16[512,128]{1,0:T(8,128)(2,1)S(1)} %place.1.refs_0_.src0), channel_id=1, source_target_pairs={{0,4},{4,16},{8,12},{12,24},{16,20},{20,32},{24,28},{28,40},{32,36... | collective-permute-start | bytes 393224 | tf_op jit(solution)/shard_map/ppermute | solution.py:344
  47.4 4.1 %collective-permute-start.2 = (bf16[512,128]{1,0:T(8,128)(2,1)S(1)}, bf16[512,128]{1,0:T(8,128)(2,1)S(1)}, u32[]{:S(2)}, u32[]{:S(2)}) collective-permute-start(bf16[512,128]{1,0:T(8,128)(2,1)S(1)} %collective-permute-done.two), channel_id=1, source_target_pairs={{0,4},{4,0},{8,12},{12,8},{16,20},{20,16},{24,28},{28,24},{32,36},... | collective-permute-start | bytes 393224 | tf_op jit(solution)/shard_map/ppermute | solution.py:344
  52.5 11.9 %copy-start.1 = (bf16[512,256]{1,0:T(8,128)(2,1)S(1)}, bf16[512,256]{1,0:T(8,128)(2,1)}, u32[]{:S(2)}) copy-start(bf16[512,256]{1,0:T(8,128)(2,1)} %out_grad_ref.1) | copy-start | bytes 786436
  52.6 11.9 %copy-start.2 = (bf16[128,256]{1,0:T(8,128)(2,1)S(1)}, bf16[128,256]{1,0:T(8,128)(2,1)}, u32[]{:S(2)}) copy-start(bf16[128,256]{1,0:T(8,128)(2,1)} %weight_ref.1) | copy-start | bytes 196612
  78.9 21.5 %all-to-all-start.3 = ((bf16[128,4,128]{2,1,0:T(4,128)(2,1)}), bf16[128,4,128]{2,1,0:T(4,128)(2,1)S(1)}, u32[]{:S(2)}, u32[]{:S(2)}) async-start(bf16[128,4,128]{2,1,0:T(4,128)(2,1)} %bitcast.8), calls=%async_computation.3 | async-start | bytes 262144 | tf_op jit(solution)/shard_map/all_to_all | solution.py:368
  88.6 4.8 %collective-permute-start.4 = (bf16[512,128]{1,0:T(8,128)(2,1)S(1)}, bf16[512,128]{1,0:T(8,128)(2,1)S(1)}, u32[]{:S(2)}, u32[]{:S(2)}) collective-permute-start(bf16[512,128]{1,0:T(8,128)(2,1)S(1)} %get-tuple-element.28), channel_id=1, source_target_pairs={{0,4},{4,0},{8,12},{12,8},{16,20},{20,16},{24,28},{28,24},{32,36},... | collective-permute-start | bytes 393224 | tf_op jit(solution)/shard_map/ppermute | solution.py:344
  91.5 9.4 %collective-permute-start.3 = (bf16[512,128]{1,0:T(8,128)(2,1)S(1)}, bf16[512,128]{1,0:T(8,128)(2,1)S(1)}, u32[]{:S(2)}, u32[]{:S(2)}) collective-permute-start(bf16[512,128]{1,0:T(8,128)(2,1)S(1)} %get-tuple-element.26), channel_id=1, source_target_pairs={{0,500},{4,0},{8,508},{12,8},{16,4},{20,16},{24,12},{28,24},{32,20... | collective-permute-start | bytes 393224 | tf_op jit(solution)/shard_map/ppermute | solution.py:344
  93.5 11.1 %collective-permute-start.5 = (bf16[512,128]{1,0:T(8,128)(2,1)S(1)}, bf16[512,128]{1,0:T(8,128)(2,1)S(1)}, u32[]{:S(2)}, u32[]{:S(2)}) collective-permute-start(bf16[512,128]{1,0:T(8,128)(2,1)S(1)} %add.1), channel_id=1, source_target_pairs={{0,504},{4,508},{8,0},{12,4},{16,8},{20,12},{24,16},{28,20},{32,24... | collective-permute-start | bytes 393224 | tf_op jit(solution)/shard_map/ppermute | solution.py:344

commit v6 on v4

--- a/solution.py
+++ b/solution.py
@@ -82,10 +82,11 @@
     features_ref, rows_ref, counts_ref, *parts, sems = refs[13:]
     pairs = tuple(zip(refs[:8], (features_ref, rows_ref, counts_ref, degree_ref, *parts, bias_ref)))
     copies = [pltpu.make_async_copy(a, b, sems.at[k]) for k, (a, b) in enumerate(pairs)]
-    for copy in copies:
+    for copy in copies[1:]:
         copy.start()
-    for copy in copies:
-        copy.wait()
+    copies[0].start()
+    copies[1].wait()
+    copies[2].wait()
     rows = features_ref.shape[0]
     slots = rows_ref.shape[0]
     high, low = slot_parts(rows_ref[...], counts_ref[...], rows)
@@ -95,10 +96,13 @@
     pick = jnp.concatenate(
         [one_hot(key == lane + float(start)) for start in range(0, rows, TILE)], axis=1
     )
+    copies[0].wait()
     sent = dot(pick, features_ref[...])
     out_ref[...] = jnp.where(key >= float(rows), UNUSED, sent).astype(BF16)
     ones = jnp.ones((8, slots), BF16)
     key_ref[...] = dot(ones, high, NT) + dot(ones, low, NT)
+    for copy in copies[3:]:
+        copy.wait()
     place = 0
     for part in parts:
         table_ref[place : place + part.shape[0]] = part[...]
@@ -286,6 +290,12 @@
     apart_ref[...] = acc_ref[3 - 2 * odd].astype(BF16)
 
 
+def row_kernel(parts_ref, out_ref):
+    count, width = parts_ref.shape
+    pairs = jnp.sum(parts_ref[...].astype(F32).reshape(count // 8, 8, width), axis=0)
+    out_ref[...] = jnp.concatenate([pairs[:4] + pairs[4:], jnp.zeros((4, width), F32)], axis=0)
+
+
 def add_kernel(two_ref, mine_ref, near_ref, out_ref, terms_ref):
     rows = out_ref.shape[0]
     out_ref[...] = (two_ref[...] + near_ref[:rows].astype(F32)).astype(BF16)
@@ -302,10 +312,8 @@
     total = own_ref[...] + in1[...].astype(F32) + in2[...].astype(F32)
     grads = scaled_rows(degree_ref, total).astype(BF16)
     slots = dot(unplace_ref[...], grads).astype(BF16)
-    count, width = terms_ref.shape
-    pairs = jnp.sum(terms_ref[...].astype(F32).reshape(count // 8, 8, width), axis=0)
-    term = jnp.concatenate([pairs[:4] + pairs[4:], jnp.zeros((TILE - 4, width), F32)], axis=0)
-    term = term.astype(BF16)
+    empty = jnp.zeros((TILE - 8, terms_ref.shape[1]), F32)
+    term = jnp.concatenate([terms_ref[...], empty], axis=0).astype(BF16)
     lines = (TILE // 8 * 12, TILE)
     owner, slot = slot_of(lines, 0)
     widen = one_hot((slot < 8) & (owner * 8 + slot == iota(lines, 1)))
@@ -462,6 +470,7 @@
     two = moved(two, two_back)
     cores = [list(range(core, blocks, 2)) for core in range(2)]
     terms = exchange(terms.reshape(blocks // 2, 4, width), "blk", cores).reshape(terms.shape)
+    terms = call(row_kernel, shape((8, TILE), F32), "row", flops=LONG)(terms)
     back = call(back_kernel, shape((blocks * (slots + 4), width), BF16), "back")(
         own, apart, two, scale, unplace, terms
     )

time: 134 us -> 136 us (1.015)
  waiting for transfers between devices: 15.8 us -> 9.54 us
  starting transfers between devices: 22.4 us -> 27.6 us
  blocking collectives: 84.5 us -> 86.9 us
    all_to_all x1, waiting for transfers between devices: 11.1 us -> 1.96 us  [exchange(): lax.all_to_all(value, axis, split_axis=0, concat_axis=0, axis_index_group...]
    ppermute x6, starting transfers between devices: 17.7 us -> 23 us  [moved(): lax.ppermute(value, 'blk', [(s, target(s) % count) for s in range(count)])]
    ppermute x6, waiting for transfers between devices: 4.69 us -> 7.59 us  [moved(): lax.ppermute(value, 'blk', [(s, target(s) % count) for s in range(count)])]
    all_to_all x4, blocking collectives: 84.5 us -> 86.9 us  [exchange(): lax.all_to_all(value, axis, split_axis=0, concat_axis=0, axis_index_group...]
    pallas_call x7 -> x8, Pallas kernels: 5.87 us -> 5.91 us  [run(): kernel_call(kernel, outs, specs, name, scratch, flops)(*arrays, *after)]
  transfers between devices with their start and end apart: 7 -> 7, of which waited for: 3 -> 5; matrix products, arithmetic and copies ran while one was open for 0% -> 0% of each run, Pallas kernels for 1% -> 1%
where the time goes in v6:
time: 136 us; the launch traced here: 135 us
  blocking collectives  86.9 us (64%)
  starting transfers between devices  27.6 us (20%)
  Pallas kernels  10.5 us (8%)
  waiting for transfers between devices  9.54 us (7%)
    all_to_all x4, blocking collectives, exchange(): lax.all_to_all(value, axis, split_axis=0, concat_axis=0, axis_index_group...  86.9 us
    ppermute x6, starting transfers between devices, moved(): lax.ppermute(value, 'blk', [(s, target(s) % count) for s in range(count)])  23 us
    ppermute x6, waiting for transfers between devices, moved(): lax.ppermute(value, 'blk', [(s, target(s) % count) for s in range(count)])  7.59 us
    pallas_call x8, Pallas kernels, run(): kernel_call(kernel, outs, specs, name, scratch, flops)(*arrays, *after)  5.91 us
    all_to_all x1, starting transfers between devices, exchange(): lax.all_to_all(value, axis, split_axis=0, concat_axis=0, axis_index_group...  4.62 us
  transfers between devices with their start and end apart: 7, of which 5 were waited for; matrix products, arithmetic and copies ran while one was open for 0% of the time, Pallas kernels for 1%

profile of v6, /device:TPU:1, one launch (start us, length us, event | category | flops | bytes accessed | tf_op | source)
XLA Modules:
  0.0 135.4 jit_solution(9410334347822754563)
XLA Ops:
  0.6 2.4 %start.1 = (bf16[1024,128]{1,0:T(8,128)(2,1)S(1)}, f32[4,128]{1,0:T(4,128)S(1)}, f32[1,256]{1,0:T(1,128)S(1)}, s32[10,4]{1,0:T(8,128)S(1)}, f32[8,1024]{1,0:T(8,128)S(1)}) custom-call(bf16[512,128]{1,0:T(8,128)(2,1)} %refs_0_.1, s32[8,128]{1,0:T(8,128)} %bitcast.21, s32[1,128]{1,0:T(1,128)} %bitcast.25, f32[4,128]{1,0:T(4,128)} %bitcast.22, s32[4,4]{1,0:T(4,128)} %refs_4_.1, ...), custom_call_target="tpu_custom_call" | custom-call | flops 100000000 | bytes 1000000 | tf_op jit(solution)/shard_map/start/pallas_call | solution.py:119
  3.1 33.6 %all_to_all.25 = bf16[128,8,128]{2,1,0:T(8,128)(2,1)S(1)} all-to-all(bf16[128,8,128]{2,1,0:T(8,128)(2,1)S(1)} %bitcast.19), channel_id=1, replica_groups=mesh['blk'=128,'rep'=4] {'blk'}, dimensions={0} | all-to-all | bytes 524288 | tf_op jit(solution)/shard_map/all_to_all | solution.py:382
  36.7 0.8 place.1.refs_0_.src0
  37.5 2.5 %collective-permute-start = (bf16[512,128]{1,0:T(8,128)(2,1)S(1)}, bf16[512,128]{1,0:T(8,128)(2,1)S(1)}, u32[]{:S(2)}, u32[]{:S(2)}) collective-permute-start(bf16[512,128]{1,0:T(8,128)(2,1)S(1)} %place.1.refs_0_.src0), channel_id=1, source_target_pairs={{0,8},{4,12},{8,16},{12,20},{16,24},{20,28},{24,32},{28,36},{32,40... | collective-permute-start | bytes 393224 | tf_op jit(solution)/shard_map/ppermute | solution.py:358
  40.0 3.0 %collective-permute-start.1 = (bf16[512,128]{1,0:T(8,128)(2,1)S(1)}, bf16[512,128]{1,0:T(8,128)(2,1)S(1)}, u32[]{:S(2)}, u32[]{:S(2)}) collective-permute-start(bf16[512,128]{1,0:T(8,128)(2,1)S(1)} %place.1.refs_0_.src0), channel_id=1, source_target_pairs={{0,4},{4,16},{8,12},{12,24},{16,20},{20,32},{24,28},{28,40},{32,36... | collective-permute-start | bytes 393224 | tf_op jit(solution)/shard_map/ppermute | solution.py:358
  43.0 4.5 %collective-permute-done.two = bf16[512,128]{1,0:T(8,128)(2,1)S(1)} collective-permute-done((bf16[512,128]{1,0:T(8,128)(2,1)S(1)}, bf16[512,128]{1,0:T(8,128)(2,1)S(1)}, u32[]{:S(2)}, u32[]{:S(2)}) %collective-permute-start) | collective-permute-done | bytes 131104 | tf_op jit(solution)/shard_map/ppermute | solution.py:358
  47.4 3.1 %collective-permute-start.2 = (bf16[512,128]{1,0:T(8,128)(2,1)S(1)}, bf16[512,128]{1,0:T(8,128)(2,1)S(1)}, u32[]{:S(2)}, u32[]{:S(2)}) collective-permute-start(bf16[512,128]{1,0:T(8,128)(2,1)S(1)} %collective-permute-done.two), channel_id=1, source_target_pairs={{0,4},{4,0},{8,12},{12,8},{16,20},{20,16},{24,28},{28,24},{32,36},... | collective-permute-start | bytes 393224 | tf_op jit(solution)/shard_map/ppermute | solution.py:358
  50.8 0.5 unplace.1.refs_1_.unplace_ref
  51.5 1.0 gather_tiles.1
  52.6 11.8 %all_to_all.26.parts_ref = bf16[4,512,128]{2,1,0:T(8,128)(2,1)S(1)} all-to-all(bf16[4,512,128]{2,1,0:T(8,128)(2,1)S(1)} %gather_tiles.1), channel_id=1, replica_groups=mesh['blk'=128,'rep'=4] {'rep'}, dimensions={0} | all-to-all | bytes 1048576 | tf_op jit(solution)/shard_map/all_to_all | solution.py:382
  64.4 1.2 dense.1
  65.6 12.3 %all_to_all.27.block_ref = bf16[4,784,128]{2,1,0:T(8,128)(2,1)S(1)} all-to-all(bf16[4,784,128]{2,1,0:T(8,128)(2,1)S(1)} %get-tuple-element.27), channel_id=1, replica_groups=mesh['blk'=128,'rep'=4] {'rep'}, dimensions={0} | all-to-all | bytes 1605632 | tf_op jit(solution)/shard_map/all_to_all | solution.py:382
  77.9 1.2 spread_tiles.1
  79.1 5.4 %collective-permute-start.4 = (bf16[768,128]{1,0:T(8,128)(2,1)S(1)}, bf16[768,128]{1,0:T(8,128)(2,1)S(1)}, u32[]{:S(2)}, u32[]{:S(2)}) collective-permute-start(bf16[768,128]{1,0:T(8,128)(2,1)S(1)} %get-tuple-element.32), channel_id=1, source_target_pairs={{0,4},{4,0},{8,12},{12,8},{16,20},{20,16},{24,28},{28,24},{32,36},... | collective-permute-start | bytes 589832 | tf_op jit(solution)/shard_map/ppermute | solution.py:358
  84.4 1.0 collective-permute-done.4.near_ref
  85.5 0.7 add.1
  86.1 4.6 %all-to-all-start.3 = ((bf16[64,4,128]{2,1,0:T(4,128)(2,1)}), bf16[64,4,128]{2,1,0:T(4,128)(2,1)S(1)}, u32[]{:S(2)}, u32[]{:S(2)}) async-start(bf16[64,4,128]{2,1,0:T(4,128)(2,1)} %bitcast.8), calls=%async_computation.3 | async-start | bytes 131072 | tf_op jit(solution)/shard_map/all_to_all | solution.py:382
  90.8 2.3 %collective-permute-start.3 = (bf16[512,128]{1,0:T(8,128)(2,1)S(1)}, bf16[512,128]{1,0:T(8,128)(2,1)S(1)}, u32[]{:S(2)}, u32[]{:S(2)}) collective-permute-start(bf16[512,128]{1,0:T(8,128)(2,1)S(1)} %get-tuple-element.29), channel_id=1, source_target_pairs={{0,500},{4,0},{8,508},{12,8},{16,4},{20,16},{24,12},{28,24},{32,20... | collective-permute-start | bytes 393224 | tf_op jit(solution)/shard_map/ppermute | solution.py:358
  93.1 6.8 %collective-permute-start.5 = (bf16[512,128]{1,0:T(8,128)(2,1)S(1)}, bf16[512,128]{1,0:T(8,128)(2,1)S(1)}, u32[]{:S(2)}, u32[]{:S(2)}) collective-permute-start(bf16[512,128]{1,0:T(8,128)(2,1)S(1)} %get-tuple-element.33), channel_id=1, source_target_pairs={{0,504},{4,508},{8,0},{12,4},{16,8},{20,12},{24,16},{28,20},{32,24... | collective-permute-start | bytes 393224 | tf_op jit(solution)/shard_map/ppermute | solution.py:358
  99.9 2.0 %all-to-all-done.3 = bf16[64,4,128]{2,1,0:T(4,128)(2,1)S(1)} async-done(((bf16[64,4,128]{2,1,0:T(4,128)(2,1)}), bf16[64,4,128]{2,1,0:T(4,128)(2,1)S(1)}, u32[]{:S(2)}, u32[]{:S(2)}) %all-to-all-start.3) | async-done | bytes 65568 | tf_op jit(solution)/shard_map/all_to_all | solution.py:382
  101.9 1.9 %collective-permute-done.5.in2 = bf16[512,128]{1,0:T(8,128)(2,1)S(1)} collective-permute-done((bf16[512,128]{1,0:T(8,128)(2,1)S(1)}, bf16[512,128]{1,0:T(8,128)(2,1)S(1)}, u32[]{:S(2)}, u32[]{:S(2)}) %collective-permute-start.5) | collective-permute-done | bytes 131104 | tf_op jit(solution)/shard_map/ppermute | solution.py:358
  103.8 0.8 back.1
  104.5 29.1 %all_to_all.28 = bf16[128,3,4,128]{3,2,1,0:T(4,128)(2,1)S(1)} all-to-all(bf16[128,3,4,128]{3,2,1,0:T(4,128)(2,1)S(1)} %bitcast.16), channel_id=1, replica_groups=mesh['blk'=128,'rep'=4] {'blk'}, dimensions={0} | all-to-all | bytes 786432 | tf_op jit(solution)/shard_map/all_to_all | solution.py:382
  133.7 1.7 %last.1 = (bf16[512,128]{1,0:T(8,128)(2,1)}, f32[128,256]{1,0:T(8,128)}, f32[1,256]{1,0:T(1,128)}) custom-call(f32[8,1024]{1,0:T(8,128)S(1)} %get-tuple-element.26.key_ref, bf16[1536,128]{1,0:T(8,128)(2,1)S(1)} %bitcast.15), custom_call_target="tpu_custom_call" | custom-call | flops 100000000 | bytes 1000000 | tf_op jit(solution)/shard_map/last/pallas_call | solution.py:46
  (11 shorter events, 0.5 us)
Async XLA Ops:
  3.1 47.5 %copy-start = (bf16[4,4,128,128]{3,2,1,0:T(8,128)(2,1)S(1)}, bf16[4,4,128,128]{3,2,1,0:T(8,128)(2,1)}, u32[]{:S(2)}) copy-start(bf16[4,4,128,128]{3,2,1,0:T(8,128)(2,1)} %param.14) | copy-start | bytes 1572868
  37.5 9.9 %collective-permute-start = (bf16[512,128]{1,0:T(8,128)(2,1)S(1)}, bf16[512,128]{1,0:T(8,128)(2,1)S(1)}, u32[]{:S(2)}, u32[]{:S(2)}) collective-permute-start(bf16[512,128]{1,0:T(8,128)(2,1)S(1)} %place.1.refs_0_.src0), channel_id=1, source_target_pairs={{0,8},{4,12},{8,16},{12,20},{16,24},{20,28},{24,32},{28,36},{32,40... | collective-permute-start | bytes 393224 | tf_op jit(solution)/shard_map/ppermute | solution.py:358
  40.0 11.3 %collective-permute-start.1 = (bf16[512,128]{1,0:T(8,128)(2,1)S(1)}, bf16[512,128]{1,0:T(8,128)(2,1)S(1)}, u32[]{:S(2)}, u32[]{:S(2)}) collective-permute-start(bf16[512,128]{1,0:T(8,128)(2,1)S(1)} %place.1.refs_0_.src0), channel_id=1, source_target_pairs={{0,4},{4,16},{8,12},{12,24},{16,20},{20,32},{24,28},{28,40},{32,36... | collective-permute-start | bytes 393224 | tf_op jit(solution)/shard_map/ppermute | solution.py:358
  47.4 4.1 %collective-permute-start.2 = (bf16[512,128]{1,0:T(8,128)(2,1)S(1)}, bf16[512,128]{1,0:T(8,128)(2,1)S(1)}, u32[]{:S(2)}, u32[]{:S(2)}) collective-permute-start(bf16[512,128]{1,0:T(8,128)(2,1)S(1)} %collective-permute-done.two), channel_id=1, source_target_pairs={{0,4},{4,0},{8,12},{12,8},{16,20},{20,16},{24,28},{28,24},{32,36},... | collective-permute-start | bytes 393224 | tf_op jit(solution)/shard_map/ppermute | solution.py:358
  52.5 11.9 %copy-start.1 = (bf16[512,256]{1,0:T(8,128)(2,1)S(1)}, bf16[512,256]{1,0:T(8,128)(2,1)}, u32[]{:S(2)}) copy-start(bf16[512,256]{1,0:T(8,128)(2,1)} %out_grad_ref.1) | copy-start | bytes 786436
  52.5 11.9 %copy-start.2 = (bf16[128,256]{1,0:T(8,128)(2,1)S(1)}, bf16[128,256]{1,0:T(8,128)(2,1)}, u32[]{:S(2)}) copy-start(bf16[128,256]{1,0:T(8,128)(2,1)} %weight_ref.1) | copy-start | bytes 196612
  79.1 6.4 %collective-permute-start.4 = (bf16[768,128]{1,0:T(8,128)(2,1)S(1)}, bf16[768,128]{1,0:T(8,128)(2,1)S(1)}, u32[]{:S(2)}, u32[]{:S(2)}) collective-permute-start(bf16[768,128]{1,0:T(8,128)(2,1)S(1)} %get-tuple-element.32), channel_id=1, source_target_pairs={{0,4},{4,0},{8,12},{12,8},{16,20},{20,16},{24,28},{28,24},{32,36},... | collective-permute-start | bytes 589832 | tf_op jit(solution)/shard_map/ppermute | solution.py:358
  86.1 15.7 %all-to-all-start.3 = ((bf16[64,4,128]{2,1,0:T(4,128)(2,1)}), bf16[64,4,128]{2,1,0:T(4,128)(2,1)S(1)}, u32[]{:S(2)}, u32[]{:S(2)}) async-start(bf16[64,4,128]{2,1,0:T(4,128)(2,1)} %bitcast.8), calls=%async_computation.3 | async-start | bytes 131072 | tf_op jit(solution)/shard_map/all_to_all | solution.py:382
  90.8 11.1 %collective-permute-start.3 = (bf16[512,128]{1,0:T(8,128)(2,1)S(1)}, bf16[512,128]{1,0:T(8,128)(2,1)S(1)}, u32[]{:S(2)}, u32[]{:S(2)}) collective-permute-start(bf16[512,128]{1,0:T(8,128)(2,1)S(1)} %get-tuple-element.29), channel_id=1, source_target_pairs={{0,500},{4,0},{8,508},{12,8},{16,4},{20,16},{24,12},{28,24},{32,20... | collective-permute-start | bytes 393224 | tf_op jit(solution)/shard_map/ppermute | solution.py:358
  93.1 10.7 %collective-permute-start.5 = (bf16[512,128]{1,0:T(8,128)(2,1)S(1)}, bf16[512,128]{1,0:T(8,128)(2,1)S(1)}, u32[]{:S(2)}, u32[]{:S(2)}) collective-permute-start(bf16[512,128]{1,0:T(8,128)(2,1)S(1)} %get-tuple-element.33), channel_id=1, source_target_pairs={{0,504},{4,508},{8,0},{12,4},{16,8},{20,12},{24,16},{28,20},{32,24... | collective-permute-start | bytes 393224 | tf_op jit(solution)/shard_map/ppermute | solution.py:358

commit v7 on v4

--- a/solution.py
+++ b/solution.py
@@ -69,23 +69,22 @@
     high = (key >> 5).astype(F32).astype(BF16)
     low = (key & 31).astype(F32).astype(BF16)
     total = owners * slots
-    expand = one_hot(quotient(iota((total, owners), 0), slots) == iota((total, owners), 1))
-    row = iota((total, slots), 0)
-    mine = row - quotient(row, slots) * slots == iota((total, slots), 1)
+    expand = one_hot(iota((total, owners), 0) // slots == iota((total, owners), 1))
+    mine = iota((total, slots), 0) % slots == iota((total, slots), 1)
     high = jnp.where(mine, dot(expand, high) * 32.0, 0.0).astype(BF16)
     low = jnp.where(mine, dot(expand, low), 0.0).astype(BF16)
     return high, low
 
 
 def start_kernel(*refs):
-    out_ref, degree_ref, bias_ref, table_ref, key_ref = refs[8:13]
-    features_ref, rows_ref, counts_ref, *parts, sems = refs[13:]
+    out_ref, degree_ref, bias_ref, table_ref, rows_ref, counts_ref = refs[8:14]
+    features_ref, *parts, sems = refs[14:]
     pairs = tuple(zip(refs[:8], (features_ref, rows_ref, counts_ref, degree_ref, *parts, bias_ref)))
     copies = [pltpu.make_async_copy(a, b, sems.at[k]) for k, (a, b) in enumerate(pairs)]
     for copy in copies:
         copy.start()
-    for copy in copies:
-        copy.wait()
+    copies[1].wait()
+    copies[2].wait()
     rows = features_ref.shape[0]
     slots = rows_ref.shape[0]
     high, low = slot_parts(rows_ref[...], counts_ref[...], rows)
@@ -95,10 +94,11 @@
     pick = jnp.concatenate(
         [one_hot(key == lane + float(start)) for start in range(0, rows, TILE)], axis=1
     )
+    copies[0].wait()
     sent = dot(pick, features_ref[...])
     out_ref[...] = jnp.where(key >= float(rows), UNUSED, sent).astype(BF16)
-    ones = jnp.ones((8, slots), BF16)
-    key_ref[...] = dot(ones, high, NT) + dot(ones, low, NT)
+    for copy in copies[3:]:
+        copy.wait()
     place = 0
     for part in parts:
         table_ref[place : place + part.shape[0]] = part[...]
@@ -119,15 +119,27 @@
             shape(degree.shape, F32),
             shape(bias_row.shape, F32),
             shape((1 + sum(a.shape[0] for a in tables), tables[0].shape[1]), jnp.int32),
-            shape((8, total), F32),
+            shape(send_rows.shape, jnp.int32),
+            shape(counts_row.shape, jnp.int32),
         ),
         in_specs=[pl.BlockSpec(memory_space=pltpu.HBM)] * 8,
-        scratch_shapes=[pltpu.VMEM(a.shape, a.dtype) for a in (features, send_rows, counts_row, *tables)]
+        scratch_shapes=[pltpu.VMEM(a.shape, a.dtype) for a in (features, *tables)]
         + [pltpu.SemaphoreType.DMA((8,))],
         compiler_params=pltpu.CompilerParams(vmem_limit_bytes=8 * 1024 * 1024),
         cost_estimate=pl.CostEstimate(flops=10**8, bytes_accessed=10**6, transcendentals=0),
         name="start",
     )(*arrays)
+
+
+def arrive_kernel(rows_ref, counts_ref, *refs):
+    out_ref = refs[-1]
+    rows = out_ref.shape[0]
+    high, low = slot_parts(rows_ref[...], counts_ref[...], rows)
+    ones = jnp.ones((8, rows_ref.shape[0]), BF16)
+    key = dot(ones, high, NT) + dot(ones, low, NT)
+    for start in range(0, key.shape[1], TILE):
+        span = slice(start, start + TILE)
+        out_ref[:, span] = one_hot(iota((rows, TILE), 0).astype(F32) == key[0:1, span])
 
 
 def transpose_kernel(tiles_ref, *refs):
@@ -298,7 +310,8 @@
     return owner, index - 12 * owner
 
 
-def back_kernel(own_ref, in1, in2, degree_ref, unplace_ref, terms_ref, out_ref):
+def back_kernel(own_ref, in1, in2, degree_ref, unplace_ref, terms_ref, *refs):
+    out_ref = refs[-1]
     total = own_ref[...] + in1[...].astype(F32) + in2[...].astype(F32)
     grads = scaled_rows(degree_ref, total).astype(BF16)
     slots = dot(unplace_ref[...], grads).astype(BF16)
@@ -315,7 +328,7 @@
         out_ref[t * lines[0] : (t + 1) * lines[0]] = group.astype(BF16)
 
 
-def last_kernel(key_ref, returned_ref, out_ref, weight_ref, bias_ref):
+def last_kernel(arrive_ref, returned_ref, out_ref, weight_ref, bias_ref):
     rows = out_ref.shape[0]
     owners = TILE // 8
     lines = (TILE + 3 * owners, 12 * owners)
@@ -331,8 +344,7 @@
     for t in range(returned_ref.shape[0] // lines[1]):
         found = dot(pick, returned_ref[t * lines[1] : (t + 1) * lines[1]])
         span = slice(t * TILE, (t + 1) * TILE)
-        here = one_hot(iota((rows, TILE), 0).astype(F32) == key_ref[0:1, span])
-        total = total + dot(here, found[:TILE].astype(BF16))
+        total = total + dot(arrive_ref[:, span], found[:TILE].astype(BF16))
         for k in range(2):
             for core in range(2):
                 start = TILE + (2 * k + core) * (owners // 2)
@@ -409,7 +421,7 @@
     tiles = tile_values.reshape(steps * most, TILE, TILE)
     tables = (tile_rows, tile_cols, tile_counts.reshape(1, steps))
 
-    outgoing, scale, bias_row, table, key = start_call(
+    outgoing, scale, bias_row, table, slot_rows, counts_row = start_call(
         features, slot_rows, counts_row, degree, tables, bias.reshape(1, hidden_width)
     )
     incoming = exchange(outgoing.reshape(blocks, slots, width), "blk").reshape(total, width)
@@ -459,18 +471,22 @@
     two, terms = call(
         add_kernel, (shape((rows, width), BF16), shape((2 * width, width), BF16)), "add"
     )(two, mine, near)
+    added = two
     two = moved(two, two_back)
     cores = [list(range(core, blocks, 2)) for core in range(2)]
     terms = exchange(terms.reshape(blocks // 2, 4, width), "blk", cores).reshape(terms.shape)
+    arrive = call(arrive_kernel, shape((rows, total), BF16), "arrive")(
+        slot_rows, counts_row, after=(added,)
+    )
     back = call(back_kernel, shape((blocks * (slots + 4), width), BF16), "back")(
-        own, apart, two, scale, unplace, terms
+        own, apart, two, scale, unplace, terms, after=(arrive,)
     )
     returned = exchange(back.reshape(blocks, 3, 4, width), "blk").reshape(back.shape)
     grad_features, grad_weight, grad_bias = call(
         last_kernel,
         (shape((rows, width), BF16), shape(weight.shape, F32), shape((1, hidden_width), F32)),
         "last",
-    )(key, returned)
+    )(arrive, returned)
     return (hidden, grad_features, grad_weight, grad_bias.reshape(hidden_width))
 
 

time: 134 us -> 134 us (level)
    pallas_call x7 -> x8, Pallas kernels: 5.87 us -> 6.81 us  [run(): kernel_call(kernel, outs, specs, name, scratch, flops)(*arrays, *after)]
  transfers between devices with their start and end apart: 7 -> 7, of which waited for: 3 -> 3; matrix products, arithmetic and copies ran while one was open for 0% -> 0% of each run, Pallas kernels for 1% -> 2%
where the time goes in v7:
time: 134 us
  blocking collectives  84.5 us (63%)
  starting transfers between devices  22.4 us (17%)
  waiting for transfers between devices  14.8 us (11%)
  Pallas kernels  11.2 us (8%)
    all_to_all x4, blocking collectives, exchange(): lax.all_to_all(value, axis, split_axis=0, concat_axis=0, axis_index_group...  84.5 us
    ppermute x6, starting transfers between devices, moved(): lax.ppermute(value, 'blk', [(s, target(s) % count) for s in range(count)])  17.7 us
    all_to_all x1, waiting for transfers between devices, exchange(): lax.all_to_all(value, axis, split_axis=0, concat_axis=0, axis_index_group...  10.1 us
    pallas_call x8, Pallas kernels, run(): kernel_call(kernel, outs, specs, name, scratch, flops)(*arrays, *after)  6.81 us
    all_to_all x1, starting transfers between devices, exchange(): lax.all_to_all(value, axis, split_axis=0, concat_axis=0, axis_index_group...  4.7 us
    ppermute x6, waiting for transfers between devices, moved(): lax.ppermute(value, 'blk', [(s, target(s) % count) for s in range(count)])  4.69 us
  transfers between devices with their start and end apart: 7, of which 3 were waited for; matrix products, arithmetic and copies ran while one was open for 0% of the time, Pallas kernels for 2%

profile of v7, /device:TPU:1, one launch (start us, length us, event | category | flops | bytes accessed | tf_op | source)
XLA Modules:
  0.0 133.8 jit_solution(15701649769985434516)
XLA Ops:
  0.6 2.2 %start.1 = (bf16[1024,128]{1,0:T(8,128)(2,1)S(1)}, f32[4,128]{1,0:T(4,128)S(1)}, f32[1,256]{1,0:T(1,128)S(1)}, s32[10,4]{1,0:T(8,128)S(1)}, s32[8,128]{1,0:T(8,128)S(1)}, /*index=5*/s32[1,128]{1,0:T(1,128)S(1)}) custom-call(bf16[512,128]{1,0:T(8,128)(2,1)} %refs_0_.1, s32[8,128]{1,0:T(8,128)} %bitcast.21, s32[1,128]{1,0:T(1,128)} %bitcast.25, ...), custom_call_target="tpu_custom_call" | custom-call | flops 100000000 | bytes 1000000 | tf_op jit(solution)/shard_map/start/pallas_call | solution.py:115
  2.9 33.6 %all_to_all.25 = bf16[128,8,128]{2,1,0:T(8,128)(2,1)S(1)} all-to-all(bf16[128,8,128]{2,1,0:T(8,128)(2,1)S(1)} %bitcast.19), channel_id=1, replica_groups=mesh['blk'=128,'rep'=4] {'blk'}, dimensions={0} | all-to-all | bytes 524288 | tf_op jit(solution)/shard_map/all_to_all | solution.py:386
  36.5 0.8 place.1.refs_0_.src0
  37.3 2.5 %collective-permute-start = (bf16[512,128]{1,0:T(8,128)(2,1)S(1)}, bf16[512,128]{1,0:T(8,128)(2,1)S(1)}, u32[]{:S(2)}, u32[]{:S(2)}) collective-permute-start(bf16[512,128]{1,0:T(8,128)(2,1)S(1)} %place.1.refs_0_.src0), channel_id=1, source_target_pairs={{0,8},{4,12},{8,16},{12,20},{16,24},{20,28},{24,32},{28,36},{32,40... | collective-permute-start | bytes 393224 | tf_op jit(solution)/shard_map/ppermute | solution.py:362
  39.8 3.0 %collective-permute-start.1 = (bf16[512,128]{1,0:T(8,128)(2,1)S(1)}, bf16[512,128]{1,0:T(8,128)(2,1)S(1)}, u32[]{:S(2)}, u32[]{:S(2)}) collective-permute-start(bf16[512,128]{1,0:T(8,128)(2,1)S(1)} %place.1.refs_0_.src0), channel_id=1, source_target_pairs={{0,4},{4,16},{8,12},{12,24},{16,20},{20,32},{24,28},{28,40},{32,36... | collective-permute-start | bytes 393224 | tf_op jit(solution)/shard_map/ppermute | solution.py:362
  42.8 4.5 %collective-permute-done.two = bf16[512,128]{1,0:T(8,128)(2,1)S(1)} collective-permute-done((bf16[512,128]{1,0:T(8,128)(2,1)S(1)}, bf16[512,128]{1,0:T(8,128)(2,1)S(1)}, u32[]{:S(2)}, u32[]{:S(2)}) %collective-permute-start) | collective-permute-done | bytes 131104 | tf_op jit(solution)/shard_map/ppermute | solution.py:362
  47.2 3.1 %collective-permute-start.2 = (bf16[512,128]{1,0:T(8,128)(2,1)S(1)}, bf16[512,128]{1,0:T(8,128)(2,1)S(1)}, u32[]{:S(2)}, u32[]{:S(2)}) collective-permute-start(bf16[512,128]{1,0:T(8,128)(2,1)S(1)} %collective-permute-done.two), channel_id=1, source_target_pairs={{0,4},{4,0},{8,12},{12,8},{16,20},{20,16},{24,28},{28,24},{32,36},... | collective-permute-start | bytes 393224 | tf_op jit(solution)/shard_map/ppermute | solution.py:362
  50.5 0.5 unplace.1.refs_1_.unplace_ref
  51.1 0.2 collective-permute-done.2.near
  51.3 1.0 gather_tiles.1
  52.3 11.9 %all_to_all.26.parts_ref = bf16[4,512,128]{2,1,0:T(8,128)(2,1)S(1)} all-to-all(bf16[4,512,128]{2,1,0:T(8,128)(2,1)S(1)} %gather_tiles.1), channel_id=1, replica_groups=mesh['blk'=128,'rep'=4] {'rep'}, dimensions={0} | all-to-all | bytes 1048576 | tf_op jit(solution)/shard_map/all_to_all | solution.py:386
  64.2 1.2 dense.1
  65.4 12.4 %all_to_all.27.block_ref = bf16[4,784,128]{2,1,0:T(8,128)(2,1)S(1)} all-to-all(bf16[4,784,128]{2,1,0:T(8,128)(2,1)S(1)} %get-tuple-element.29), channel_id=1, replica_groups=mesh['blk'=128,'rep'=4] {'rep'}, dimensions={0} | all-to-all | bytes 1605632 | tf_op jit(solution)/shard_map/all_to_all | solution.py:386
  77.7 1.2 spread_tiles.1
  78.9 5.3 %collective-permute-start.3 = (bf16[768,128]{1,0:T(8,128)(2,1)S(1)}, bf16[768,128]{1,0:T(8,128)(2,1)S(1)}, u32[]{:S(2)}, u32[]{:S(2)}) collective-permute-start(bf16[768,128]{1,0:T(8,128)(2,1)S(1)} %get-tuple-element.32), channel_id=1, source_target_pairs={{0,4},{4,0},{8,12},{12,8},{16,20},{20,16},{24,28},{28,24},{32,36},... | collective-permute-start | bytes 589832 | tf_op jit(solution)/shard_map/ppermute | solution.py:362
  84.2 1.9 %collective-permute-start.4 = (bf16[512,128]{1,0:T(8,128)(2,1)S(1)}, bf16[512,128]{1,0:T(8,128)(2,1)S(1)}, u32[]{:S(2)}, u32[]{:S(2)}) collective-permute-start(bf16[512,128]{1,0:T(8,128)(2,1)S(1)} %get-tuple-element.35), channel_id=1, source_target_pairs={{0,500},{4,0},{8,508},{12,8},{16,4},{20,16},{24,12},{28,24},{32,20... | collective-permute-start | bytes 393224 | tf_op jit(solution)/shard_map/ppermute | solution.py:362
  86.2 0.7 add.1
  86.9 1.9 %collective-permute-start.5 = (bf16[512,128]{1,0:T(8,128)(2,1)S(1)}, bf16[512,128]{1,0:T(8,128)(2,1)S(1)}, u32[]{:S(2)}, u32[]{:S(2)}) collective-permute-start(bf16[512,128]{1,0:T(8,128)(2,1)S(1)} %get-tuple-element.33.refs_0_), channel_id=1, source_target_pairs={{0,504},{4,508},{8,0},{12,4},{16,8},{20,12},{24,16},{28,20},{32,24... | collective-permute-start | bytes 393224 | tf_op jit(solution)/shard_map/ppermute | solution.py:362
  88.8 4.7 %all-to-all-start.3 = ((bf16[64,4,128]{2,1,0:T(4,128)(2,1)}), bf16[64,4,128]{2,1,0:T(4,128)(2,1)S(1)}, u32[]{:S(2)}, u32[]{:S(2)}) async-start(bf16[64,4,128]{2,1,0:T(4,128)(2,1)} %bitcast.8), calls=%async_computation.3 | async-start | bytes 131072 | tf_op jit(solution)/shard_map/all_to_all | solution.py:386
  93.5 0.9 arrive.1.refs_0_.arrive_ref
  94.4 10.1 %all-to-all-done.3 = bf16[64,4,128]{2,1,0:T(4,128)(2,1)S(1)} async-done(((bf16[64,4,128]{2,1,0:T(4,128)(2,1)}), bf16[64,4,128]{2,1,0:T(4,128)(2,1)S(1)}, u32[]{:S(2)}, u32[]{:S(2)}) %all-to-all-start.3) | async-done | bytes 65568 | tf_op jit(solution)/shard_map/all_to_all | solution.py:386
  104.6 0.8 back.1
  105.4 26.7 %all_to_all.28 = bf16[128,3,4,128]{3,2,1,0:T(4,128)(2,1)S(1)} all-to-all(bf16[128,3,4,128]{3,2,1,0:T(4,128)(2,1)S(1)} %bitcast.16), channel_id=1, replica_groups=mesh['blk'=128,'rep'=4] {'blk'}, dimensions={0} | all-to-all | bytes 786432 | tf_op jit(solution)/shard_map/all_to_all | solution.py:386
  132.0 1.7 %last.1 = (bf16[512,128]{1,0:T(8,128)(2,1)}, f32[128,256]{1,0:T(8,128)}, f32[1,256]{1,0:T(1,128)}) custom-call(bf16[512,1024]{1,0:T(8,128)(2,1)S(1)} %arrive.1.refs_0_.arrive_ref, bf16[1536,128]{1,0:T(8,128)(2,1)S(1)} %bitcast.15), custom_call_target="tpu_custom_call" | custom-call | flops 100000000 | bytes 1000000 | tf_op jit(solution)/shard_map/last/pallas_call | solution.py:46
  (11 shorter events, 0.2 us)
Async XLA Ops:
  2.9 47.5 %copy-start = (bf16[4,4,128,128]{3,2,1,0:T(8,128)(2,1)S(1)}, bf16[4,4,128,128]{3,2,1,0:T(8,128)(2,1)}, u32[]{:S(2)}) copy-start(bf16[4,4,128,128]{3,2,1,0:T(8,128)(2,1)} %param.14) | copy-start | bytes 1572868
  37.3 9.9 %collective-permute-start = (bf16[512,128]{1,0:T(8,128)(2,1)S(1)}, bf16[512,128]{1,0:T(8,128)(2,1)S(1)}, u32[]{:S(2)}, u32[]{:S(2)}) collective-permute-start(bf16[512,128]{1,0:T(8,128)(2,1)S(1)} %place.1.refs_0_.src0), channel_id=1, source_target_pairs={{0,8},{4,12},{8,16},{12,20},{16,24},{20,28},{24,32},{28,36},{32,40... | collective-permute-start | bytes 393224 | tf_op jit(solution)/shard_map/ppermute | solution.py:362
  39.8 11.3 %collective-permute-start.1 = (bf16[512,128]{1,0:T(8,128)(2,1)S(1)}, bf16[512,128]{1,0:T(8,128)(2,1)S(1)}, u32[]{:S(2)}, u32[]{:S(2)}) collective-permute-start(bf16[512,128]{1,0:T(8,128)(2,1)S(1)} %place.1.refs_0_.src0), channel_id=1, source_target_pairs={{0,4},{4,16},{8,12},{12,24},{16,20},{20,32},{24,28},{28,40},{32,36... | collective-permute-start | bytes 393224 | tf_op jit(solution)/shard_map/ppermute | solution.py:362
  47.2 4.1 %collective-permute-start.2 = (bf16[512,128]{1,0:T(8,128)(2,1)S(1)}, bf16[512,128]{1,0:T(8,128)(2,1)S(1)}, u32[]{:S(2)}, u32[]{:S(2)}) collective-permute-start(bf16[512,128]{1,0:T(8,128)(2,1)S(1)} %collective-permute-done.two), channel_id=1, source_target_pairs={{0,4},{4,0},{8,12},{12,8},{16,20},{20,16},{24,28},{28,24},{32,36},... | collective-permute-start | bytes 393224 | tf_op jit(solution)/shard_map/ppermute | solution.py:362
  52.3 11.9 %copy-start.1 = (bf16[512,256]{1,0:T(8,128)(2,1)S(1)}, bf16[512,256]{1,0:T(8,128)(2,1)}, u32[]{:S(2)}) copy-start(bf16[512,256]{1,0:T(8,128)(2,1)} %out_grad_ref.1) | copy-start | bytes 786436
  52.3 11.9 %copy-start.2 = (bf16[128,256]{1,0:T(8,128)(2,1)S(1)}, bf16[128,256]{1,0:T(8,128)(2,1)}, u32[]{:S(2)}) copy-start(bf16[128,256]{1,0:T(8,128)(2,1)} %weight_ref.1) | copy-start | bytes 196612
  78.9 7.3 %collective-permute-start.3 = (bf16[768,128]{1,0:T(8,128)(2,1)S(1)}, bf16[768,128]{1,0:T(8,128)(2,1)S(1)}, u32[]{:S(2)}, u32[]{:S(2)}) collective-permute-start(bf16[768,128]{1,0:T(8,128)(2,1)S(1)} %get-tuple-element.32), channel_id=1, source_target_pairs={{0,4},{4,0},{8,12},{12,8},{16,20},{20,16},{24,28},{28,24},{32,36},... | collective-permute-start | bytes 589832 | tf_op jit(solution)/shard_map/ppermute | solution.py:362
  84.2 10.2 %collective-permute-start.4 = (bf16[512,128]{1,0:T(8,128)(2,1)S(1)}, bf16[512,128]{1,0:T(8,128)(2,1)S(1)}, u32[]{:S(2)}, u32[]{:S(2)}) collective-permute-start(bf16[512,128]{1,0:T(8,128)(2,1)S(1)} %get-tuple-element.35), channel_id=1, source_target_pairs={{0,500},{4,0},{8,508},{12,8},{16,4},{20,16},{24,12},{28,24},{32,20... | collective-permute-start | bytes 393224 | tf_op jit(solution)/shard_map/ppermute | solution.py:362
  86.9 17.7 %collective-permute-start.5 = (bf16[512,128]{1,0:T(8,128)(2,1)S(1)}, bf16[512,128]{1,0:T(8,128)(2,1)S(1)}, u32[]{:S(2)}, u32[]{:S(2)}) collective-permute-start(bf16[512,128]{1,0:T(8,128)(2,1)S(1)} %get-tuple-element.33.refs_0_), channel_id=1, source_target_pairs={{0,504},{4,508},{8,0},{12,4},{16,8},{20,12},{24,16},{28,20},{32,24... | collective-permute-start | bytes 393224 | tf_op jit(solution)/shard_map/ppermute | solution.py:362
  88.8 15.8 %all-to-all-start.3 = ((bf16[64,4,128]{2,1,0:T(4,128)(2,1)}), bf16[64,4,128]{2,1,0:T(4,128)(2,1)S(1)}, u32[]{:S(2)}, u32[]{:S(2)}) async-start(bf16[64,4,128]{2,1,0:T(4,128)(2,1)} %bitcast.8), calls=%async_computation.3 | async-start | bytes 131072 | tf_op jit(solution)/shard_map/all_to_all | solution.py:386

commit v8 on v7

--- a/solution.py
+++ b/solution.py
@@ -298,6 +298,13 @@
     apart_ref[...] = acc_ref[3 - 2 * odd].astype(BF16)
 
 
+def row_kernel(parts_ref, *refs):
+    out_ref = refs[-1]
+    count, width = parts_ref.shape
+    pairs = jnp.sum(parts_ref[...].astype(F32).reshape(count // 8, 8, width), axis=0)
+    out_ref[...] = jnp.concatenate([pairs[:4] + pairs[4:], jnp.zeros((4, width), F32)], axis=0)
+
+
 def add_kernel(two_ref, mine_ref, near_ref, out_ref, terms_ref):
     rows = out_ref.shape[0]
     out_ref[...] = (two_ref[...] + near_ref[:rows].astype(F32)).astype(BF16)
@@ -315,10 +322,8 @@
     total = own_ref[...] + in1[...].astype(F32) + in2[...].astype(F32)
     grads = scaled_rows(degree_ref, total).astype(BF16)
     slots = dot(unplace_ref[...], grads).astype(BF16)
-    count, width = terms_ref.shape
-    pairs = jnp.sum(terms_ref[...].astype(F32).reshape(count // 8, 8, width), axis=0)
-    term = jnp.concatenate([pairs[:4] + pairs[4:], jnp.zeros((TILE - 4, width), F32)], axis=0)
-    term = term.astype(BF16)
+    empty = jnp.zeros((TILE - 8, terms_ref.shape[1]), F32)
+    term = jnp.concatenate([terms_ref[...], empty], axis=0).astype(BF16)
     lines = (TILE // 8 * 12, TILE)
     owner, slot = slot_of(lines, 0)
     widen = one_hot((slot < 8) & (owner * 8 + slot == iota(lines, 1)))
@@ -478,6 +483,7 @@
     arrive = call(arrive_kernel, shape((rows, total), BF16), "arrive")(
         slot_rows, counts_row, after=(added,)
     )
+    terms = call(row_kernel, shape((8, TILE), F32), "row", flops=LONG)(terms, after=(two,))
     back = call(back_kernel, shape((blocks * (slots + 4), width), BF16), "back")(
         own, apart, two, scale, unplace, terms, after=(arrive,)
     )

time: 134 us -> 135 us (level)
  waiting for transfers between devices: 14.8 us -> 13 us
  blocking collectives: 84.5 us -> 86.2 us
    all_to_all x1, waiting for transfers between devices: 10.1 us -> 7.26 us  [exchange(): lax.all_to_all(value, axis, split_axis=0, concat_axis=0, axis_index_group...]
    all_to_all x4, blocking collectives: 84.5 us -> 86.2 us  [exchange(): lax.all_to_all(value, axis, split_axis=0, concat_axis=0, axis_index_group...]
    pallas_call x8 -> x9, Pallas kernels: 6.81 us -> 6.86 us  [run(): kernel_call(kernel, outs, specs, name, scratch, flops)(*arrays, *after)]
  transfers between devices with their start and end apart: 7 -> 7, of which waited for: 3 -> 4; matrix products, arithmetic and copies ran while one was open for 0% -> 0% of each run, Pallas kernels for 2% -> 1%
where the time goes in v8:
time: 135 us
  blocking collectives  86.2 us (64%)
  starting transfers between devices  23.3 us (17%)
  waiting for transfers between devices  13 us (10%)
  Pallas kernels  11.3 us (8%)
    all_to_all x4, blocking collectives, exchange(): lax.all_to_all(value, axis, split_axis=0, concat_axis=0, axis_index_group...  86.2 us
    ppermute x6, starting transfers between devices, moved(): lax.ppermute(value, 'blk', [(s, target(s) % count) for s in range(count)])  18.6 us
    all_to_all x1, waiting for transfers between devices, exchange(): lax.all_to_all(value, axis, split_axis=0, concat_axis=0, axis_index_group...  7.26 us
    pallas_call x9, Pallas kernels, run(): kernel_call(kernel, outs, specs, name, scratch, flops)(*arrays, *after)  6.86 us
    ppermute x6, waiting for transfers between devices, moved(): lax.ppermute(value, 'blk', [(s, target(s) % count) for s in range(count)])  5.73 us
    all_to_all x1, starting transfers between devices, exchange(): lax.all_to_all(value, axis, split_axis=0, concat_axis=0, axis_index_group...  4.69 us
  transfers between devices with their start and end apart: 7, of which 4 were waited for; matrix products, arithmetic and copies ran while one was open for 0% of the time, Pallas kernels for 1%

profile of v8, /device:TPU:1, one launch (start us, length us, event | category | flops | bytes accessed | tf_op | source)
XLA Modules:
  0.0 134.6 jit_solution(1878568072000339144)
XLA Ops:
  0.6 2.2 %start.1 = (bf16[1024,128]{1,0:T(8,128)(2,1)S(1)}, f32[4,128]{1,0:T(4,128)S(1)}, f32[1,256]{1,0:T(1,128)S(1)}, s32[10,4]{1,0:T(8,128)S(1)}, s32[8,128]{1,0:T(8,128)S(1)}, /*index=5*/s32[1,128]{1,0:T(1,128)S(1)}) custom-call(bf16[512,128]{1,0:T(8,128)(2,1)} %refs_0_.1, s32[8,128]{1,0:T(8,128)} %bitcast.21, s32[1,128]{1,0:T(1,128)} %bitcast.25, ...), custom_call_target="tpu_custom_call" | custom-call | flops 100000000 | bytes 1000000 | tf_op jit(solution)/shard_map/start/pallas_call | solution.py:115
  2.9 33.6 %all_to_all.25 = bf16[128,8,128]{2,1,0:T(8,128)(2,1)S(1)} all-to-all(bf16[128,8,128]{2,1,0:T(8,128)(2,1)S(1)} %bitcast.19), channel_id=1, replica_groups=mesh['blk'=128,'rep'=4] {'blk'}, dimensions={0} | all-to-all | bytes 524288 | tf_op jit(solution)/shard_map/all_to_all | solution.py:391
  36.5 0.8 place.1.refs_0_.src0
  37.3 2.5 %collective-permute-start = (bf16[512,128]{1,0:T(8,128)(2,1)S(1)}, bf16[512,128]{1,0:T(8,128)(2,1)S(1)}, u32[]{:S(2)}, u32[]{:S(2)}) collective-permute-start(bf16[512,128]{1,0:T(8,128)(2,1)S(1)} %place.1.refs_0_.src0), channel_id=1, source_target_pairs={{0,8},{4,12},{8,16},{12,20},{16,24},{20,28},{24,32},{28,36},{32,40... | collective-permute-start | bytes 393224 | tf_op jit(solution)/shard_map/ppermute | solution.py:367
  39.8 3.0 %collective-permute-start.1 = (bf16[512,128]{1,0:T(8,128)(2,1)S(1)}, bf16[512,128]{1,0:T(8,128)(2,1)S(1)}, u32[]{:S(2)}, u32[]{:S(2)}) collective-permute-start(bf16[512,128]{1,0:T(8,128)(2,1)S(1)} %place.1.refs_0_.src0), channel_id=1, source_target_pairs={{0,4},{4,16},{8,12},{12,24},{16,20},{20,32},{24,28},{28,40},{32,36... | collective-permute-start | bytes 393224 | tf_op jit(solution)/shard_map/ppermute | solution.py:367
  42.8 4.5 %collective-permute-done.two = bf16[512,128]{1,0:T(8,128)(2,1)S(1)} collective-permute-done((bf16[512,128]{1,0:T(8,128)(2,1)S(1)}, bf16[512,128]{1,0:T(8,128)(2,1)S(1)}, u32[]{:S(2)}, u32[]{:S(2)}) %collective-permute-start) | collective-permute-done | bytes 131104 | tf_op jit(solution)/shard_map/ppermute | solution.py:367
  47.2 3.1 %collective-permute-start.2 = (bf16[512,128]{1,0:T(8,128)(2,1)S(1)}, bf16[512,128]{1,0:T(8,128)(2,1)S(1)}, u32[]{:S(2)}, u32[]{:S(2)}) collective-permute-start(bf16[512,128]{1,0:T(8,128)(2,1)S(1)} %collective-permute-done.two), channel_id=1, source_target_pairs={{0,4},{4,0},{8,12},{12,8},{16,20},{20,16},{24,28},{28,24},{32,36},... | collective-permute-start | bytes 393224 | tf_op jit(solution)/shard_map/ppermute | solution.py:367
  50.5 0.5 unplace.1.refs_1_.unplace_ref
  51.3 1.0 gather_tiles.1
  52.3 11.9 %all_to_all.26.parts_ref = bf16[4,512,128]{2,1,0:T(8,128)(2,1)S(1)} all-to-all(bf16[4,512,128]{2,1,0:T(8,128)(2,1)S(1)} %gather_tiles.1), channel_id=1, replica_groups=mesh['blk'=128,'rep'=4] {'rep'}, dimensions={0} | all-to-all | bytes 1048576 | tf_op jit(solution)/shard_map/all_to_all | solution.py:391
  64.2 1.2 dense.1
  65.4 12.4 %all_to_all.27.block_ref = bf16[4,784,128]{2,1,0:T(8,128)(2,1)S(1)} all-to-all(bf16[4,784,128]{2,1,0:T(8,128)(2,1)S(1)} %get-tuple-element.29), channel_id=1, replica_groups=mesh['blk'=128,'rep'=4] {'rep'}, dimensions={0} | all-to-all | bytes 1605632 | tf_op jit(solution)/shard_map/all_to_all | solution.py:391
  77.7 1.2 spread_tiles.1
  78.9 5.3 %collective-permute-start.3 = (bf16[768,128]{1,0:T(8,128)(2,1)S(1)}, bf16[768,128]{1,0:T(8,128)(2,1)S(1)}, u32[]{:S(2)}, u32[]{:S(2)}) collective-permute-start(bf16[768,128]{1,0:T(8,128)(2,1)S(1)} %get-tuple-element.32), channel_id=1, source_target_pairs={{0,4},{4,0},{8,12},{12,8},{16,20},{20,16},{24,28},{28,24},{32,36},... | collective-permute-start | bytes 589832 | tf_op jit(solution)/shard_map/ppermute | solution.py:367
  84.2 1.0 collective-permute-done.3.near_ref
  85.3 0.7 add.1
  86.0 1.9 %collective-permute-start.5 = (bf16[512,128]{1,0:T(8,128)(2,1)S(1)}, bf16[512,128]{1,0:T(8,128)(2,1)S(1)}, u32[]{:S(2)}, u32[]{:S(2)}) collective-permute-start(bf16[512,128]{1,0:T(8,128)(2,1)S(1)} %get-tuple-element.33.refs_0_), channel_id=1, source_target_pairs={{0,504},{4,508},{8,0},{12,4},{16,8},{20,12},{24,16},{28,20},{32,24... | collective-permute-start | bytes 393224 | tf_op jit(solution)/shard_map/ppermute | solution.py:367
  87.9 4.7 %all-to-all-start.3 = ((bf16[64,4,128]{2,1,0:T(4,128)(2,1)}), bf16[64,4,128]{2,1,0:T(4,128)(2,1)S(1)}, u32[]{:S(2)}, u32[]{:S(2)}) async-start(bf16[64,4,128]{2,1,0:T(4,128)(2,1)} %bitcast.8), calls=%async_computation.3 | async-start | bytes 131072 | tf_op jit(solution)/shard_map/all_to_all | solution.py:391
  92.6 2.8 %collective-permute-start.4 = (bf16[512,128]{1,0:T(8,128)(2,1)S(1)}, bf16[512,128]{1,0:T(8,128)(2,1)S(1)}, u32[]{:S(2)}, u32[]{:S(2)}) collective-permute-start(bf16[512,128]{1,0:T(8,128)(2,1)S(1)} %get-tuple-element.35), channel_id=1, source_target_pairs={{0,500},{4,0},{8,508},{12,8},{16,4},{20,16},{24,12},{28,24},{32,20... | collective-permute-start | bytes 393224 | tf_op jit(solution)/shard_map/ppermute | solution.py:367
  95.4 1.0 arrive.1.refs_0_.arrive_ref
  96.4 7.3 %all-to-all-done.3 = bf16[64,4,128]{2,1,0:T(4,128)(2,1)S(1)} async-done(((bf16[64,4,128]{2,1,0:T(4,128)(2,1)}), bf16[64,4,128]{2,1,0:T(4,128)(2,1)S(1)}, u32[]{:S(2)}, u32[]{:S(2)}) %all-to-all-start.3) | async-done | bytes 65568 | tf_op jit(solution)/shard_map/all_to_all | solution.py:391
  103.7 0.8 back.1
  104.5 28.4 %all_to_all.28 = bf16[128,3,4,128]{3,2,1,0:T(4,128)(2,1)S(1)} all-to-all(bf16[128,3,4,128]{3,2,1,0:T(4,128)(2,1)S(1)} %bitcast.15), channel_id=1, replica_groups=mesh['blk'=128,'rep'=4] {'blk'}, dimensions={0} | all-to-all | bytes 786432 | tf_op jit(solution)/shard_map/all_to_all | solution.py:391
  132.9 1.7 %last.1 = (bf16[512,128]{1,0:T(8,128)(2,1)}, f32[128,256]{1,0:T(8,128)}, f32[1,256]{1,0:T(1,128)}) custom-call(bf16[512,1024]{1,0:T(8,128)(2,1)S(1)} %arrive.1.refs_0_.arrive_ref, bf16[1536,128]{1,0:T(8,128)(2,1)S(1)} %bitcast.16), custom_call_target="tpu_custom_call" | custom-call | flops 100000000 | bytes 1000000 | tf_op jit(solution)/shard_map/last/pallas_call | solution.py:46
  (12 shorter events, 0.5 us)
Async XLA Ops:
  2.9 47.5 %copy-start = (bf16[4,4,128,128]{3,2,1,0:T(8,128)(2,1)S(1)}, bf16[4,4,128,128]{3,2,1,0:T(8,128)(2,1)}, u32[]{:S(2)}) copy-start(bf16[4,4,128,128]{3,2,1,0:T(8,128)(2,1)} %param.14) | copy-start | bytes 1572868
  37.3 9.9 %collective-permute-start = (bf16[512,128]{1,0:T(8,128)(2,1)S(1)}, bf16[512,128]{1,0:T(8,128)(2,1)S(1)}, u32[]{:S(2)}, u32[]{:S(2)}) collective-permute-start(bf16[512,128]{1,0:T(8,128)(2,1)S(1)} %place.1.refs_0_.src0), channel_id=1, source_target_pairs={{0,8},{4,12},{8,16},{12,20},{16,24},{20,28},{24,32},{28,36},{32,40... | collective-permute-start | bytes 393224 | tf_op jit(solution)/shard_map/ppermute | solution.py:367
  39.8 11.3 %collective-permute-start.1 = (bf16[512,128]{1,0:T(8,128)(2,1)S(1)}, bf16[512,128]{1,0:T(8,128)(2,1)S(1)}, u32[]{:S(2)}, u32[]{:S(2)}) collective-permute-start(bf16[512,128]{1,0:T(8,128)(2,1)S(1)} %place.1.refs_0_.src0), channel_id=1, source_target_pairs={{0,4},{4,16},{8,12},{12,24},{16,20},{20,32},{24,28},{28,40},{32,36... | collective-permute-start | bytes 393224 | tf_op jit(solution)/shard_map/ppermute | solution.py:367
  47.2 4.1 %collective-permute-start.2 = (bf16[512,128]{1,0:T(8,128)(2,1)S(1)}, bf16[512,128]{1,0:T(8,128)(2,1)S(1)}, u32[]{:S(2)}, u32[]{:S(2)}) collective-permute-start(bf16[512,128]{1,0:T(8,128)(2,1)S(1)} %collective-permute-done.two), channel_id=1, source_target_pairs={{0,4},{4,0},{8,12},{12,8},{16,20},{20,16},{24,28},{28,24},{32,36},... | collective-permute-start | bytes 393224 | tf_op jit(solution)/shard_map/ppermute | solution.py:367
  52.3 11.9 %copy-start.1 = (bf16[512,256]{1,0:T(8,128)(2,1)S(1)}, bf16[512,256]{1,0:T(8,128)(2,1)}, u32[]{:S(2)}) copy-start(bf16[512,256]{1,0:T(8,128)(2,1)} %out_grad_ref.1) | copy-start | bytes 786436
  52.3 11.9 %copy-start.2 = (bf16[128,256]{1,0:T(8,128)(2,1)S(1)}, bf16[128,256]{1,0:T(8,128)(2,1)}, u32[]{:S(2)}) copy-start(bf16[128,256]{1,0:T(8,128)(2,1)} %weight_ref.1) | copy-start | bytes 196612
  78.9 6.4 %collective-permute-start.3 = (bf16[768,128]{1,0:T(8,128)(2,1)S(1)}, bf16[768,128]{1,0:T(8,128)(2,1)S(1)}, u32[]{:S(2)}, u32[]{:S(2)}) collective-permute-start(bf16[768,128]{1,0:T(8,128)(2,1)S(1)} %get-tuple-element.32), channel_id=1, source_target_pairs={{0,4},{4,0},{8,12},{12,8},{16,20},{20,16},{24,28},{28,24},{32,36},... | collective-permute-start | bytes 589832 | tf_op jit(solution)/shard_map/ppermute | solution.py:367
  86.0 17.7 %collective-permute-start.5 = (bf16[512,128]{1,0:T(8,128)(2,1)S(1)}, bf16[512,128]{1,0:T(8,128)(2,1)S(1)}, u32[]{:S(2)}, u32[]{:S(2)}) collective-permute-start(bf16[512,128]{1,0:T(8,128)(2,1)S(1)} %get-tuple-element.33.refs_0_), channel_id=1, source_target_pairs={{0,504},{4,508},{8,0},{12,4},{16,8},{20,12},{24,16},{28,20},{32,24... | collective-permute-start | bytes 393224 | tf_op jit(solution)/shard_map/ppermute | solution.py:367
  87.9 15.8 %all-to-all-start.3 = ((bf16[64,4,128]{2,1,0:T(4,128)(2,1)}), bf16[64,4,128]{2,1,0:T(4,128)(2,1)S(1)}, u32[]{:S(2)}, u32[]{:S(2)}) async-start(bf16[64,4,128]{2,1,0:T(4,128)(2,1)} %bitcast.8), calls=%async_computation.3 | async-start | bytes 131072 | tf_op jit(solution)/shard_map/all_to_all | solution.py:391
  92.6 11.1 %collective-permute-start.4 = (bf16[512,128]{1,0:T(8,128)(2,1)S(1)}, bf16[512,128]{1,0:T(8,128)(2,1)S(1)}, u32[]{:S(2)}, u32[]{:S(2)}) collective-permute-start(bf16[512,128]{1,0:T(8,128)(2,1)S(1)} %get-tuple-element.35), channel_id=1, source_target_pairs={{0,500},{4,0},{8,508},{12,8},{16,4},{20,16},{24,12},{28,24},{32,20... | collective-permute-start | bytes 393224 | tf_op jit(solution)/shard_map/ppermute | solution.py:367

commit v9 on v8

--- a/solution.py
+++ b/solution.py
@@ -483,7 +483,7 @@
     arrive = call(arrive_kernel, shape((rows, total), BF16), "arrive")(
         slot_rows, counts_row, after=(added,)
     )
-    terms = call(row_kernel, shape((8, TILE), F32), "row", flops=LONG)(terms, after=(two,))
+    terms = call(row_kernel, shape((8, TILE), F32), "row", flops=LONG)(terms, after=(apart,))
     back = call(back_kernel, shape((blocks * (slots + 4), width), BF16), "back")(
         own, apart, two, scale, unplace, terms, after=(arrive,)
     )

time: 135 us -> 134 us (level)
  waiting for transfers between devices: 13 us -> 8.23 us
  starting transfers between devices: 23.3 us -> 27 us
    all_to_all x1, waiting for transfers between devices: 7.26 us -> 3.54 us  [exchange(): lax.all_to_all(value, axis, split_axis=0, concat_axis=0, axis_index_group...]
    ppermute x6, starting transfers between devices: 18.6 us -> 22.3 us  [moved(): lax.ppermute(value, 'blk', [(s, target(s) % count) for s in range(count)])]
  transfers between devices with their start and end apart: 7 -> 7, of which waited for: 4 -> 3; matrix products, arithmetic and copies ran while one was open for 0% -> 0% of each run, Pallas kernels for 1% -> 2%
where the time goes in v9:
time: 134 us; the launch traced here: 133 us
  blocking collectives  86.2 us (64%)
  starting transfers between devices  27 us (20%)
  Pallas kernels  11.3 us (8%)
  waiting for transfers between devices  8.23 us (6%)
    all_to_all x4, blocking collectives, exchange(): lax.all_to_all(value, axis, split_axis=0, concat_axis=0, axis_index_group...  86.2 us
    ppermute x6, starting transfers between devices, moved(): lax.ppermute(value, 'blk', [(s, target(s) % count) for s in range(count)])  22.3 us
    pallas_call x9, Pallas kernels, run(): kernel_call(kernel, outs, specs, name, scratch, flops)(*arrays, *after)  6.87 us
    ppermute x6, waiting for transfers between devices, moved(): lax.ppermute(value, 'blk', [(s, target(s) % count) for s in range(count)])  4.69 us
    all_to_all x1, starting transfers between devices, exchange(): lax.all_to_all(value, axis, split_axis=0, concat_axis=0, axis_index_group...  4.62 us
    all_to_all x1, waiting for transfers between devices, exchange(): lax.all_to_all(value, axis, split_axis=0, concat_axis=0, axis_index_group...  3.54 us
  transfers between devices with their start and end apart: 7, of which 3 were waited for; matrix products, arithmetic and copies ran while one was open for 0% of the time, Pallas kernels for 2%

profile of v9, /device:TPU:1, one launch (start us, length us, event | category | flops | bytes accessed | tf_op | source)
XLA Modules:
  0.0 133.5 jit_solution(13178861751669641354)
XLA Ops:
  0.6 2.2 %start.1 = (bf16[1024,128]{1,0:T(8,128)(2,1)S(1)}, f32[4,128]{1,0:T(4,128)S(1)}, f32[1,256]{1,0:T(1,128)S(1)}, s32[10,4]{1,0:T(8,128)S(1)}, s32[8,128]{1,0:T(8,128)S(1)}, /*index=5*/s32[1,128]{1,0:T(1,128)S(1)}) custom-call(bf16[512,128]{1,0:T(8,128)(2,1)} %refs_0_.1, s32[8,128]{1,0:T(8,128)} %bitcast.21, s32[1,128]{1,0:T(1,128)} %bitcast.25, ...), custom_call_target="tpu_custom_call" | custom-call | flops 100000000 | bytes 1000000 | tf_op jit(solution)/shard_map/start/pallas_call | solution.py:115
  2.9 33.6 %all_to_all.25 = bf16[128,8,128]{2,1,0:T(8,128)(2,1)S(1)} all-to-all(bf16[128,8,128]{2,1,0:T(8,128)(2,1)S(1)} %bitcast.19), channel_id=1, replica_groups=mesh['blk'=128,'rep'=4] {'blk'}, dimensions={0} | all-to-all | bytes 524288 | tf_op jit(solution)/shard_map/all_to_all | solution.py:391
  36.5 0.8 place.1.refs_0_.src0
  37.3 2.5 %collective-permute-start = (bf16[512,128]{1,0:T(8,128)(2,1)S(1)}, bf16[512,128]{1,0:T(8,128)(2,1)S(1)}, u32[]{:S(2)}, u32[]{:S(2)}) collective-permute-start(bf16[512,128]{1,0:T(8,128)(2,1)S(1)} %place.1.refs_0_.src0), channel_id=1, source_target_pairs={{0,8},{4,12},{8,16},{12,20},{16,24},{20,28},{24,32},{28,36},{32,40... | collective-permute-start | bytes 393224 | tf_op jit(solution)/shard_map/ppermute | solution.py:367
  39.8 3.0 %collective-permute-start.1 = (bf16[512,128]{1,0:T(8,128)(2,1)S(1)}, bf16[512,128]{1,0:T(8,128)(2,1)S(1)}, u32[]{:S(2)}, u32[]{:S(2)}) collective-permute-start(bf16[512,128]{1,0:T(8,128)(2,1)S(1)} %place.1.refs_0_.src0), channel_id=1, source_target_pairs={{0,4},{4,16},{8,12},{12,24},{16,20},{20,32},{24,28},{28,40},{32,36... | collective-permute-start | bytes 393224 | tf_op jit(solution)/shard_map/ppermute | solution.py:367
  42.8 4.5 %collective-permute-done.two = bf16[512,128]{1,0:T(8,128)(2,1)S(1)} collective-permute-done((bf16[512,128]{1,0:T(8,128)(2,1)S(1)}, bf16[512,128]{1,0:T(8,128)(2,1)S(1)}, u32[]{:S(2)}, u32[]{:S(2)}) %collective-permute-start) | collective-permute-done | bytes 131104 | tf_op jit(solution)/shard_map/ppermute | solution.py:367
  47.2 3.1 %collective-permute-start.2 = (bf16[512,128]{1,0:T(8,128)(2,1)S(1)}, bf16[512,128]{1,0:T(8,128)(2,1)S(1)}, u32[]{:S(2)}, u32[]{:S(2)}) collective-permute-start(bf16[512,128]{1,0:T(8,128)(2,1)S(1)} %collective-permute-done.two), channel_id=1, source_target_pairs={{0,4},{4,0},{8,12},{12,8},{16,20},{20,16},{24,28},{28,24},{32,36},... | collective-permute-start | bytes 393224 | tf_op jit(solution)/shard_map/ppermute | solution.py:367
  50.5 0.5 unplace.1.refs_1_.unplace_ref
  51.1 0.2 collective-permute-done.2.near
  51.3 1.0 gather_tiles.1
  52.3 11.9 %all_to_all.26.parts_ref = bf16[4,512,128]{2,1,0:T(8,128)(2,1)S(1)} all-to-all(bf16[4,512,128]{2,1,0:T(8,128)(2,1)S(1)} %gather_tiles.1), channel_id=1, replica_groups=mesh['blk'=128,'rep'=4] {'rep'}, dimensions={0} | all-to-all | bytes 1048576 | tf_op jit(solution)/shard_map/all_to_all | solution.py:391
  64.2 1.2 dense.1
  65.4 12.4 %all_to_all.27.block_ref = bf16[4,784,128]{2,1,0:T(8,128)(2,1)S(1)} all-to-all(bf16[4,784,128]{2,1,0:T(8,128)(2,1)S(1)} %get-tuple-element.29), channel_id=1, replica_groups=mesh['blk'=128,'rep'=4] {'rep'}, dimensions={0} | all-to-all | bytes 1605632 | tf_op jit(solution)/shard_map/all_to_all | solution.py:391
  77.7 1.2 spread_tiles.1
  78.9 5.3 %collective-permute-start.3 = (bf16[768,128]{1,0:T(8,128)(2,1)S(1)}, bf16[768,128]{1,0:T(8,128)(2,1)S(1)}, u32[]{:S(2)}, u32[]{:S(2)}) collective-permute-start(bf16[768,128]{1,0:T(8,128)(2,1)S(1)} %get-tuple-element.32), channel_id=1, source_target_pairs={{0,4},{4,0},{8,12},{12,8},{16,20},{20,16},{24,28},{28,24},{32,36},... | collective-permute-start | bytes 589832 | tf_op jit(solution)/shard_map/ppermute | solution.py:367
  84.2 1.9 %collective-permute-start.4 = (bf16[512,128]{1,0:T(8,128)(2,1)S(1)}, bf16[512,128]{1,0:T(8,128)(2,1)S(1)}, u32[]{:S(2)}, u32[]{:S(2)}) collective-permute-start(bf16[512,128]{1,0:T(8,128)(2,1)S(1)} %get-tuple-element.35), channel_id=1, source_target_pairs={{0,500},{4,0},{8,508},{12,8},{16,4},{20,16},{24,12},{28,24},{32,20... | collective-permute-start | bytes 393224 | tf_op jit(solution)/shard_map/ppermute | solution.py:367
  86.2 0.7 add.1
  86.9 4.6 %all-to-all-start.3 = ((bf16[64,4,128]{2,1,0:T(4,128)(2,1)}), bf16[64,4,128]{2,1,0:T(4,128)(2,1)S(1)}, u32[]{:S(2)}, u32[]{:S(2)}) async-start(bf16[64,4,128]{2,1,0:T(4,128)(2,1)} %bitcast.8), calls=%async_computation.3 | async-start | bytes 131072 | tf_op jit(solution)/shard_map/all_to_all | solution.py:391
  91.5 6.6 %collective-permute-start.5 = (bf16[512,128]{1,0:T(8,128)(2,1)S(1)}, bf16[512,128]{1,0:T(8,128)(2,1)S(1)}, u32[]{:S(2)}, u32[]{:S(2)}) collective-permute-start(bf16[512,128]{1,0:T(8,128)(2,1)S(1)} %get-tuple-element.33.refs_0_), channel_id=1, source_target_pairs={{0,504},{4,508},{8,0},{12,4},{16,8},{20,12},{24,16},{28,20},{32,24... | collective-permute-start | bytes 393224 | tf_op jit(solution)/shard_map/ppermute | solution.py:367
  98.0 1.0 arrive.1.refs_0_.arrive_ref
  99.0 3.5 %all-to-all-done.3 = bf16[64,4,128]{2,1,0:T(4,128)(2,1)S(1)} async-done(((bf16[64,4,128]{2,1,0:T(4,128)(2,1)}), bf16[64,4,128]{2,1,0:T(4,128)(2,1)S(1)}, u32[]{:S(2)}, u32[]{:S(2)}) %all-to-all-start.3) | async-done | bytes 65568 | tf_op jit(solution)/shard_map/all_to_all | solution.py:391
  102.6 0.8 back.1
  103.4 28.4 %all_to_all.28 = bf16[128,3,4,128]{3,2,1,0:T(4,128)(2,1)S(1)} all-to-all(bf16[128,3,4,128]{3,2,1,0:T(4,128)(2,1)S(1)} %bitcast.15), channel_id=1, replica_groups=mesh['blk'=128,'rep'=4] {'blk'}, dimensions={0} | all-to-all | bytes 786432 | tf_op jit(solution)/shard_map/all_to_all | solution.py:391
  131.8 1.7 %last.1 = (bf16[512,128]{1,0:T(8,128)(2,1)}, f32[128,256]{1,0:T(8,128)}, f32[1,256]{1,0:T(1,128)}) custom-call(bf16[512,1024]{1,0:T(8,128)(2,1)S(1)} %arrive.1.refs_0_.arrive_ref, bf16[1536,128]{1,0:T(8,128)(2,1)S(1)} %bitcast.16), custom_call_target="tpu_custom_call" | custom-call | flops 100000000 | bytes 1000000 | tf_op jit(solution)/shard_map/last/pallas_call | solution.py:46
  (12 shorter events, 0.3 us)
Async XLA Ops:
  2.9 47.5 %copy-start = (bf16[4,4,128,128]{3,2,1,0:T(8,128)(2,1)S(1)}, bf16[4,4,128,128]{3,2,1,0:T(8,128)(2,1)}, u32[]{:S(2)}) copy-start(bf16[4,4,128,128]{3,2,1,0:T(8,128)(2,1)} %param.14) | copy-start | bytes 1572868
  37.3 9.9 %collective-permute-start = (bf16[512,128]{1,0:T(8,128)(2,1)S(1)}, bf16[512,128]{1,0:T(8,128)(2,1)S(1)}, u32[]{:S(2)}, u32[]{:S(2)}) collective-permute-start(bf16[512,128]{1,0:T(8,128)(2,1)S(1)} %place.1.refs_0_.src0), channel_id=1, source_target_pairs={{0,8},{4,12},{8,16},{12,20},{16,24},{20,28},{24,32},{28,36},{32,40... | collective-permute-start | bytes 393224 | tf_op jit(solution)/shard_map/ppermute | solution.py:367
  39.8 11.3 %collective-permute-start.1 = (bf16[512,128]{1,0:T(8,128)(2,1)S(1)}, bf16[512,128]{1,0:T(8,128)(2,1)S(1)}, u32[]{:S(2)}, u32[]{:S(2)}) collective-permute-start(bf16[512,128]{1,0:T(8,128)(2,1)S(1)} %place.1.refs_0_.src0), channel_id=1, source_target_pairs={{0,4},{4,16},{8,12},{12,24},{16,20},{20,32},{24,28},{28,40},{32,36... | collective-permute-start | bytes 393224 | tf_op jit(solution)/shard_map/ppermute | solution.py:367
  47.2 4.1 %collective-permute-start.2 = (bf16[512,128]{1,0:T(8,128)(2,1)S(1)}, bf16[512,128]{1,0:T(8,128)(2,1)S(1)}, u32[]{:S(2)}, u32[]{:S(2)}) collective-permute-start(bf16[512,128]{1,0:T(8,128)(2,1)S(1)} %collective-permute-done.two), channel_id=1, source_target_pairs={{0,4},{4,0},{8,12},{12,8},{16,20},{20,16},{24,28},{28,24},{32,36},... | collective-permute-start | bytes 393224 | tf_op jit(solution)/shard_map/ppermute | solution.py:367
  52.3 11.9 %copy-start.1 = (bf16[512,256]{1,0:T(8,128)(2,1)S(1)}, bf16[512,256]{1,0:T(8,128)(2,1)}, u32[]{:S(2)}) copy-start(bf16[512,256]{1,0:T(8,128)(2,1)} %out_grad_ref.1) | copy-start | bytes 786436
  52.3 11.9 %copy-start.2 = (bf16[128,256]{1,0:T(8,128)(2,1)S(1)}, bf16[128,256]{1,0:T(8,128)(2,1)}, u32[]{:S(2)}) copy-start(bf16[128,256]{1,0:T(8,128)(2,1)} %weight_ref.1) | copy-start | bytes 196612
  78.9 7.3 %collective-permute-start.3 = (bf16[768,128]{1,0:T(8,128)(2,1)S(1)}, bf16[768,128]{1,0:T(8,128)(2,1)S(1)}, u32[]{:S(2)}, u32[]{:S(2)}) collective-permute-start(bf16[768,128]{1,0:T(8,128)(2,1)S(1)} %get-tuple-element.32), channel_id=1, source_target_pairs={{0,4},{4,0},{8,12},{12,8},{16,20},{20,16},{24,28},{28,24},{32,36},... | collective-permute-start | bytes 589832 | tf_op jit(solution)/shard_map/ppermute | solution.py:367
  84.2 14.8 %collective-permute-start.4 = (bf16[512,128]{1,0:T(8,128)(2,1)S(1)}, bf16[512,128]{1,0:T(8,128)(2,1)S(1)}, u32[]{:S(2)}, u32[]{:S(2)}) collective-permute-start(bf16[512,128]{1,0:T(8,128)(2,1)S(1)} %get-tuple-element.35), channel_id=1, source_target_pairs={{0,500},{4,0},{8,508},{12,8},{16,4},{20,16},{24,12},{28,24},{32,20... | collective-permute-start | bytes 393224 | tf_op jit(solution)/shard_map/ppermute | solution.py:367
  86.9 15.7 %all-to-all-start.3 = ((bf16[64,4,128]{2,1,0:T(4,128)(2,1)}), bf16[64,4,128]{2,1,0:T(4,128)(2,1)S(1)}, u32[]{:S(2)}, u32[]{:S(2)}) async-start(bf16[64,4,128]{2,1,0:T(4,128)(2,1)} %bitcast.8), calls=%async_computation.3 | async-start | bytes 131072 | tf_op jit(solution)/shard_map/all_to_all | solution.py:391
  91.5 11.1 %collective-permute-start.5 = (bf16[512,128]{1,0:T(8,128)(2,1)S(1)}, bf16[512,128]{1,0:T(8,128)(2,1)S(1)}, u32[]{:S(2)}, u32[]{:S(2)}) collective-permute-start(bf16[512,128]{1,0:T(8,128)(2,1)S(1)} %get-tuple-element.33.refs_0_), channel_id=1, source_target_pairs={{0,504},{4,508},{8,0},{12,4},{16,8},{20,12},{24,16},{28,20},{32,24... | collective-permute-start | bytes 393224 | tf_op jit(solution)/shard_map/ppermute | solution.py:367
